TPU v7x, 32 devices: a whole 2x2x4 slice. The times are simulated.
32 devices in a mesh: sp: 8 (over y, x, core), dp: 4 (over z).
Axes of the slice: x: 2, y: 2, z: 4, core: 2. Of those that a mesh axis runs over, the one named last changes fastest.
Arguments:
- tokens: bfloat16 [4, 3072, 768], P('dp', 'sp'), may hold values from -6 to 6
- ln1_gain: float32 [768], replicated, may hold values from 0.5 to 1.5
- ln1_shift: float32 [768], replicated, may hold values from -1.2 to 1.2
- w_qkv: bfloat16 [768, 2304], replicated, may hold values from -0.21875 to 0.21875
- w_out: bfloat16 [768, 768], replicated, may hold values from -1.75 to 1.75
- ln2_gain: float32 [768], replicated, may hold values from 0.5 to 1.5
- ln2_shift: float32 [768], replicated, may hold values from -1.2 to 1.2
- w_router: bfloat16 [768, 16], replicated, may hold values from -0.21875 to 0.21875
- train_w1: bfloat16 [8, 768, 3072], P('sp', None, 'dp'), may hold values from -0.21875 to 0.21875
- train_w2: bfloat16 [8, 3072, 768], P('sp', 'dp'), may hold values from -0.109375 to 0.109375
- frozen_w1: bfloat16 [8, 768, 3072], P('sp', None, 'dp'), may hold values from -0.21875 to 0.21875
- frozen_w2: bfloat16 [8, 3072, 768], P('sp', 'dp'), may hold values from -0.109375 to 0.109375
- routes: int32 [4, 3072, 2], P('dp', 'sp'), may hold values from 0 to 15, all different within a row; in each aligned block of 384 rows (0 to 383, 384 to 767, ..., all dimensions but the last counted through in order) at most 96 rows name the same one
- cotangent: bfloat16 [4, 3072, 768], P('dp', 'sp'), may hold values from -6 to 6
Outputs:
- block_out: bfloat16 [4, 3072, 768], P('dp', 'sp')
- tokens_grad: float32 [4, 3072, 768], P('dp', 'sp')
- ln1_gain_grad: float32 [768], replicated
- ln1_shift_grad: float32 [768], replicated
- qkv_grad: float32 [768, 2304], replicated
- out_proj_grad: float32 [768, 768], replicated
- ln2_gain_grad: float32 [768], replicated
- ln2_shift_grad: float32 [768], replicated
- router_grad: float32 [768, 16], replicated
- train_w1_grad: float32 [8, 768, 3072], P('sp', None, 'dp')
- train_w2_grad: float32 [8, 3072, 768], P('sp', 'dp')
Inputs may be any that keep to these rules, and one draw needn't show every extreme that they name: `routes`: each token names two different experts. Among the 384 tokens of one device no expert is named more than 96 times, and on some device some expert is named exactly 96 times.
All inputs are finite; a program needn't handle non-finite values.
Results may differ from a plain program's by a relative error of at most 0.025.
Values may be sent and summed in bfloat16 or wider, within the bound.
A program may use at most 384 MiB of HBM per device.

v0:
```python
import jax
import jax.numpy as jnp
from jax import lax
from jax.sharding import PartitionSpec as P

HEADS = 12
HEAD_DIM = 64
LEN_A = 1024
LEN_B = 2048
PAIRS = 1


EPSILON = 1e-05
NEGATIVE = -1e30


def from_behind(value, axis, steps):
    count = lax.axis_size(axis)
    first, last = (max(0, -steps), min(count, count - steps))
    return lax.ppermute(value, axis, [(source, source + steps) for source in range(first, last)])


def shifted(value, axis, steps):
    count = lax.axis_size(axis)
    pairs = [(source, (source + steps) % count) for source in range(count)]
    return lax.ppermute(value, axis, pairs)


def layer_norm(inputs, gain_vec, shift_vec):
    centre = jnp.mean(inputs, axis=-1, keepdims=True)
    centred = inputs - centre
    spread = jnp.mean(centred * centred, axis=-1, keepdims=True)
    return centred * lax.rsqrt(spread + EPSILON) * gain_vec + shift_vec


def split_heads(packed):
    return packed.reshape(packed.shape[0], packed.shape[1], HEADS, HEAD_DIM)


def keep_mask(length, diagonal):
    indices = jnp.arange(length, dtype=jnp.int32)
    return jnp.logical_or(jnp.logical_not(diagonal), indices[:, None] >= indices[None, :])


def empty_state(count, length):
    return (
        jnp.full((count, HEADS, length), NEGATIVE, jnp.float32),
        jnp.zeros((count, HEADS, length), jnp.float32),
        jnp.zeros((count, length, HEADS, HEAD_DIM), jnp.float32),
    )


def forward_block(running, queries, keyval, diagonal):
    peaks, totals, summed = running
    model_width = queries.shape[2]
    key_rows = split_heads(keyval[..., :model_width])
    value_rows = split_heads(keyval[..., model_width:])
    scores = jnp.einsum(
        "sqhd,skhd->shqk", split_heads(queries), key_rows, preferred_element_type=jnp.float32
    ) * HEAD_DIM ** (-0.5)
    scores = jnp.where(keep_mask(queries.shape[1], diagonal), scores, NEGATIVE)
    new_peaks = jnp.maximum(peaks, jnp.max(scores, axis=-1))
    factor = jnp.exp(peaks - new_peaks)
    weight = jnp.exp(scores - new_peaks[..., None])
    totals = totals * factor + jnp.sum(weight, axis=-1)
    update = jnp.einsum(
        "shqk,skhd->sqhd",
        weight.astype(jnp.bfloat16),
        value_rows,
        preferred_element_type=jnp.float32,
    )
    summed = summed * jnp.transpose(factor, (0, 2, 1))[..., None] + update
    return (new_peaks, totals, summed)


def finish_state(running):
    peaks, totals, summed = running
    attended = summed / jnp.transpose(totals, (0, 2, 1))[..., None]
    return (attended.reshape(summed.shape[0], summed.shape[1], -1), peaks + jnp.log(totals))


def backward_block(grad_query, grad_keyval, queries, grad_out, log_total, deltas, keyval, diagonal):
    model_width = queries.shape[2]
    key_rows = split_heads(keyval[..., :model_width])
    value_rows = split_heads(keyval[..., model_width:])
    out_heads = split_heads(grad_out)
    scale_factor = HEAD_DIM ** (-0.5)
    scores = (
        jnp.einsum(
            "sqhd,skhd->shqk", split_heads(queries), key_rows, preferred_element_type=jnp.float32
        )
        * scale_factor
    )
    scores = jnp.where(keep_mask(queries.shape[1], diagonal), scores, NEGATIVE)
    probability = jnp.exp(scores - log_total[..., None])
    grad_value = jnp.einsum(
        "shqk,sqhd->skhd",
        probability.astype(jnp.bfloat16),
        out_heads,
        preferred_element_type=jnp.float32,
    )
    grad_prob = jnp.einsum(
        "sqhd,skhd->shqk", out_heads, value_rows, preferred_element_type=jnp.float32
    )
    grad_score = (probability * (grad_prob - deltas[..., None])).astype(jnp.bfloat16)
    grad_query = (
        grad_query
        + jnp.einsum("shqk,skhd->sqhd", grad_score, key_rows, preferred_element_type=jnp.float32)
        * scale_factor
    )
    grad_key = (
        jnp.einsum(
            "shqk,sqhd->skhd", grad_score, split_heads(queries), preferred_element_type=jnp.float32
        )
        * scale_factor
    )
    count, length = (queries.shape[0], queries.shape[1])
    grad_keyval = grad_keyval + jnp.concatenate(
        [
            grad_key.reshape(count, length, model_width),
            grad_value.reshape(count, length, model_width),
        ],
        axis=-1,
    )
    return (grad_query, grad_keyval)


def head_delta(grad_out, attended):
    product = split_heads(grad_out.astype(jnp.float32)) * split_heads(attended)
    return jnp.transpose(jnp.sum(product, axis=-1), (0, 2, 1))


def gelu_backward(pre_act, grad_hidden):
    unused, pullback = jax.vjp(jax.nn.gelu, pre_act)
    return pullback(grad_hidden)[0].astype(jnp.bfloat16)


def shards(
    tokens,
    ln1_gain,
    ln1_shift,
    w_qkv,
    w_out,
    ln2_gain,
    ln2_shift,
    w_router,
    train_w1,
    train_w2,
    frozen_w1,
    frozen_w2,
    routes,
    cotangent,
):
    sp_count = lax.axis_size("sp")
    my_index = lax.axis_index("sp")
    token_count = tokens.shape[1]
    model_width = tokens.shape[2]
    seq_count = PAIRS * sp_count // 8
    short_len = LEN_A // sp_count
    long_len = LEN_B // sp_count
    split_at = seq_count * short_len
    capacity = 2 * token_count // sp_count
    slot_total = sp_count * capacity
    inputs = tokens[0].astype(jnp.float32)
    first_norm_full, first_pullback = jax.vjp(layer_norm, inputs, ln1_gain, ln1_shift)
    first_norm = first_norm_full.astype(jnp.bfloat16)
    projected = jnp.dot(first_norm, w_qkv, preferred_element_type=jnp.float32).astype(jnp.bfloat16)
    group_short = projected[:split_at].reshape(seq_count, short_len, 3 * model_width)
    group_long = projected[split_at:].reshape(seq_count, long_len, 3 * model_width)
    query_short = group_short[..., :model_width]
    keyval_short = group_short[..., model_width:]
    query_long = group_long[..., :model_width]
    keyval_long = group_long[..., model_width:]

    def visit(step_index, kv_short, kv_long, states):
        source = my_index - step_index

        def visit_compute_live(current):
            return (
                forward_block(current[0], query_short, kv_short, source == my_index),
                forward_block(current[1], query_long, kv_long, source == my_index),
            )

        return lax.cond(source >= 0, visit_compute_live, lambda current: current, states)

    def forward_turn(step_index, carry):
        kv_short, kv_long, states = carry
        states = visit(step_index, kv_short, kv_long, states)
        kv_short, kv_long = from_behind((kv_short, kv_long), "sp", 1)
        return (kv_short, kv_long, states)

    start_states = (empty_state(seq_count, short_len), empty_state(seq_count, long_len))
    kv_short, kv_long, states = lax.fori_loop(
        0, sp_count - 1, forward_turn, (keyval_short, keyval_long, start_states)
    )
    states = visit(sp_count - 1, kv_short, kv_long, states)
    attended_short, log_short = finish_state(states[0])
    attended_long, log_long = finish_state(states[1])
    attended = jnp.concatenate(
        [attended_short.reshape(-1, model_width), attended_long.reshape(-1, model_width)], axis=0
    )
    attended_low = attended.astype(jnp.bfloat16)
    middle = inputs + jnp.dot(attended_low, w_out, preferred_element_type=jnp.float32)
    second_norm_full, second_pullback = jax.vjp(layer_norm, middle, ln2_gain, ln2_shift)
    second_norm = second_norm_full.astype(jnp.bfloat16)
    expert_ids = routes[0]
    logits = jnp.dot(second_norm, w_router, preferred_element_type=jnp.float32)
    matches = (expert_ids[..., None] == jnp.arange(2 * sp_count, dtype=jnp.int32)).astype(
        jnp.float32
    )
    chosen = jnp.sum(matches * logits[:, None, :], axis=-1)
    top_logit = jnp.max(chosen, axis=-1, keepdims=True)
    exped = jnp.exp(chosen - top_logit)
    gates = exped / jnp.sum(exped, axis=-1, keepdims=True)
    flat_matches = matches.astype(jnp.int32).reshape(token_count * 2, 2 * sp_count)
    before = jnp.cumsum(flat_matches, axis=0) - flat_matches
    slot_index = jnp.sum(before * flat_matches, axis=-1)
    flat_ids = expert_ids.reshape(-1)
    frozen_flag = (flat_ids >= sp_count).astype(jnp.int32)
    positions = ((flat_ids - frozen_flag * sp_count) * 2 + frozen_flag) * capacity + slot_index
    anchor = jnp.arange(token_count * 2, dtype=jnp.int32) // 2

    def pack_routes(route_rows):
        buffer = (
            jnp.zeros((sp_count * 2 * capacity, model_width), jnp.bfloat16)
            .at[positions]
            .set(route_rows)
        )
        return buffer.reshape(sp_count, 2, capacity, model_width)

    def unpack_kinds(arrived):
        return (
            arrived[:, 0].reshape(slot_total, model_width),
            arrived[:, 1].reshape(slot_total, model_width),
        )

    def pack_kinds(first_rows, second_rows):
        return jnp.stack(
            [
                first_rows.astype(jnp.bfloat16).reshape(sp_count, capacity, model_width),
                second_rows.astype(jnp.bfloat16).reshape(sp_count, capacity, model_width),
            ],
            axis=1,
        )

    arrived = lax.all_to_all(
        pack_routes(second_norm[anchor]), "sp", split_axis=0, concat_axis=0, tiled=True
    )
    rows_train, rows_frozen = unpack_kinds(arrived)
    gathered = (
        lax.all_gather(rows_train, "dp", axis=0, tiled=True),
        lax.all_gather(rows_frozen, "dp", axis=0, tiled=True),
    )
    inputs_train, inputs_frozen = (gathered[0], gathered[1])
    first_train, second_train = (train_w1[0], train_w2[0])
    first_frozen, second_frozen = (frozen_w1[0], frozen_w2[0])
    pre_train = jnp.dot(inputs_train, first_train, preferred_element_type=jnp.float32)
    pre_frozen = jnp.dot(inputs_frozen, first_frozen, preferred_element_type=jnp.float32)
    hidden_train = jax.nn.gelu(pre_train).astype(jnp.bfloat16)
    hidden_frozen = jax.nn.gelu(pre_frozen).astype(jnp.bfloat16)
    part_train = hidden_train
    part_frozen = hidden_frozen
    produced = lax.psum_scatter(
        jnp.concatenate(
            [
                jnp.dot(part_train, second_train, preferred_element_type=jnp.float32),
                jnp.dot(part_frozen, second_frozen, preferred_element_type=jnp.float32),
            ],
            axis=1,
        ).astype(jnp.bfloat16),
        "dp",
        scatter_dimension=0,
        tiled=True,
    ).astype(jnp.float32)
    out_train = produced[:, :model_width]
    out_frozen = produced[:, model_width:]
    collected = lax.all_to_all(
        pack_kinds(out_train, out_frozen), "sp", split_axis=0, concat_axis=0, tiled=True
    )
    expert_out = (
        collected.reshape(sp_count * 2 * capacity, model_width)[positions]
        .astype(jnp.float32)
        .reshape(token_count, 2, model_width)
    )
    block_out = (middle + jnp.sum(gates[..., None] * expert_out, axis=1)).astype(jnp.bfloat16)
    upstream = cotangent[0].astype(jnp.float32)
    route_grads = (
        (gates[..., None] * upstream[:, None, :])
        .astype(jnp.bfloat16)
        .reshape(token_count * 2, model_width)
    )
    grad_gate = jnp.sum(upstream[:, None, :] * expert_out, axis=-1)
    grad_chosen = gates * (grad_gate - jnp.sum(gates * grad_gate, axis=-1, keepdims=True))
    grad_logits = jnp.sum(matches * grad_chosen[..., None], axis=1)
    router_part = jnp.einsum(
        "td,te->de", second_norm.astype(jnp.float32), grad_logits, precision=lax.Precision.HIGHEST
    )
    router_back = jnp.einsum(
        "te,de->td", grad_logits, w_router.astype(jnp.float32), precision=lax.Precision.HIGHEST
    )
    sent = lax.all_to_all(pack_routes(route_grads), "sp", split_axis=0, concat_axis=0, tiled=True)
    grads_train, grads_frozen = unpack_kinds(sent)
    gathered_grads = (
        lax.all_gather(grads_train, "dp", axis=0, tiled=True),
        lax.all_gather(grads_frozen, "dp", axis=0, tiled=True),
    )
    out_grad_train, out_grad_frozen = (gathered_grads[0], gathered_grads[1])
    pre_grad_train = gelu_backward(
        pre_train,
        jnp.einsum("rd,fd->rf", out_grad_train, second_train, preferred_element_type=jnp.float32),
    )
    pre_grad_frozen = gelu_backward(
        pre_frozen,
        jnp.einsum("rd,fd->rf", out_grad_frozen, second_frozen, preferred_element_type=jnp.float32),
    )
    first_grad = jnp.einsum(
        "rd,rf->df", inputs_train, pre_grad_train, preferred_element_type=jnp.float32
    )
    second_grad = jnp.einsum(
        "rf,rd->fd", hidden_train, out_grad_train, preferred_element_type=jnp.float32
    )
    part_train = pre_grad_train
    part_frozen = pre_grad_frozen
    returned = lax.psum_scatter(
        jnp.concatenate(
            [
                jnp.einsum(
                    "rf,df->rd", part_train, first_train, preferred_element_type=jnp.float32
                ),
                jnp.einsum(
                    "rf,df->rd", part_frozen, first_frozen, preferred_element_type=jnp.float32
                ),
            ],
            axis=1,
        ).astype(jnp.bfloat16),
        "dp",
        scatter_dimension=0,
        tiled=True,
    ).astype(jnp.float32)
    in_grad_train = returned[:, :model_width]
    in_grad_frozen = returned[:, model_width:]
    came_back = lax.all_to_all(
        pack_kinds(in_grad_train, in_grad_frozen), "sp", split_axis=0, concat_axis=0, tiled=True
    )
    routed_back = came_back.reshape(sp_count * 2 * capacity, model_width)[positions].astype(
        jnp.float32
    )
    grad_second = router_back + jnp.sum(routed_back.reshape(token_count, 2, model_width), axis=1)
    middle_part, gain_two_grad, shift_two_grad = second_pullback(grad_second)
    grad_middle = upstream + middle_part
    grad_branch = grad_middle.astype(jnp.bfloat16)
    out_proj_part = jnp.einsum(
        "td,te->de", attended_low, grad_branch, preferred_element_type=jnp.float32
    )
    grad_attended = jnp.einsum(
        "te,de->td", grad_branch, w_out, preferred_element_type=jnp.float32
    ).astype(jnp.bfloat16)
    grad_out_short = grad_attended[:split_at].reshape(seq_count, short_len, model_width)
    grad_out_long = grad_attended[split_at:].reshape(seq_count, long_len, model_width)
    delta_short = head_delta(grad_out_short, attended_short)
    delta_long = head_delta(grad_out_long, attended_long)

    def pass_sums(sums):
        return (
            shifted(sums[0].astype(jnp.bfloat16), "sp", -1).astype(jnp.float32),
            shifted(sums[1].astype(jnp.bfloat16), "sp", -1).astype(jnp.float32),
        )

    def revisit(step_index, kv_short, kv_long, grads):
        source = (my_index + step_index) % sp_count

        def revisit_compute_live(current):
            new_short = backward_block(
                current[0],
                current[2],
                query_short,
                grad_out_short,
                log_short,
                delta_short,
                kv_short,
                source == my_index,
            )
            new_long = backward_block(
                current[1],
                current[3],
                query_long,
                grad_out_long,
                log_long,
                delta_long,
                kv_long,
                source == my_index,
            )
            return (new_short[0], new_long[0], new_short[1], new_long[1])

        return lax.cond(source <= my_index, revisit_compute_live, lambda current: current, grads)

    def backward_turn(step_index, carry):
        kv_short, kv_long, grads = carry
        grads = revisit(step_index, kv_short, kv_long, grads)
        moved = pass_sums((grads[2], grads[3]))
        kv_short, kv_long = shifted((kv_short, kv_long), "sp", -1)
        return (kv_short, kv_long, (grads[0], grads[1], moved[0], moved[1]))

    start_grads = (
        jnp.zeros((seq_count, short_len, HEADS, HEAD_DIM), jnp.float32),
        jnp.zeros((seq_count, long_len, HEADS, HEAD_DIM), jnp.float32),
        jnp.zeros((seq_count, short_len, 2 * model_width), jnp.float32),
        jnp.zeros((seq_count, long_len, 2 * model_width), jnp.float32),
    )
    kv_short, kv_long, grads = lax.fori_loop(
        0, sp_count - 1, backward_turn, (keyval_short, keyval_long, start_grads)
    )
    grads = revisit(sp_count - 1, kv_short, kv_long, grads)
    moved = pass_sums((grads[2], grads[3]))
    qkv_short = jnp.concatenate(
        [grads[0].reshape(seq_count, short_len, model_width), moved[0]], axis=-1
    ).reshape(-1, 3 * model_width)
    qkv_long = jnp.concatenate(
        [grads[1].reshape(seq_count, long_len, model_width), moved[1]], axis=-1
    ).reshape(-1, 3 * model_width)
    grad_projected = jnp.concatenate([qkv_short, qkv_long], axis=0).astype(jnp.bfloat16)
    qkv_part = jnp.einsum(
        "td,te->de", first_norm, grad_projected, preferred_element_type=jnp.float32
    )
    grad_first = jnp.einsum("te,de->td", grad_projected, w_qkv, preferred_element_type=jnp.float32)
    input_part, gain_one_grad, shift_one_grad = first_pullback(grad_first)
    tokens_grad = grad_middle + input_part
    shared = lax.psum(
        (
            qkv_part,
            out_proj_part,
            router_part,
            gain_one_grad,
            shift_one_grad,
            gain_two_grad,
            shift_two_grad,
        ),
        ("sp", "dp"),
    )
    return (
        block_out[None],
        tokens_grad[None],
        shared[3],
        shared[4],
        shared[0],
        shared[1],
        shared[5],
        shared[6],
        shared[2],
        first_grad[None],
        second_grad[None],
    )


def solution(mesh):
    in_specs = (
        P("dp", "sp", None),
        P(),
        P(),
        P(),
        P(),
        P(),
        P(),
        P(),
        P("sp", None, "dp"),
        P("sp", "dp", None),
        P("sp", None, "dp"),
        P("sp", "dp", None),
        P("dp", "sp", None),
        P("dp", "sp", None),
    )
    out_specs = (
        P("dp", "sp", None),
        P("dp", "sp", None),
        P(),
        P(),
        P(),
        P(),
        P(),
        P(),
        P(),
        P("sp", None, "dp"),
        P("sp", "dp", None),
    )
    return jax.shard_map(shards, mesh=mesh, in_specs=in_specs, out_specs=out_specs, check_vma=False)
```

profile of v0, /device:TPU:0, one launch (start us, length us, event | category | flops | bytes accessed | tf_op | source)
XLA Modules:
  0.0 1708.9 jit_solution(15040450680066182224)
XLA Ops:
  44.9 133.4 %while.53 = (s32[]{:T(128)}, bf16[1,128,1536]{1,2,0:T(8,128)(2,1)}, bf16[1,256,1536]{1,2,0:T(8,128)(2,1)}, f32[1,12,128]{2,1,0:T(8,128)}, f32[1,12,128]{2,1,0:T(...) while((s32[]{:T(128)}, bf16[1,128,1536]{1,2,0:T(8,128)(2,1)}, ...), condition=%wide.region_9.10_spmd, body=%wide.region_2.9_spmd.sunk | while | flops 262452736 | bytes 37135072 | solution.py:193
  188.1 23.5 %scatter_custom_fusion = bf16[1536,768]{1,0:T(8,128)(2,1)} fusion(s32[768]{0:T(1024)S(1)} %fusion.167, bf16[384,768]{1,0:T(8,128)(2,1)} %add_convert_fusion.1, s32[1024]{0:T(1024)} %pad_clamp_fusion.1, bf16[]{:T(256)} %constant.168.clone.1), kind=kCustom, calls=%fused_computation.222 | custom fusion | bytes 2359808 | tf_op jit(solution)/shard_map/scatter | solution.py:227
  211.7 45.8 %all_to_all.20 = bf16[8,2,96,768]{3,2,1,0:T(8,128)(2,1)S(1)} all-to-all(bf16[8,2,96,768]{3,2,1,0:T(8,128)(2,1)} %bitcast.447), channel_id=1, replica_groups=mesh['sp'=8,'dp'=4] {'sp'}, dimensions={0} | all-to-all | bytes 4718592 | tf_op jit(solution)/shard_map/all_to_all | solution.py:246
  283.0 32.9 %all_to_all.21 = bf16[8,2,96,768]{3,2,1,0:T(8,128)(2,1)S(1)} all-to-all(bf16[8,2,96,768]{3,2,1,0:T(8,128)(2,1)} %bitcast.446), channel_id=1, replica_groups=mesh['sp'=8,'dp'=4] {'sp'}, dimensions={0} | all-to-all | bytes 4718592 | tf_op jit(solution)/shard_map/all_to_all | solution.py:301
  318.8 29.2 %all-gather.5.cloned.1.call-done = bf16[3072,768]{1,0:T(8,128)(2,1)} async-done(((bf16[768,768]{1,0:T(8,128)(2,1)}), bf16[3072,768]{1,0:T(8,128)(2,1)}) %all-gather.5.cloned.1.call-update) | async-done | bytes 4718608 | tf_op jit(solution)/shard_map/all_gather | solution.py:251
  358.6 79.4 %all-gather.9.cloned.1.call-done = bf16[3072,768]{1,0:T(8,128)(2,1)} async-done(((bf16[768,768]{1,0:T(8,128)(2,1)}), bf16[3072,768]{1,0:T(8,128)(2,1)}) %all-gather.9.cloned.1.call-update) | async-done | bytes 4718608 | tf_op jit(solution)/shard_map/all_gather | solution.py:304
  457.9 70.1 %all-gather.7.cloned.1.call-done = bf16[3072,768]{1,0:T(8,128)(2,1)} async-done(((bf16[768,768]{1,0:T(8,128)(2,1)}), bf16[3072,768]{1,0:T(8,128)(2,1)}) %all-gather.7.cloned.1.call-update) | async-done | bytes 4718608 | tf_op jit(solution)/shard_map/all_gather | solution.py:252
  538.7 79.3 %all-gather.11.cloned.1.call-done = bf16[3072,768]{1,0:T(8,128)(2,1)} async-done(((bf16[768,768]{1,0:T(8,128)(2,1)}), bf16[3072,768]{1,0:T(8,128)(2,1)}) %all-gather.11.cloned.1.call-update) | async-done | bytes 4718608 | tf_op jit(solution)/shard_map/all_gather | solution.py:305
  662.1 141.1 %reduce-scatter.5.cloned.1.call-done = bf16[768,1536]{0,1:T(8,128)(2,1)} async-done(((bf16[3072,1536]{0,1:T(8,128)(2,1)}), bf16[768,1536]{0,1:T(8,128)(2,1)}) %reduce-scatter.5.cloned.1.call-update) | async-done | bytes 2359312 | tf_op jit(solution)/shard_map/reduce_scatter | solution.py:324
  819.5 148.0 %reduce-scatter.3.cloned.1.call-done = bf16[768,1536]{0,1:T(8,128)(2,1)} async-done(((bf16[3072,1536]{0,1:T(8,128)(2,1)}), bf16[768,1536]{0,1:T(8,128)(2,1)}) %reduce-scatter.3.cloned.1.call-update) | async-done | bytes 2359312 | tf_op jit(solution)/shard_map/reduce_scatter | solution.py:263
  1061.8 388.2 %while.54 = (s32[]{:T(128)}, bf16[1,128,1536]{1,2,0:T(8,128)(2,1)}, bf16[1,256,1536]{1,2,0:T(8,128)(2,1)}, f32[1,128,12,64]{1,3,2,0:T(8,128)}, f32[1,256,12,64]{...) while((s32[]{:T(128)}, bf16[1,128,1536]{1,2,0:T(8,128)(2,1)}, ...), condition=%wide.region_40.41_spmd.clone, body=%wide.region_37.40_spmd.clone.sunk | while | flops 642383872 | bytes 83567656 | solution.py:410
  1123.4 20.5 %collective-permute-start.5 = (bf16[1,256,1536]{1,2,0:T(8,128)(2,1)}, bf16[1,256,1536]{1,2,0:T(8,128)(2,1)}, u32[]{:S(2)}, u32[]{:S(2)}) collective-permute-start(bf16[1,256,1536]{1,2,0:T(8,128)(2,1)} %convert_element_type.374), channel_id=1, source_target_pairs={{0,28},{4,0},{8,4},{12,8},{16,12},{20,16},{24,20},{28,24},{1,29},{... | collective-permute-start | bytes 2359304 | tf_op jit(solution)/shard_map/while/body/eval_jaxpr/ppermute | solution.py:26
  1145.8 20.5 %collective-permute-done.4 = bf16[1,128,1536]{1,2,0:T(8,128)(2,1)} collective-permute-done((bf16[1,128,1536]{1,2,0:T(8,128)(2,1)}, bf16[1,128,1536]{1,2,0:T(8,128)(2,1)}, u32[]{:S(2)}, u32[]{:S(2)}) %collective-permute-start.4) | collective-permute-done | bytes 393248 | tf_op jit(solution)/shard_map/while/body/eval_jaxpr/ppermute | solution.py:26
  1179.2 20.5 %collective-permute-start.5 = (bf16[1,256,1536]{1,2,0:T(8,128)(2,1)}, bf16[1,256,1536]{1,2,0:T(8,128)(2,1)}, u32[]{:S(2)}, u32[]{:S(2)}) collective-permute-start(bf16[1,256,1536]{1,2,0:T(8,128)(2,1)} %convert_element_type.374), channel_id=1, source_target_pairs={{0,28},{4,0},{8,4},{12,8},{16,12},{20,16},{24,20},{28,24},{1,29},{... | collective-permute-start | bytes 2359304 | tf_op jit(solution)/shard_map/while/body/eval_jaxpr/ppermute | solution.py:26
  1201.7 20.5 %collective-permute-done.4 = bf16[1,128,1536]{1,2,0:T(8,128)(2,1)} collective-permute-done((bf16[1,128,1536]{1,2,0:T(8,128)(2,1)}, bf16[1,128,1536]{1,2,0:T(8,128)(2,1)}, u32[]{:S(2)}, u32[]{:S(2)}) %collective-permute-start.4) | collective-permute-done | bytes 393248 | tf_op jit(solution)/shard_map/while/body/eval_jaxpr/ppermute | solution.py:26
  1235.1 20.5 %collective-permute-start.5 = (bf16[1,256,1536]{1,2,0:T(8,128)(2,1)}, bf16[1,256,1536]{1,2,0:T(8,128)(2,1)}, u32[]{:S(2)}, u32[]{:S(2)}) collective-permute-start(bf16[1,256,1536]{1,2,0:T(8,128)(2,1)} %convert_element_type.374), channel_id=1, source_target_pairs={{0,28},{4,0},{8,4},{12,8},{16,12},{20,16},{24,20},{28,24},{1,29},{... | collective-permute-start | bytes 2359304 | tf_op jit(solution)/shard_map/while/body/eval_jaxpr/ppermute | solution.py:26
  1257.5 20.5 %collective-permute-done.4 = bf16[1,128,1536]{1,2,0:T(8,128)(2,1)} collective-permute-done((bf16[1,128,1536]{1,2,0:T(8,128)(2,1)}, bf16[1,128,1536]{1,2,0:T(8,128)(2,1)}, u32[]{:S(2)}, u32[]{:S(2)}) %collective-permute-start.4) | collective-permute-done | bytes 393248 | tf_op jit(solution)/shard_map/while/body/eval_jaxpr/ppermute | solution.py:26
  1290.9 20.5 %collective-permute-start.5 = (bf16[1,256,1536]{1,2,0:T(8,128)(2,1)}, bf16[1,256,1536]{1,2,0:T(8,128)(2,1)}, u32[]{:S(2)}, u32[]{:S(2)}) collective-permute-start(bf16[1,256,1536]{1,2,0:T(8,128)(2,1)} %convert_element_type.374), channel_id=1, source_target_pairs={{0,28},{4,0},{8,4},{12,8},{16,12},{20,16},{24,20},{28,24},{1,29},{... | collective-permute-start | bytes 2359304 | tf_op jit(solution)/shard_map/while/body/eval_jaxpr/ppermute | solution.py:26
  1313.4 20.5 %collective-permute-done.4 = bf16[1,128,1536]{1,2,0:T(8,128)(2,1)} collective-permute-done((bf16[1,128,1536]{1,2,0:T(8,128)(2,1)}, bf16[1,128,1536]{1,2,0:T(8,128)(2,1)}, u32[]{:S(2)}, u32[]{:S(2)}) %collective-permute-start.4) | collective-permute-done | bytes 393248 | tf_op jit(solution)/shard_map/while/body/eval_jaxpr/ppermute | solution.py:26
  1369.2 20.5 %collective-permute-done.4 = bf16[1,128,1536]{1,2,0:T(8,128)(2,1)} collective-permute-done((bf16[1,128,1536]{1,2,0:T(8,128)(2,1)}, bf16[1,128,1536]{1,2,0:T(8,128)(2,1)}, u32[]{:S(2)}, u32[]{:S(2)}) %collective-permute-start.4) | collective-permute-done | bytes 393248 | tf_op jit(solution)/shard_map/while/body/eval_jaxpr/ppermute | solution.py:26
  1425.1 20.5 %collective-permute-done.4 = bf16[1,128,1536]{1,2,0:T(8,128)(2,1)} collective-permute-done((bf16[1,128,1536]{1,2,0:T(8,128)(2,1)}, bf16[1,128,1536]{1,2,0:T(8,128)(2,1)}, u32[]{:S(2)}, u32[]{:S(2)}) %collective-permute-start.4) | collective-permute-done | bytes 393248 | tf_op jit(solution)/shard_map/while/body/eval_jaxpr/ppermute | solution.py:26
  1455.6 21.7 %collective-permute-start.7 = (bf16[1,256,1536]{1,2,0:T(8,128)(2,1)S(1)}, bf16[1,256,1536]{1,2,0:T(8,128)(2,1)S(1)}, u32[]{:S(2)}, u32[]{:S(2)}) collective-permute-start(bf16[1,256,1536]{1,2,0:T(8,128)(2,1)S(1)} %convert_element_type.256), channel_id=1, source_target_pairs={{0,28},{4,0},{8,4},{12,8},{16,12},{20,16},{24,20},{28,24},{1,29},{... | collective-permute-start | bytes 2359304 | tf_op jit(solution)/shard_map/ppermute | solution.py:26
  1525.0 42.9 %all-reduce = (f32[768]{0:T(1024)}, f32[768]{0:T(1024)}, f32[768]{0:T(1024)}, f32[768]{0:T(1024)}, f32[768,16]{0,1:T(8,128)}) all-reduce(f32[768]{0:T(1024)} %get-tuple-element.1294, f32[768]{0:T(1024)} %get-tuple-element.1297, f32[768]{0:T(1024)} %get-tuple-element.1290, ...), channel_id=1, replica_groups=mesh['sp'=8,'dp'=4] {'sp','dp'}, use_global_device_ids=true, to_apply=%region_46.47 | all-reduce | flops 15360 | bytes 122880 | tf_op jit(solution)/shard_map/psum | solution.py:428
  1572.0 121.9 %all-reduce.4.cloned.1.call-done = (f32[768,2304]{1,0:T(8,128)}, f32[768,768]{1,0:T(8,128)}) async-done(((f32[768,2304]{1,0:T(8,128)}, f32[768,768]{1,0:T(8,128)}), (f32[768,2304]{1,0:T(8,128)}, f32[768,768]{1,0:T(8,128)})) %all-reduce.4.cloned.1.call-update) | async-done | bytes 9437200 | tf_op jit(solution)/shard_map/psum | solution.py:428
  (524 shorter events, 686.4 us)
Async XLA Ops:
  7.2 340.8 %all-gather.5.cloned.1.call-start = ((), (), s32[]{:S(2)}) async-start(), calls=%async_computation.6 | async-start | bytes 5898240 | tf_op jit(solution)/shard_map/all_gather | solution.py:251
  259.1 179.0 %all-gather.9.cloned.1.call-start = ((), (), s32[]{:S(2)}) async-start(), calls=%async_computation.9 | async-start | bytes 5898240 | tf_op jit(solution)/shard_map/all_gather | solution.py:304
  317.5 210.6 %all-gather.7.cloned.1.call-start = ((), (), s32[]{:S(2)}) async-start(), calls=%async_computation.7 | async-start | bytes 5898240 | tf_op jit(solution)/shard_map/all_gather | solution.py:252
  318.2 299.8 %all-gather.11.cloned.1.call-start = ((), (), s32[]{:S(2)}) async-start(), calls=%async_computation.10 | async-start | bytes 5898240 | tf_op jit(solution)/shard_map/all_gather | solution.py:305
  318.8 484.4 %reduce-scatter.5.cloned.1.call-start = ((), (), s32[]{:S(2)}) async-start(), calls=%async_computation.11 | async-start | bytes 11796480 | tf_op jit(solution)/shard_map/reduce_scatter | solution.py:324
  643.3 324.3 %reduce-scatter.3.cloned.1.call-start = ((), (), s32[]{:S(2)}) async-start(), calls=%async_computation.8 | async-start | bytes 11796480 | tf_op jit(solution)/shard_map/reduce_scatter | solution.py:263
  815.1 163.8 %all-to-all-start.3 = ((bf16[8,2,96,768]{3,2,1,0:T(8,128)(2,1)}), bf16[8,2,96,768]{3,2,1,0:T(8,128)(2,1)}, u32[]{:S(2)}, u32[]{:S(2)}) async-start(bf16[8,2,96,768]{3,2,1,0:T(8,128)(2,1)} %copy.176), calls=%async_computation.5 | async-start | bytes 4718592 | tf_op jit(solution)/shard_map/all_to_all | solution.py:342
  978.9 33.9 %all-to-all-start.1 = ((bf16[8,2,96,768]{3,2,1,0:T(8,128)(2,1)}), bf16[8,2,96,768]{3,2,1,0:T(8,128)(2,1)}, u32[]{:S(2)}, u32[]{:S(2)}) async-start(bf16[8,2,96,768]{3,2,1,0:T(8,128)(2,1)} %copy.170), calls=%async_computation.2 | async-start | bytes 4718592 | tf_op jit(solution)/shard_map/all_to_all | solution.py:277
  983.3 710.6 %all-reduce.4.cloned.1.call-start = ((), (), s32[]{:S(2)}) async-start(), calls=%async_computation.12 | async-start | bytes 18874368 | tf_op jit(solution)/shard_map/psum | solution.py:428
  1088.0 26.8 %collective-permute-start.3 = (bf16[1,256,1536]{1,2,0:T(8,128)(2,1)}, bf16[1,256,1536]{1,2,0:T(8,128)(2,1)}, u32[]{:S(2)}, u32[]{:S(2)}) collective-permute-start(bf16[1,256,1536]{1,2,0:T(8,128)(2,1)} %copy.263), channel_id=1, source_target_pairs={{0,28},{4,0},{8,4},{12,8},{16,12},{20,16},{24,20},{28,24},{1,29},{... | collective-permute-start | bytes 2359304 | tf_op jit(solution)/shard_map/while/body/eval_jaxpr/ppermute | solution.py:26
  1123.4 44.9 %collective-permute-start.5 = (bf16[1,256,1536]{1,2,0:T(8,128)(2,1)}, bf16[1,256,1536]{1,2,0:T(8,128)(2,1)}, u32[]{:S(2)}, u32[]{:S(2)}) collective-permute-start(bf16[1,256,1536]{1,2,0:T(8,128)(2,1)} %convert_element_type.374), channel_id=1, source_target_pairs={{0,28},{4,0},{8,4},{12,8},{16,12},{20,16},{24,20},{28,24},{1,29},{... | collective-permute-start | bytes 2359304 | tf_op jit(solution)/shard_map/while/body/eval_jaxpr/ppermute | solution.py:26
  1143.8 26.8 %collective-permute-start.3 = (bf16[1,256,1536]{1,2,0:T(8,128)(2,1)}, bf16[1,256,1536]{1,2,0:T(8,128)(2,1)}, u32[]{:S(2)}, u32[]{:S(2)}) collective-permute-start(bf16[1,256,1536]{1,2,0:T(8,128)(2,1)} %copy.263), channel_id=1, source_target_pairs={{0,28},{4,0},{8,4},{12,8},{16,12},{20,16},{24,20},{28,24},{1,29},{... | collective-permute-start | bytes 2359304 | tf_op jit(solution)/shard_map/while/body/eval_jaxpr/ppermute | solution.py:26
  1145.8 24.9 %collective-permute-start.2 = (bf16[1,128,1536]{1,2,0:T(8,128)(2,1)}, bf16[1,128,1536]{1,2,0:T(8,128)(2,1)}, u32[]{:S(2)}, u32[]{:S(2)}) collective-permute-start(bf16[1,128,1536]{1,2,0:T(8,128)(2,1)} %copy.262), channel_id=1, source_target_pairs={{0,28},{4,0},{8,4},{12,8},{16,12},{20,16},{24,20},{28,24},{1,29},{... | collective-permute-start | bytes 1179656 | tf_op jit(solution)/shard_map/while/body/eval_jaxpr/ppermute | solution.py:26
  1179.2 44.9 %collective-permute-start.5 = (bf16[1,256,1536]{1,2,0:T(8,128)(2,1)}, bf16[1,256,1536]{1,2,0:T(8,128)(2,1)}, u32[]{:S(2)}, u32[]{:S(2)}) collective-permute-start(bf16[1,256,1536]{1,2,0:T(8,128)(2,1)} %convert_element_type.374), channel_id=1, source_target_pairs={{0,28},{4,0},{8,4},{12,8},{16,12},{20,16},{24,20},{28,24},{1,29},{... | collective-permute-start | bytes 2359304 | tf_op jit(solution)/shard_map/while/body/eval_jaxpr/ppermute | solution.py:26
  1199.7 26.8 %collective-permute-start.3 = (bf16[1,256,1536]{1,2,0:T(8,128)(2,1)}, bf16[1,256,1536]{1,2,0:T(8,128)(2,1)}, u32[]{:S(2)}, u32[]{:S(2)}) collective-permute-start(bf16[1,256,1536]{1,2,0:T(8,128)(2,1)} %copy.263), channel_id=1, source_target_pairs={{0,28},{4,0},{8,4},{12,8},{16,12},{20,16},{24,20},{28,24},{1,29},{... | collective-permute-start | bytes 2359304 | tf_op jit(solution)/shard_map/while/body/eval_jaxpr/ppermute | solution.py:26
  1235.1 44.9 %collective-permute-start.5 = (bf16[1,256,1536]{1,2,0:T(8,128)(2,1)}, bf16[1,256,1536]{1,2,0:T(8,128)(2,1)}, u32[]{:S(2)}, u32[]{:S(2)}) collective-permute-start(bf16[1,256,1536]{1,2,0:T(8,128)(2,1)} %convert_element_type.374), channel_id=1, source_target_pairs={{0,28},{4,0},{8,4},{12,8},{16,12},{20,16},{24,20},{28,24},{1,29},{... | collective-permute-start | bytes 2359304 | tf_op jit(solution)/shard_map/while/body/eval_jaxpr/ppermute | solution.py:26
  1255.5 26.8 %collective-permute-start.3 = (bf16[1,256,1536]{1,2,0:T(8,128)(2,1)}, bf16[1,256,1536]{1,2,0:T(8,128)(2,1)}, u32[]{:S(2)}, u32[]{:S(2)}) collective-permute-start(bf16[1,256,1536]{1,2,0:T(8,128)(2,1)} %copy.263), channel_id=1, source_target_pairs={{0,28},{4,0},{8,4},{12,8},{16,12},{20,16},{24,20},{28,24},{1,29},{... | collective-permute-start | bytes 2359304 | tf_op jit(solution)/shard_map/while/body/eval_jaxpr/ppermute | solution.py:26
  1290.9 44.9 %collective-permute-start.5 = (bf16[1,256,1536]{1,2,0:T(8,128)(2,1)}, bf16[1,256,1536]{1,2,0:T(8,128)(2,1)}, u32[]{:S(2)}, u32[]{:S(2)}) collective-permute-start(bf16[1,256,1536]{1,2,0:T(8,128)(2,1)} %convert_element_type.374), channel_id=1, source_target_pairs={{0,28},{4,0},{8,4},{12,8},{16,12},{20,16},{24,20},{28,24},{1,29},{... | collective-permute-start | bytes 2359304 | tf_op jit(solution)/shard_map/while/body/eval_jaxpr/ppermute | solution.py:26
  1311.4 26.8 %collective-permute-start.3 = (bf16[1,256,1536]{1,2,0:T(8,128)(2,1)}, bf16[1,256,1536]{1,2,0:T(8,128)(2,1)}, u32[]{:S(2)}, u32[]{:S(2)}) collective-permute-start(bf16[1,256,1536]{1,2,0:T(8,128)(2,1)} %copy.263), channel_id=1, source_target_pairs={{0,28},{4,0},{8,4},{12,8},{16,12},{20,16},{24,20},{28,24},{1,29},{... | collective-permute-start | bytes 2359304 | tf_op jit(solution)/shard_map/while/body/eval_jaxpr/ppermute | solution.py:26
  1346.8 44.9 %collective-permute-start.5 = (bf16[1,256,1536]{1,2,0:T(8,128)(2,1)}, bf16[1,256,1536]{1,2,0:T(8,128)(2,1)}, u32[]{:S(2)}, u32[]{:S(2)}) collective-permute-start(bf16[1,256,1536]{1,2,0:T(8,128)(2,1)} %convert_element_type.374), channel_id=1, source_target_pairs={{0,28},{4,0},{8,4},{12,8},{16,12},{20,16},{24,20},{28,24},{1,29},{... | collective-permute-start | bytes 2359304 | tf_op jit(solution)/shard_map/while/body/eval_jaxpr/ppermute | solution.py:26
  1367.3 26.8 %collective-permute-start.3 = (bf16[1,256,1536]{1,2,0:T(8,128)(2,1)}, bf16[1,256,1536]{1,2,0:T(8,128)(2,1)}, u32[]{:S(2)}, u32[]{:S(2)}) collective-permute-start(bf16[1,256,1536]{1,2,0:T(8,128)(2,1)} %copy.263), channel_id=1, source_target_pairs={{0,28},{4,0},{8,4},{12,8},{16,12},{20,16},{24,20},{28,24},{1,29},{... | collective-permute-start | bytes 2359304 | tf_op jit(solution)/shard_map/while/body/eval_jaxpr/ppermute | solution.py:26
  1402.6 44.9 %collective-permute-start.5 = (bf16[1,256,1536]{1,2,0:T(8,128)(2,1)}, bf16[1,256,1536]{1,2,0:T(8,128)(2,1)}, u32[]{:S(2)}, u32[]{:S(2)}) collective-permute-start(bf16[1,256,1536]{1,2,0:T(8,128)(2,1)} %convert_element_type.374), channel_id=1, source_target_pairs={{0,28},{4,0},{8,4},{12,8},{16,12},{20,16},{24,20},{28,24},{1,29},{... | collective-permute-start | bytes 2359304 | tf_op jit(solution)/shard_map/while/body/eval_jaxpr/ppermute | solution.py:26
  1423.1 26.8 %collective-permute-start.3 = (bf16[1,256,1536]{1,2,0:T(8,128)(2,1)}, bf16[1,256,1536]{1,2,0:T(8,128)(2,1)}, u32[]{:S(2)}, u32[]{:S(2)}) collective-permute-start(bf16[1,256,1536]{1,2,0:T(8,128)(2,1)} %copy.263), channel_id=1, source_target_pairs={{0,28},{4,0},{8,4},{12,8},{16,12},{20,16},{24,20},{28,24},{1,29},{... | collective-permute-start | bytes 2359304 | tf_op jit(solution)/shard_map/while/body/eval_jaxpr/ppermute | solution.py:26
  1455.6 36.4 %collective-permute-start.7 = (bf16[1,256,1536]{1,2,0:T(8,128)(2,1)S(1)}, bf16[1,256,1536]{1,2,0:T(8,128)(2,1)S(1)}, u32[]{:S(2)}, u32[]{:S(2)}) collective-permute-start(bf16[1,256,1536]{1,2,0:T(8,128)(2,1)S(1)} %convert_element_type.256), channel_id=1, source_target_pairs={{0,28},{4,0},{8,4},{12,8},{16,12},{20,16},{24,20},{28,24},{1,29},{... | collective-permute-start | bytes 2359304 | tf_op jit(solution)/shard_map/ppermute | solution.py:26
  (123 other events, 1058.3 us)
Sparse Core Ops, SparseCore 0:
  259.2 88.7 all-gather.4
  350.1 87.8 all-gather.8
  440.2 87.8 all-gather.6
  530.1 87.8 all-gather.10
  643.4 159.7 reduce-scatter.4
  805.4 162.1 reduce-scatter.2
  1499.8 194.0 all-reduce.3
where the time goes:
time: 1720 us; the launch traced here: 1710 us
  waiting for transfers between devices  848 us (49%)
  starting transfers between devices  247 us (14%)
  local copies, waits for them, and re-layouts  193 us (11%)
  other arithmetic  162 us (9%)
  matrix products  122 us (7%)
  blocking collectives  122 us (7%)
    ppermute x30, waiting for transfers between devices, shifted(): return lax.ppermute(value, axis, pairs)  153 us
    reduce_scatter x1, waiting for transfers between devices, shards(): lax.psum_scatter(jnp.concatenate([jnp.dot(part_train, second_train, prefe...  148 us
    ppermute x30, starting transfers between devices, shifted(): return lax.ppermute(value, axis, pairs)  147 us
    reduce_scatter x1, waiting for transfers between devices, shards(): lax.psum_scatter(jnp.concatenate([jnp.einsum('rf,df->rd', part_train, fir...  141 us
    psum x1, waiting for transfers between devices, shards(): lax.psum((qkv_part, out_proj_part, router_part, gain_one_grad, shift_one_...  122 us
    ppermute x14, starting transfers between devices, from_behind(): lax.ppermute(value, axis, [(source, source + steps) for source in range(f...  90.6 us
    all_gather x1, waiting for transfers between devices, shards(): lax.all_gather(grads_train, 'dp', axis=0, tiled=True)  79.4 us
    all_gather x1, waiting for transfers between devices, shards(): lax.all_gather(grads_frozen, 'dp', axis=0, tiled=True)  79.3 us
  transfers between devices with their start and end apart: 53, of which 22 were waited for; matrix products, arithmetic and copies ran while one was open for 12% of the time, Pallas kernels for 0%

commit v1 on v0

v1 whole, which is shorter than its diff:
```python
import functools

import jax
import jax.numpy as jnp
from jax import lax
from jax.experimental import pallas as pl
from jax.experimental.pallas import tpu as pltpu
from jax.sharding import PartitionSpec as P

HEADS = 12
HEAD_DIM = 64
LEN_A = 1024
LEN_B = 2048
PAIRS = HEADS // 2
WIDE = 2 * HEAD_DIM
UNIT = 3 * LEN_A
BLOCK = 256
EPSILON = 1e-05
NEGATIVE = -1e30
MESH = pl.DeviceIdType.MESH
DMA = pltpu.SemaphoreType.DMA
F32 = jnp.float32
BF16 = jnp.bfloat16
VMEM = pl.BlockSpec(memory_space=pltpu.VMEM)


def dot(a, b):
    return jnp.dot(a, b, preferred_element_type=F32)


def dot_t(a, b):
    return lax.dot_general(a, b, (((1,), (1,)), ((), ())), preferred_element_type=F32)


def t_dot(a, b):
    return lax.dot_general(a, b, (((0,), (0,)), ((), ())), preferred_element_type=F32)


def normed(value):
    centre = jnp.mean(value, axis=-1, keepdims=True)
    centred = value - centre
    spread = jnp.mean(centred * centred, axis=-1, keepdims=True)
    scale = lax.rsqrt(spread + EPSILON)
    return centred * scale, scale


def norm_back(grad, gain, hat, scale):
    scaled = grad * gain
    first = jnp.mean(scaled, axis=-1, keepdims=True)
    second = jnp.mean(scaled * hat, axis=-1, keepdims=True)
    return (scaled - first - hat * second) * scale


class Layout:
    def __init__(self, n_sp):
        self.n = n_sp
        self.sequences = n_sp // 8
        self.short = LEN_A // n_sp
        self.long = LEN_B // n_sp
        self.split = self.sequences * self.short

    def owners(self):
        found = []
        for seq in range(self.sequences):
            for pair in range(PAIRS):
                number = seq * PAIRS + pair
                found.append((number + number // 3 + 1, True, self.split + seq * self.long, self.long, pair, 0))
                found.append((4 * (seq * 2 + pair // 3), False, seq * self.short, self.short, pair, (pair % 3) * LEN_A))
        return found

    def role(self, me):
        is_short = lax.rem(me, 4) == 0
        number = me - me // 4 - 1
        group = me // 4
        seq = jnp.where(is_short, group // 2, number // PAIRS)
        pair = jnp.where(is_short, 3 * lax.rem(group, 2), lax.rem(number, PAIRS))
        return is_short, seq, pair

    def task(self, is_short, index):
        per = LEN_A // BLOCK
        start = jnp.where(is_short, (index // per) * LEN_A, 0)
        block = jnp.where(is_short, lax.rem(index, per), index)
        return pl.multiple_of(start, BLOCK), block

    def tasks(self, is_short):
        return jnp.where(is_short, 3 * LEN_A // BLOCK, LEN_B // BLOCK)


def greet(n):
    me = lax.axis_index("sp")
    barrier = pltpu.get_barrier_semaphore()
    for step in range(1, n):
        pl.semaphore_signal(barrier, inc=1, device_id={"sp": lax.rem(me + step, n)}, device_id_type=MESH)
    pl.semaphore_wait(barrier, n - 1)


def remote(source, target, send_sem, recv_sem, device):
    return pltpu.make_async_remote_copy(
        src_ref=source, dst_ref=target, send_sem=send_sem, recv_sem=recv_sem, device_id={"sp": device}, device_id_type=MESH
    )


def lanes_first():
    return lax.broadcasted_iota(jnp.int32, (1, WIDE), 1) < HEAD_DIM


def halves(value):
    keep = lanes_first()
    zero = jnp.zeros_like(value)
    return jnp.where(keep, value, zero), jnp.where(keep, zero, value)


def causal(rows):
    return lax.broadcasted_iota(jnp.int32, (rows, rows), 0) >= lax.broadcasted_iota(jnp.int32, (rows, rows), 1)


def to_owners(lay, me, cols, slot, source, target, send_sems, recv_sem, local_sem, wanted):
    started = []
    for number, (owner, is_long, start, rows, pair, unit) in enumerate(lay.owners()):
        if pair not in wanted:
            continue
        piece = source.at[pl.ds(start, rows), pl.ds(cols(pair), WIDE)]
        place = target(unit + me * rows, rows)
        far = remote(piece, place, send_sems.at[slot(number)], recv_sem, owner)
        near = pltpu.make_async_copy(piece, place, local_sem)

        @pl.when(me != owner)
        def _():
            far.start()

        @pl.when(me == owner)
        def _():
            near.start()
            near.wait()

        started.append((owner, far))
    return started


def finish_sends(me, started):
    for owner, copy in started:

        @pl.when(me != owner)
        def _():
            copy.wait_send()


def wait_unit(lay, is_short, buffer, sem):
    for short, rows in ((True, 3 * (lay.n - 1) * lay.short), (False, (lay.n - 1) * lay.long)):

        @pl.when(is_short == short)
        def _():
            piece = buffer.at[pl.ds(0, rows)]
            pltpu.make_async_copy(piece, piece, sem).wait()


def send_home(lay, me, is_short, seq, first_pair, base, block, unit_start, source, target, base_col, send_sem, recv_sem, local_sem):
    for short, rows in ((True, lay.short), (False, lay.long)):

        @pl.when(is_short == short)
        def _():
            pair = first_pair + (unit_start // LEN_A if short else 0)
            column = pl.multiple_of(base_col + pair * WIDE, WIDE)
            first = pl.multiple_of(seq * rows + (0 if short else lay.split), 16)
            for part in range(BLOCK // rows):
                home = block * (BLOCK // rows) + part
                piece = source.at[pl.ds(pl.multiple_of(base + part * rows, 16), rows)]
                place = target.at[pl.ds(first, rows), pl.ds(column, WIDE)]

                @pl.when(home != me)
                def _():
                    remote(piece, place, send_sem, recv_sem, home).start()

                @pl.when(home == me)
                def _():
                    near = pltpu.make_async_copy(piece, place, local_sem)
                    near.start()
                    near.wait()


def wait_home(lay, is_short, scratch, sem, tensors, sent):
    for short in (True, False):
        own = 3 * lay.short if short else lay.long
        if sent:
            rows = (3 * LEN_A if short else LEN_B) - own
        else:
            rows = PAIRS * lay.sequences * (lay.short + lay.long) - own

        @pl.when(is_short == short)
        def _():
            for _ in range(tensors):
                piece = scratch.at[pl.ds(0, rows)]
                pltpu.make_async_copy(piece, piece, sem).wait()


def attend_kernel(
    lay, tokens, gain, shift, w_qkv, first_norm, unit, attended, log_total, home, staged, staged_out, send, recv, out_send, home_recv, local
):
    me = lax.axis_index("sp")
    is_short, seq, first_pair = lay.role(me)
    greet(lay.n)
    hat, _ = normed(tokens[...].astype(F32))
    first_norm[...] = (hat * gain[...] + shift[...]).astype(BF16)
    started = []
    for chunk in range(9):
        kind, third = divmod(chunk, 3)
        made = dot(first_norm[...], w_qkv[:, chunk * 2 * WIDE : (chunk + 1) * 2 * WIDE]).astype(BF16)
        staged[chunk] = made * BF16(HEAD_DIM**-0.5) if kind == 0 else made
        count = len(lay.owners())
        started += to_owners(
            lay,
            me,
            lambda pair: (pair % 2) * WIDE,
            lambda number: chunk * count + number,
            staged.at[chunk],
            lambda start, rows: unit.at[kind, pl.ds(pl.multiple_of(start, 16), rows)],
            send,
            recv.at[kind],
            local,
            (2 * third, 2 * third + 1),
        )
    for kind in range(3):
        wait_unit(lay, is_short, unit.at[kind], recv.at[kind])
    keep = lanes_first()
    lower = causal(BLOCK)

    def task(index, carry):
        start, block = lay.task(is_short, index)
        base = pl.multiple_of(start + block * BLOCK, BLOCK)
        queries = halves(unit[0, pl.ds(base, BLOCK)])

        def visit(place, state, diagonal):
            keys = unit[1, pl.ds(place, BLOCK)]
            values = unit[2, pl.ds(place, BLOCK)]
            result = []
            for (peak, total, summed), query in zip(state, queries):
                scores = dot_t(query, keys)
                if diagonal:
                    scores = jnp.where(lower, scores, NEGATIVE)
                new_peak = jnp.maximum(peak, jnp.max(scores, axis=1, keepdims=True))
                factor = jnp.exp(peak - new_peak)
                weight = jnp.exp(scores - new_peak)
                total = total * factor + jnp.sum(weight, axis=1, keepdims=True)
                summed = summed * factor + dot(weight.astype(BF16), values)
                result.append((new_peak, total, summed))
            return tuple(result)

        empty = (jnp.full((BLOCK, 1), NEGATIVE, F32), jnp.zeros((BLOCK, 1), F32), jnp.zeros((BLOCK, WIDE), F32))
        state = lax.fori_loop(
            0, block, lambda j, state: visit(pl.multiple_of(start + j * BLOCK, BLOCK), state, False), (empty, empty)
        )
        (peak_a, total_a, summed_a), (peak_b, total_b, summed_b) = visit(base, state, True)
        result = jnp.where(keep, summed_a / total_a, summed_b / total_b)
        attended[pl.ds(base, BLOCK)] = result
        staged_out[pl.ds(base, BLOCK)] = result.astype(BF16)
        log_total[pl.ds(base, BLOCK)] = jnp.where(keep, peak_a + jnp.log(total_a), peak_b + jnp.log(total_b))
        send_home(
            lay, me, is_short, seq, first_pair, base, block, start, staged_out, home, 0, out_send, home_recv, local
        )
        return carry

    lax.fori_loop(0, lay.tasks(is_short), task, 0)
    finish_sends(me, started)
    wait_home(lay, is_short, staged_out, out_send, 1, True)
    wait_home(lay, is_short, staged_out, home_recv, 1, False)


def attend(lay, tokens, gain, shift, w_qkv):
    count, width = tokens.shape
    owners = len(lay.owners())
    return pl.pallas_call(
        functools.partial(attend_kernel, lay),
        out_shape=(
            jax.ShapeDtypeStruct((count, width), BF16),
            jax.ShapeDtypeStruct((3, UNIT, WIDE), BF16),
            jax.ShapeDtypeStruct((UNIT, WIDE), F32),
            jax.ShapeDtypeStruct((UNIT, WIDE), F32),
            jax.ShapeDtypeStruct((count, width), BF16),
        ),
        in_specs=[VMEM] * 4,
        out_specs=[VMEM] * 5,
        scratch_shapes=[
            pltpu.VMEM((9, count, 2 * WIDE), BF16),
            pltpu.VMEM((UNIT, WIDE), BF16),
            DMA((9 * owners,)),
            DMA((3,)),
            DMA,
            DMA,
            DMA,
        ],
        compiler_params=pltpu.CompilerParams(collective_id=0, has_side_effects=True, vmem_limit_bytes=48 * 2**20),
        cost_estimate=pl.CostEstimate(flops=6 * 10**9, bytes_accessed=20 * 2**20, transcendentals=5 * 10**6),
        name="attend",
    )(tokens, gain, shift, w_qkv)


def one_hot_rows(lay, capacity, routes_t):
    n = lay.n
    experts, count = 2 * n, routes_t.shape[1]
    index = lax.broadcasted_iota(jnp.int32, (experts, count), 0)
    matches = [(index == routes_t[c : c + 1]).astype(F32) for c in range(2)]
    earlier = (
        lax.broadcasted_iota(jnp.int32, (count, count), 0) < lax.broadcasted_iota(jnp.int32, (count, count), 1)
    ).astype(F32)
    rank = dot((matches[0] + matches[1]).astype(BF16), earlier.astype(BF16))
    place = rank + (((index % n) * 2 + index // n) * capacity).astype(F32)
    slots = lax.broadcasted_iota(jnp.int32, (experts * capacity, count), 0)
    return [(slots == jnp.sum(m * place, axis=0, keepdims=True).astype(jnp.int32)).astype(F32).astype(BF16) for m in matches]


def one_hot_columns(lay, capacity, routes):
    n = lay.n
    experts, count = 2 * n, routes.shape[0]
    index = lax.broadcasted_iota(jnp.int32, (count, 128), 1)
    matches = [(index == routes[:, c : c + 1]).astype(F32) for c in range(2)]
    earlier = (
        lax.broadcasted_iota(jnp.int32, (count, count), 0) > lax.broadcasted_iota(jnp.int32, (count, count), 1)
    ).astype(F32)
    rank = dot(earlier.astype(BF16), (matches[0] + matches[1]).astype(BF16))
    place = rank + (((index % n) * 2 + index // n) * capacity).astype(F32)
    slots = lax.broadcasted_iota(jnp.int32, (count, experts * capacity), 1)
    hot = [(slots == jnp.sum(m * place, axis=1, keepdims=True).astype(jnp.int32)).astype(F32).astype(BF16) for m in matches]
    return hot, matches


def dispatch_kernel(
    lay, capacity, tokens, attended, w_out, gain, shift, w_router, routes, routes_t, cotangent,
    middle_out, second_out, gates_out, rows_in, rows_grad, packed, packed_grad, send, recv, local,
):
    n = lay.n
    me = lax.axis_index("sp")
    greet(n)
    middle = tokens[...].astype(F32) + dot(attended[...], w_out[...])
    middle_out[...] = middle
    hat, _ = normed(middle)
    second = (hat * gain[...] + shift[...]).astype(BF16)
    second_out[...] = second
    hot = one_hot_rows(lay, capacity, routes_t[...])
    started = []

    def spread(source, target, which):
        for kind in range(2):
            near = pltpu.make_async_copy(
                source.at[pl.ds(pl.multiple_of((me * 2 + kind) * capacity, 16), capacity)],
                target.at[kind, pl.ds(pl.multiple_of(me * capacity, 16), capacity)],
                local.at[which, kind],
            )
            near.start()
            for step in range(1, n):
                to = lax.rem(me + step, n)
                copy = remote(
                    source.at[pl.ds(pl.multiple_of((to * 2 + kind) * capacity, 16), capacity)],
                    target.at[kind, pl.ds(pl.multiple_of(me * capacity, 16), capacity)],
                    send.at[which, kind, step],
                    recv.at[which, kind, step],
                    to,
                )
                copy.start()
                started.append(copy)
            started.append(near)

    packed[...] = dot(hot[0] + hot[1], second).astype(BF16)
    spread(packed, rows_in, 0)
    logits = dot(second, w_router[...])
    index = lax.broadcasted_iota(jnp.int32, logits.shape, 1)
    chosen = [jnp.sum(jnp.where(index == routes[:, c : c + 1], logits, 0.0), axis=1, keepdims=True) for c in range(2)]
    top = jnp.maximum(chosen[0], chosen[1])
    exped = [jnp.exp(value - top) for value in chosen]
    gates = [value / (exped[0] + exped[1]) for value in exped]
    upstream = cotangent[...].astype(F32)
    lane = lax.broadcasted_iota(jnp.int32, gates_out.shape, 1)
    gates_out[...] = jnp.where(lane == 0, gates[0], gates[1])
    packed_grad[...] = (
        dot(hot[0], (gates[0] * upstream).astype(BF16)) + dot(hot[1], (gates[1] * upstream).astype(BF16))
    ).astype(BF16)
    spread(packed_grad, rows_grad, 1)
    for copy in started:
        copy.wait()


def dispatch(lay, capacity, tokens, attended, w_out, gain, shift, w_router, routes, cotangent):
    count, width = tokens.shape
    n = lay.n
    slots = 2 * n * capacity
    return pl.pallas_call(
        functools.partial(dispatch_kernel, lay, capacity),
        out_shape=(
            jax.ShapeDtypeStruct((count, width), F32),
            jax.ShapeDtypeStruct((count, width), BF16),
            jax.ShapeDtypeStruct((count, 128), F32),
            jax.ShapeDtypeStruct((2, n * capacity, width), BF16),
            jax.ShapeDtypeStruct((2, n * capacity, width), BF16),
        ),
        in_specs=[VMEM] * 9,
        out_specs=[VMEM] * 5,
        scratch_shapes=[
            pltpu.VMEM((slots, width), BF16),
            pltpu.VMEM((slots, width), BF16),
            DMA((2, 2, n)),
            DMA((2, 2, n)),
            DMA((2, 2)),
        ],
        compiler_params=pltpu.CompilerParams(collective_id=1, has_side_effects=True, vmem_limit_bytes=48 * 2**20),
        cost_estimate=pl.CostEstimate(flops=4 * 10**9, bytes_accessed=20 * 2**20, transcendentals=10**4),
        name="dispatch",
    )(tokens, attended, w_out, gain, shift, w_router, routes, routes.T, cotangent)


ROWS = 256


def gelu_parts(value):
    root = 0.7978845608028654
    square = value * value
    bent = jnp.tanh(root * value * (1.0 + 0.044715 * square))
    half = 0.5 + 0.5 * bent
    slope = half + 0.5 * value * (1.0 - bent * bent) * (root + 3.0 * 0.044715 * root * square)
    return value * half, slope


def expert_kernel(trained, rows_ref, grads_ref, first, second, out, grad_in, *rest):
    if trained:
        first_grad, second_grad, out_sum, in_sum, hidden, pre_grad = rest
    else:
        out_sum, in_sum, hidden, pre_grad = rest
    step = pl.program_id(0)
    total = rows_ref.shape[0]
    for start in range(0, total, ROWS):
        part = pl.ds(start, ROWS)
        pre = dot(rows_ref[part], first[0])
        active, slope = gelu_parts(pre)
        active = active.astype(BF16)
        hidden[part] = active
        back = (dot_t(grads_ref[part], second[0]) * slope).astype(BF16)
        pre_grad[part] = back
        produced = dot(active, second[0])
        returned = dot_t(back, first[0])

        @pl.when(step == 0)
        def _():
            out_sum[part] = produced
            in_sum[part] = returned

        @pl.when(step > 0)
        def _():
            out_sum[part] += produced
            in_sum[part] += returned

    if trained:
        first_grad[0] = t_dot(rows_ref[...], pre_grad[...]).astype(BF16)
        second_grad[0] = t_dot(hidden[...], grads_ref[...]).astype(BF16)

    @pl.when(step == pl.num_programs(0) - 1)
    def _():
        out[...] = out_sum[...].astype(BF16)
        grad_in[...] = in_sum[...].astype(BF16)


def expert(trained, rows, grads, first, second):
    slices, width, hidden = first.shape
    total = rows.shape[0]
    whole = pl.BlockSpec((total, width), lambda k: (0, 0))
    first_spec = pl.BlockSpec((1, width, hidden), lambda k: (k, 0, 0))
    second_spec = pl.BlockSpec((1, hidden, width), lambda k: (k, 0, 0))
    out_shape = [jax.ShapeDtypeStruct((total, width), BF16)] * 2
    out_specs = [whole, whole]
    if trained:
        out_shape += [jax.ShapeDtypeStruct(first.shape, BF16), jax.ShapeDtypeStruct(second.shape, BF16)]
        out_specs += [first_spec, second_spec]
    return pl.pallas_call(
        functools.partial(expert_kernel, trained),
        grid=(slices,),
        out_shape=out_shape,
        in_specs=[whole, whole, first_spec, second_spec],
        out_specs=out_specs,
        scratch_shapes=[
            pltpu.VMEM((total, width), F32),
            pltpu.VMEM((total, width), F32),
            pltpu.VMEM((total, hidden), BF16),
            pltpu.VMEM((total, hidden), BF16),
        ],
        compiler_params=pltpu.CompilerParams(vmem_limit_bytes=48 * 2**20),
        cost_estimate=pl.CostEstimate(
            flops=slices * total * width * hidden * (12 if trained else 8), bytes_accessed=20 * 2**20, transcendentals=10**6
        ),
        name="trained_expert" if trained else "frozen_expert",
    )(rows, grads, first, second)


def combine_kernel(
    lay, capacity, out_train, out_frozen, grad_train, grad_frozen, middle, second, gates, attended, w_out, gain, w_router, routes, cotangent,
    block_out, middle_grad, attended_grad, out_proj, router, gain_grad, shift_grad,
    got, got_grad, send, recv, local,
):
    n = lay.n
    me = lax.axis_index("sp")
    greet(n)
    started = [[], []]
    for which, (sources, target) in enumerate((((out_train, out_frozen), got), ((grad_train, grad_frozen), got_grad))):
        for kind, source in enumerate(sources):
            place = target.at[pl.ds(pl.multiple_of((me * 2 + kind) * capacity, 16), capacity)]
            near = pltpu.make_async_copy(
                source.at[pl.ds(pl.multiple_of(me * capacity, 16), capacity)], place, local.at[which, kind]
            )
            near.start()
            for step in range(1, n):
                to = lax.rem(me + step, n)
                copy = remote(
                    source.at[pl.ds(pl.multiple_of(to * capacity, 16), capacity)],
                    place,
                    send.at[which, kind, step],
                    recv.at[which, kind, step],
                    to,
                )
                copy.start()
                started[which].append(copy)
            started[which].append(near)
    hot, matches = one_hot_columns(lay, capacity, routes[...])
    upstream = cotangent[...].astype(F32)
    gate = [gates[:, c : c + 1] for c in range(2)]
    for copy in started[0]:
        copy.wait()
    total = middle[...]
    grad_gate = []
    for c in range(2):
        produced = dot(hot[c], got[...])
        total = total + gate[c] * produced
        grad_gate.append(jnp.sum(upstream * produced, axis=1, keepdims=True))
    block_out[...] = total.astype(BF16)
    mean_grad = gate[0] * grad_gate[0] + gate[1] * grad_gate[1]
    grad_logits = sum(matches[c] * (gate[c] * (grad_gate[c] - mean_grad)) for c in range(2))
    high = grad_logits.astype(BF16)
    low = (grad_logits - high.astype(F32)).astype(BF16)
    router[...] = t_dot(second[...], high) + t_dot(second[...], low)
    grad_second = dot_t(high, w_router[...]) + dot_t(low, w_router[...])
    for copy in started[1]:
        copy.wait()
    grad_second = grad_second + dot(hot[0] + hot[1], got_grad[...])
    hat, scale = normed(middle[...])
    gain_grad[...] = jnp.sum(grad_second * hat, axis=0, keepdims=True)
    shift_grad[...] = jnp.sum(grad_second, axis=0, keepdims=True)
    grad = upstream + norm_back(grad_second, gain[...], hat, scale)
    middle_grad[...] = grad
    branch = grad.astype(BF16)
    attended_grad[...] = dot_t(branch, w_out[...]).astype(BF16)
    out_proj[...] = t_dot(attended[...], branch)


def combine(lay, capacity, outs, grads, middle, second, gates, attended, w_out, gain, w_router, routes, cotangent):
    count, width = middle.shape
    n = lay.n
    slots = 2 * n * capacity
    return pl.pallas_call(
        functools.partial(combine_kernel, lay, capacity),
        out_shape=(
            jax.ShapeDtypeStruct((count, width), BF16),
            jax.ShapeDtypeStruct((count, width), F32),
            jax.ShapeDtypeStruct((count, width), BF16),
            jax.ShapeDtypeStruct((width, width), F32),
            jax.ShapeDtypeStruct((width, 128), F32),
            jax.ShapeDtypeStruct((1, width), F32),
            jax.ShapeDtypeStruct((1, width), F32),
        ),
        in_specs=[VMEM] * 13,
        out_specs=[VMEM] * 7,
        scratch_shapes=[
            pltpu.VMEM((slots, width), BF16),
            pltpu.VMEM((slots, width), BF16),
            DMA((2, 2, n)),
            DMA((2, 2, n)),
            DMA((2, 2)),
        ],
        compiler_params=pltpu.CompilerParams(collective_id=2, has_side_effects=True, vmem_limit_bytes=48 * 2**20),
        cost_estimate=pl.CostEstimate(flops=6 * 10**9, bytes_accessed=30 * 2**20, transcendentals=10**4),
        name="combine",
    )(*outs, *grads, middle, second, gates, attended, w_out, gain, w_router, routes, cotangent)


def attend_back_kernel(
    lay, unit, attended, log_total, grad_attended, first_norm, tokens, gain, w_qkv, middle_grad,
    tokens_grad, qkv_grad, gain_grad, shift_grad,
    grad_out, deltas, query_sum, staged, home, send, recv, out_send, home_recv, local,
):
    me = lax.axis_index("sp")
    is_short, seq, first_pair = lay.role(me)
    greet(lay.n)
    started = to_owners(
        lay,
        me,
        lambda pair: pair * WIDE,
        lambda number: number,
        grad_attended,
        lambda start, rows: grad_out.at[pl.ds(pl.multiple_of(start, 16), rows)],
        send,
        recv,
        local,
        range(PAIRS),
    )
    query_sum[...] = jnp.zeros_like(query_sum)
    keep = lanes_first()
    lower = causal(BLOCK)
    wait_unit(lay, is_short, grad_out, recv)

    def make_delta(index, carry):
        part = pl.ds(pl.multiple_of(index * BLOCK, BLOCK), BLOCK)
        first, second = halves(grad_out[part].astype(F32) * attended[part])
        deltas[part] = jnp.where(
            keep, jnp.sum(first, axis=1, keepdims=True), jnp.sum(second, axis=1, keepdims=True)
        )
        return carry

    lax.fori_loop(0, lay.tasks(is_short), make_delta, 0)
    per = jnp.where(is_short, LEN_A // BLOCK, LEN_B // BLOCK)

    def task(index, carry):
        start, block = lay.task(is_short, index)
        base = pl.multiple_of(start + block * BLOCK, BLOCK)
        keys = unit[1, pl.ds(base, BLOCK)]
        values = unit[2, pl.ds(base, BLOCK)]
        key_both = jnp.concatenate(halves(keys), axis=0)

        def visit(place, state, diagonal):
            part = pl.ds(place, BLOCK)
            grad_key, grad_value = state
            queries = halves(unit[0, part])
            outs = halves(grad_out[part])
            weights, grads = [], []
            for which, (query, out) in enumerate(zip(queries, outs)):
                column = which * HEAD_DIM
                scores = dot_t(query, keys)
                if diagonal:
                    scores = jnp.where(lower, scores, NEGATIVE)
                weight = jnp.exp(scores - log_total[part, column : column + 1])
                grad = weight * (dot_t(out, values) - deltas[part, column : column + 1])
                weights.append(weight.astype(BF16))
                grads.append(grad.astype(BF16))
            grad_value = grad_value + t_dot(jnp.concatenate(weights, axis=0), jnp.concatenate(outs, axis=0))
            grad_key = grad_key + t_dot(jnp.concatenate(grads, axis=0), jnp.concatenate(queries, axis=0))
            query_sum[part] += dot(jnp.concatenate(grads, axis=1), key_both)
            return grad_key, grad_value

        zero = jnp.zeros((BLOCK, WIDE), F32)
        state = visit(base, (zero, zero), True)
        grad_key, grad_value = lax.fori_loop(
            block + 1, per, lambda i, state: visit(pl.multiple_of(start + i * BLOCK, BLOCK), state, False), state
        )
        part = pl.ds(base, BLOCK)
        staged[0, part] = (query_sum[part] * HEAD_DIM**-0.5).astype(BF16)
        staged[1, part] = grad_key.astype(BF16)
        staged[2, part] = grad_value.astype(BF16)
        for kind in range(3):
            send_home(
                lay, me, is_short, seq, first_pair, base, block, start, staged.at[kind], home, kind * PAIRS * WIDE,
                out_send.at[kind], home_recv.at[kind], local,
            )
        return carry

    lax.fori_loop(0, lay.tasks(is_short), task, 0)
    for kind in range(3):
        wait_home(lay, is_short, staged.at[kind], home_recv.at[kind], 1, False)
    grad_first = dot_t(home[...], w_qkv[...])
    hat, scale = normed(tokens[...].astype(F32))
    gain_grad[...] = jnp.sum(grad_first * hat, axis=0, keepdims=True)
    shift_grad[...] = jnp.sum(grad_first, axis=0, keepdims=True)
    tokens_grad[...] = middle_grad[...] + norm_back(grad_first, gain[...], hat, scale)
    for chunk in range(0, 3 * PAIRS * WIDE, 2 * WIDE):
        qkv_grad[:, chunk : chunk + 2 * WIDE] = t_dot(first_norm[...], home[:, chunk : chunk + 2 * WIDE])
    finish_sends(me, started)
    for kind in range(3):
        wait_home(lay, is_short, staged.at[kind], out_send.at[kind], 1, True)


def attend_back(lay, unit, attended, log_total, grad_attended, first_norm, tokens, gain, w_qkv, middle_grad):
    count, width = tokens.shape
    owners = len(lay.owners())
    return pl.pallas_call(
        functools.partial(attend_back_kernel, lay),
        out_shape=(
            jax.ShapeDtypeStruct((count, width), F32),
            jax.ShapeDtypeStruct((width, 3 * width), F32),
            jax.ShapeDtypeStruct((1, width), F32),
            jax.ShapeDtypeStruct((1, width), F32),
        ),
        in_specs=[VMEM] * 9,
        out_specs=[VMEM] * 4,
        scratch_shapes=[
            pltpu.VMEM((UNIT, WIDE), BF16),
            pltpu.VMEM((UNIT, WIDE), F32),
            pltpu.VMEM((UNIT, WIDE), F32),
            pltpu.VMEM((3, UNIT, WIDE), BF16),
            pltpu.VMEM((count, 3 * width), BF16),
            DMA((owners,)),
            DMA,
            DMA((3,)),
            DMA((3,)),
            DMA,
        ],
        compiler_params=pltpu.CompilerParams(collective_id=3, has_side_effects=True, vmem_limit_bytes=48 * 2**20),
        cost_estimate=pl.CostEstimate(flops=10 * 10**9, bytes_accessed=30 * 2**20, transcendentals=5 * 10**6),
        name="attend_back",
    )(unit, attended, log_total, grad_attended, first_norm, tokens, gain, w_qkv, middle_grad)


def shards(
    tokens, ln1_gain, ln1_shift, w_qkv, w_out, ln2_gain, ln2_shift, w_router,
    train_w1, train_w2, frozen_w1, frozen_w2, routes, cotangent,
):
    n = lax.axis_size("sp")
    lay = Layout(n)
    tokens, routes, cotangent = tokens[0], routes[0], cotangent[0]
    count = tokens.shape[0]
    capacity = 2 * count // n
    experts = w_router.shape[1]
    row = lambda vector: vector.reshape(1, -1)
    router_wide = jnp.pad(w_router, ((0, 0), (0, 128 - experts)))
    whole = [lax.all_gather(weight[0], "dp") for weight in (train_w1, train_w2, frozen_w1, frozen_w2)]
    first_norm, unit, attended, log_total, attended_low = attend(lay, tokens, row(ln1_gain), row(ln1_shift), w_qkv)
    middle, second, gates, rows, grads = dispatch(
        lay, capacity, tokens, attended_low, w_out, row(ln2_gain), row(ln2_shift), router_wide, routes, cotangent
    )
    out_train, in_train, first_grad, second_grad = expert(True, rows[0], grads[0], whole[0], whole[1])
    out_frozen, in_frozen = expert(False, rows[1], grads[1], whole[2], whole[3])
    first_grad = lax.psum_scatter(first_grad, "dp", scatter_dimension=0).astype(F32)
    second_grad = lax.psum_scatter(second_grad, "dp", scatter_dimension=0).astype(F32)
    block_out, middle_grad, attended_grad, out_proj, router, gain_two, shift_two = combine(
        lay, capacity, (out_train, out_frozen), (in_train, in_frozen), middle, second, gates, attended_low, w_out,
        row(ln2_gain), router_wide, routes, cotangent,
    )
    tokens_grad, qkv_grad, gain_one, shift_one = attend_back(
        lay, unit, attended, log_total, attended_grad, first_norm, tokens, row(ln1_gain), w_qkv, middle_grad
    )
    small = lax.psum((out_proj, router[:, :experts], gain_two, shift_two), ("sp", "dp"))
    last = lax.psum((qkv_grad, gain_one, shift_one), ("sp", "dp"))
    return (
        block_out[None],
        tokens_grad[None],
        last[1][0],
        last[2][0],
        last[0],
        small[0],
        small[2][0],
        small[3][0],
        small[1],
        first_grad[None],
        second_grad[None],
    )


def solution(mesh):
    in_specs = (
        P("dp", "sp", None), P(), P(), P(), P(), P(), P(), P(),
        P("sp", None, "dp"), P("sp", "dp", None), P("sp", None, "dp"), P("sp", "dp", None),
        P("dp", "sp", None), P("dp", "sp", None),
    )
    out_specs = (
        P("dp", "sp", None), P("dp", "sp", None), P(), P(), P(), P(), P(), P(), P(),
        P("sp", None, "dp"), P("sp", "dp", None),
    )
    return jax.shard_map(shards, mesh=mesh, in_specs=in_specs, out_specs=out_specs, check_vma=False)
```

time: 1720 us -> 906 us (0.53)
  waiting for transfers between devices: 848 us -> 515 us
  Pallas kernels: 0 us -> 287 us
  starting transfers between devices: 247 us -> 0.27 us
  local copies, waits for them, and re-layouts: 193 us -> 21.5 us
  other arithmetic: 162 us -> 5.9 us
  matrix products: 122 us -> 0 us
  blocking collectives: 122 us -> 58.2 us
    pallas_call x0 -> x6, Pallas kernels: none -> 287 us  [the longest x1 63 us: dispatch(): pl.pallas_call(functools.partial(dispatch_kernel, lay, capacity), out_sha...]
    ppermute x44 -> x0, starting transfers between devices: 238 us -> none  [the longest x30 147 us: shifted(): return lax.ppermute(value, axis, pairs)]
    ppermute x44 -> x0, waiting for transfers between devices: 158 us -> none  [the longest x30 153 us: shifted(): return lax.ppermute(value, axis, pairs)]
    dot_general x32 -> x0, matrix products: 122 us -> none  [the longest x1 16 us: shards(): jnp.einsum('rf,df->rd', part_frozen, first_frozen, preferred_element_type...]
    reduce_scatter x2, waiting for transfers between devices: 289 us -> 174 us  [the longest x1 88.2 us: shards(): lax.psum_scatter(first_grad, 'dp', scatter_dimension=0).astype(F32)]
    all_to_all x2 -> x0, blocking collectives: 78.7 us -> none  [the longest x1 45.8 us: shards(): lax.all_to_all(pack_routes(second_norm[anchor]), 'sp', split_axis=0, conc...]
    all_gather x4, waiting for transfers between devices: 258 us -> 197 us  [shards(): lax.all_gather(weight[0], 'dp')]
    convert_element_type x34 -> x2, other arithmetic: 65.3 us -> 5.84 us  [the longest x1 3 us: shards(): lax.psum_scatter(second_grad, 'dp', scatter_dimension=0).astype(F32)]
  transfers between devices with their start and end apart: 53 -> 7, of which waited for: 22 -> 6; matrix products, arithmetic and copies ran while one was open for 12% -> 1% of each run, Pallas kernels for 0% -> 17%
where the time goes in v1:
time: 906 us; the launch traced here: 902 us
  waiting for transfers between devices  515 us (57%)
  Pallas kernels  287 us (32%)
  blocking collectives  58.2 us (6%)
  local copies, waits for them, and re-layouts  21.5 us (2%)
  between operations  14.8 us (2%)
    all_gather x4, waiting for transfers between devices, shards(): lax.all_gather(weight[0], 'dp')  197 us
    psum x1, waiting for transfers between devices, shards(): last = lax.psum((qkv_grad, gain_one, shift_one), ('sp', 'dp'))  141 us
    reduce_scatter x1, waiting for transfers between devices, shards(): lax.psum_scatter(first_grad, 'dp', scatter_dimension=0).astype(F32)  88.2 us
    reduce_scatter x1, waiting for transfers between devices, shards(): lax.psum_scatter(second_grad, 'dp', scatter_dimension=0).astype(F32)  85.4 us
    pallas_call x1, Pallas kernels, dispatch(): pl.pallas_call(functools.partial(dispatch_kernel, lay, capacity), out_sha...  63 us
    pallas_call x1, Pallas kernels, combine(): pl.pallas_call(functools.partial(combine_kernel, lay, capacity), out_shap...  62.1 us
    psum x1, blocking collectives, shards(): last = lax.psum((qkv_grad, gain_one, shift_one), ('sp', 'dp'))  58.2 us
    pallas_call x1, Pallas kernels, attend(): pl.pallas_call(functools.partial(attend_kernel, lay), out_shape=(jax.Shap...  57.7 us
  transfers between devices with their start and end apart: 7, of which 6 were waited for; matrix products, arithmetic and copies ran while one was open for 1% of the time, Pallas kernels for 17%

profile of v1, /device:TPU:0, one launch (start us, length us, event | category | flops | bytes accessed | tf_op | source)
XLA Modules:
  0.0 902.2 jit_solution(16689052038696383017)
XLA Ops:
  10.7 57.7 %attend.1 = (bf16[384,768]{1,0:T(8,128)(2,1)S(1)}, bf16[3,3072,128]{2,1,0:T(8,128)(2,1)}, f32[3072,128]{1,0:T(8,128)S(1)}, f32[3072,128]{1,0:T(8,128)S(1)}, bf16[384,768]{1,0:T(8,128)(2,1)S(1)}) custom-call(bf16[384,768]{1,0:T(8,128)(2,1)S(1)} %bitcast.24, f32[1,768]{1,0:T(1,128)S(1)} %reshape.36.gain, f32[1,768]{1,0:T(1,128)S(1)} %reshape.37.shift, ...), custom_call_target="tpu_custom_call" | custom-call | flops 6000000000 | bytes 20971520 | tf_op jit(solution)/shard_map/attend/pallas_call | solution.py:271
  68.4 1.1 copy-done.15
  70.4 63.0 %dispatch.1 = (f32[384,768]{1,0:T(8,128)S(1)}, bf16[384,768]{1,0:T(8,128)(2,1)S(1)}, f32[384,128]{1,0:T(8,128)S(1)}, bf16[2,768,768]{2,1,0:T(8,128)(2,1)}, bf16[2,768,768]{2,1,0:T(8,128)(2,1)}) custom-call(bf16[384,768]{1,0:T(8,128)(2,1)S(1)} %bitcast.25, bf16[384,768]{1,0:T(8,128)(2,1)S(1)} %get-tuple-element.38.attended, bf16[768,768]{1,0:T(8,128)(2,1)S(1)} %copy-done.5, ...), custom_call_target="tpu_custom_call" | custom-call | flops 4000000000 | bytes 20971520 | tf_op jit(solution)/shard_map/dispatch/pallas_call | solution.py:385
  133.4 1.1 copy-done.10
  136.0 3.7 slice_bitcast_fusion
  139.7 51.6 %all-gather.7.cloned.1.call-done.second = bf16[4,768,768]{2,1,0:T(8,128)(2,1)} async-done(((bf16[1,768,768]{2,1,0:T(8,128)(2,1)}), bf16[4,768,768]{2,1,0:T(8,128)(2,1)}) %all-gather.7.cloned.1.call-update) | async-done | bytes 4718608 | tf_op jit(solution)/shard_map/all_gather | solution.py:716
  191.2 1.3 copy-done
  192.5 30.4 %trained_expert.1 = (bf16[768,768]{1,0:T(8,128)(2,1)S(1)}, bf16[768,768]{1,0:T(8,128)(2,1)S(1)}, bf16[4,768,768]{2,1,0:T(8,128)(2,1)}, bf16[4,768,768]{2,1,0:T(8,128)(2,1)}) custom-call(bf16[768,768]{1,0:T(8,128)(2,1)S(1)} %copy-done, bf16[768,768]{1,0:T(8,128)(2,1)S(1)} %get-tuple-element.95.grads_ref, ...), custom_call_target="tpu_custom_call" | custom-call | flops 21743271936 | bytes 20971520 | tf_op jit(solution)/shard_map/trained_expert/pallas_call | solution.py:470
  223.9 1.0 copy-done.12
  225.0 55.7 %all-gather.11.cloned.1.call-done.second = bf16[4,768,768]{2,1,0:T(8,128)(2,1)} async-done(((bf16[1,768,768]{2,1,0:T(8,128)(2,1)}), bf16[4,768,768]{2,1,0:T(8,128)(2,1)}) %all-gather.11.cloned.1.call-update) | async-done | bytes 4718608 | tf_op jit(solution)/shard_map/all_gather | solution.py:716
  280.7 89.3 %all-gather.9.cloned.1.call-done.first = bf16[4,768,768]{2,1,0:T(8,128)(2,1)} async-done(((bf16[1,768,768]{2,1,0:T(8,128)(2,1)}), bf16[4,768,768]{2,1,0:T(8,128)(2,1)}) %all-gather.9.cloned.1.call-update) | async-done | bytes 4718608 | tf_op jit(solution)/shard_map/all_gather | solution.py:716
  370.1 20.8 %frozen_expert.1 = (bf16[768,768]{1,0:T(8,128)(2,1)S(1)}, bf16[768,768]{1,0:T(8,128)(2,1)S(1)}) custom-call(bf16[768,768]{1,0:T(8,128)(2,1)S(1)} %get-tuple-element.99.rows_ref, bf16[768,768]{1,0:T(8,128)(2,1)S(1)} %get-tuple-element.94.grads_ref, bf16[4,768,768]{2,1,0:T(8,128)(2,1)} %all-gather.9.cloned.1.call-done.first, ...), custom_call_target="tpu_custom_call" | custom-call | flops 14495514624 | bytes 20971520 | tf_op jit(solution)/shard_map/frozen_expert/pallas_call | solution.py:470
  391.8 1.0 copy-done.14
  392.9 62.1 %combine.1 = (bf16[384,768]{1,0:T(8,128)(2,1)S(1)}, f32[384,768]{1,0:T(8,128)S(1)}, bf16[384,768]{1,0:T(8,128)(2,1)S(1)}, f32[768,768]{1,0:T(8,128)}, f32[768,12...) custom-call(bf16[768,768]{1,0:T(8,128)(2,1)} %copy-done.11, bf16[768,768]{1,0:T(8,128)(2,1)} %copy-done.13, ...), custom_call_target="tpu_custom_call" | custom-call | flops 6000000000 | bytes 31457280 | tf_op jit(solution)/shard_map/combine/pallas_call | solution.py:553
  455.1 52.8 %attend_back.1 = (f32[384,768]{1,0:T(8,128)S(1)}, f32[768,2304]{1,0:T(8,128)}, f32[1,768]{1,0:T(1,128)S(1)}, f32[1,768]{1,0:T(1,128)S(1)}) custom-call(bf16[3,3072,128]{2,1,0:T(8,128)(2,1)} %get-tuple-element.49.unit, f32[3072,128]{1,0:T(8,128)S(1)} %copy-done.16, f32[3072,128]{1,0:T(8,128)} %copy-done.17, ...), custom_call_target="tpu_custom_call" | custom-call | flops 10000000000 | bytes 31457280 | tf_op jit(solution)/shard_map/attend_back/pallas_call | solution.py:676
  509.3 58.2 %all-reduce.1 = (f32[768]{0:T(1024)}, f32[768]{0:T(1024)}, f32[768]{0:T(1024)}, f32[768]{0:T(1024)}, f32[768,16]{1,0:T(8,128)S(1)}) all-reduce(f32[768]{0:T(1024)S(1)} %reduce, f32[768]{0:T(1024)S(1)} %reduce.1, f32[768]{0:T(1024)S(1)} %reduce.2, f32[768]{0:T(1024)S(1)} %reduce.3, ...), channel_id=1, replica_groups=mesh['sp'=8,'dp'=4] {'sp','dp'}, use_global_device_ids=true, to_apply=%region_0.1 | all-reduce | flops 15360 | bytes 122880 | tf_op jit(solution)/shard_map/psum | solution.py:733
  568.2 140.9 %all-reduce.5.cloned.1.call-done = (f32[768,2304]{1,0:T(8,128)}, f32[768,768]{1,0:T(8,128)}) async-done(((f32[768,2304]{1,0:T(8,128)}, f32[768,768]{1,0:T(8,128)}), (f32[768,2304]{1,0:T(8,128)}, f32[768,768]{1,0:T(8,128)})) %all-reduce.5.cloned.1.call-update) | async-done | bytes 9437200 | tf_op jit(solution)/shard_map/psum | solution.py:733
  709.1 88.2 %reduce-scatter.3.cloned.1.call-done = bf16[1,768,768]{2,1,0:T(8,128)(2,1)} async-done(((bf16[4,768,768]{2,1,0:T(8,128)(2,1)}), bf16[1,768,768]{2,1,0:T(8,128)(2,1)}) %reduce-scatter.3.cloned.1.call-update) | async-done | bytes 1179664 | tf_op jit(solution)/shard_map/reduce_scatter | solution.py:723
  797.3 2.8 convert_element_type.10
  800.1 85.4 %reduce-scatter.5.cloned.1.call-done = bf16[1,768,768]{2,1,0:T(8,128)(2,1)} async-done(((bf16[4,768,768]{2,1,0:T(8,128)(2,1)}), bf16[1,768,768]{2,1,0:T(8,128)(2,1)}) %reduce-scatter.5.cloned.1.call-update) | async-done | bytes 1179664 | tf_op jit(solution)/shard_map/reduce_scatter | solution.py:724
  885.5 3.0 convert_element_type.11
  889.3 1.0 copy.40
  890.3 3.2 copy.41
  893.7 1.4 copy.42
  (92 shorter events, 10.8 us)
Async XLA Ops:
  7.2 132.5 %all-gather.5.cloned.1.call-start = ((), (), s32[]{:S(2)}) async-start(), calls=%async_computation.2 | async-start | bytes 5898240 | tf_op jit(solution)/shard_map/all_gather | solution.py:716
  7.9 183.3 %all-gather.7.cloned.1.call-start = ((), (), s32[]{:S(2)}) async-start(), calls=%async_computation.3 | async-start | bytes 5898240 | tf_op jit(solution)/shard_map/all_gather | solution.py:716
  8.7 272.0 %all-gather.11.cloned.1.call-start = ((), (), s32[]{:S(2)}) async-start(), calls=%async_computation.5 | async-start | bytes 5898240 | tf_op jit(solution)/shard_map/all_gather | solution.py:716
  9.5 360.6 %all-gather.9.cloned.1.call-start = ((), (), s32[]{:S(2)}) async-start(), calls=%async_computation.4 | async-start | bytes 5898240 | tf_op jit(solution)/shard_map/all_gather | solution.py:716
  10.0 699.1 %all-reduce.5.cloned.1.call-start = ((), (), s32[]{:S(2)}) async-start(), calls=%async_computation.8 | async-start | bytes 18874368 | tf_op jit(solution)/shard_map/psum | solution.py:733
  10.3 60.1 %copy-start.1 = (s32[1,384,2]{2,1,0:T(8,128)}, s32[1,384,2]{2,1,0:T(8,128)S(1)}, u32[]{:S(2)}) copy-start(s32[1,384,2]{2,1,0:T(8,128)S(1)} %copy.30) | copy-start | bytes 9220
  10.7 59.7 %copy-start.3 = (bf16[768,128]{1,0:T(8,128)(2,1)}, bf16[768,128]{1,0:T(8,128)(2,1)S(1)}, u32[]{:S(2)}) copy-start(bf16[768,128]{1,0:T(8,128)(2,1)S(1)} %pad.4.w_router) | copy-start | bytes 589828
  10.7 59.7 %copy-start.5 = (bf16[768,768]{1,0:T(8,128)(2,1)S(1)}, bf16[768,768]{1,0:T(8,128)(2,1)}, u32[]{:S(2)}) copy-start(bf16[768,768]{1,0:T(8,128)(2,1)} %w_out.3) | copy-start | bytes 3538948
  10.7 59.7 %copy-start.6 = (bf16[1,384,768]{2,1,0:T(8,128)(2,1)S(1)}, bf16[1,384,768]{2,1,0:T(8,128)(2,1)}, u32[]{:S(2)}) copy-start(bf16[1,384,768]{2,1,0:T(8,128)(2,1)} %param.27) | copy-start | bytes 1769476
  70.4 63.0 %copy-start.17 = (f32[3072,128]{1,0:T(8,128)}, f32[3072,128]{1,0:T(8,128)S(1)}, u32[]{:S(2)}) copy-start(f32[3072,128]{1,0:T(8,128)S(1)} %get-tuple-element.51.log_total) | copy-start | bytes 4718596
  70.4 63.0 %copy-start.18 = (bf16[384,768]{1,0:T(8,128)(2,1)}, bf16[384,768]{1,0:T(8,128)(2,1)S(1)}, u32[]{:S(2)}) copy-start(bf16[384,768]{1,0:T(8,128)(2,1)S(1)} %get-tuple-element.38.attended) | copy-start | bytes 1769476
  370.0 22.8 %copy-start.2 = (s32[1,384,2]{2,1,0:T(8,128)S(1)}, s32[1,384,2]{2,1,0:T(8,128)}, u32[]{:S(2)}) copy-start(s32[1,384,2]{2,1,0:T(8,128)} %copy-done.1) | copy-start | bytes 9220
  370.0 22.8 %copy-start.4 = (bf16[768,128]{1,0:T(8,128)(2,1)S(1)}, bf16[768,128]{1,0:T(8,128)(2,1)}, u32[]{:S(2)}) copy-start(bf16[768,128]{1,0:T(8,128)(2,1)} %copy-done.3) | copy-start | bytes 589828
  370.0 22.8 %copy-start.7 = (bf16[1,384,768]{2,1,0:T(8,128)(2,1)S(1)}, bf16[1,384,768]{2,1,0:T(8,128)(2,1)}, u32[]{:S(2)}) copy-start(bf16[1,384,768]{2,1,0:T(8,128)(2,1)} %param.27) | copy-start | bytes 1769476
  370.0 22.8 %copy-start.19 = (bf16[384,768]{1,0:T(8,128)(2,1)S(1)}, bf16[384,768]{1,0:T(8,128)(2,1)}, u32[]{:S(2)}) copy-start(bf16[384,768]{1,0:T(8,128)(2,1)} %copy-done.18) | copy-start | bytes 1769476
  370.0 22.8 %copy-start.21 = (bf16[384,768]{1,0:T(8,128)(2,1)S(1)}, bf16[384,768]{1,0:T(8,128)(2,1)}, u32[]{:S(2)}) copy-start(bf16[384,768]{1,0:T(8,128)(2,1)} %copy-done.20) | copy-start | bytes 1769476
  370.0 22.8 %copy-start.25 = (f32[384,128]{1,0:T(8,128)S(1)}, f32[384,128]{1,0:T(8,128)}, u32[]{:S(2)}) copy-start(f32[384,128]{1,0:T(8,128)} %copy-done.24) | copy-start | bytes 589828
  392.9 62.1 %copy-start.9 = (bf16[1,384,768]{2,1,0:T(8,128)(2,1)S(1)}, bf16[1,384,768]{2,1,0:T(8,128)(2,1)}, u32[]{:S(2)}) copy-start(bf16[1,384,768]{2,1,0:T(8,128)(2,1)} %param.14) | copy-start | bytes 1769476
  392.9 62.1 %copy-start.16 = (f32[3072,128]{1,0:T(8,128)S(1)}, f32[3072,128]{1,0:T(8,128)}, u32[]{:S(2)}) copy-start(f32[3072,128]{1,0:T(8,128)} %copy-done.15) | copy-start | bytes 4718596
  392.9 62.1 %copy-start.23 = (bf16[384,768]{1,0:T(8,128)(2,1)S(1)}, bf16[384,768]{1,0:T(8,128)(2,1)}, u32[]{:S(2)}) copy-start(bf16[384,768]{1,0:T(8,128)(2,1)} %copy-done.22) | copy-start | bytes 1769476
  507.9 289.4 %reduce-scatter.3.cloned.1.call-start = ((), (), s32[]{:S(2)}) async-start(), calls=%async_computation.6 | async-start | bytes 5898240 | tf_op jit(solution)/shard_map/reduce_scatter | solution.py:723
  508.4 377.1 %reduce-scatter.5.cloned.1.call-start = ((), (), s32[]{:S(2)}) async-start(), calls=%async_computation.7 | async-start | bytes 5898240 | tf_op jit(solution)/shard_map/reduce_scatter | solution.py:724
  885.5 4.8 copy-start.26
  890.3 3.4 copy-start.27
  (17 other events, 19.3 us)
Sparse Core Ops, SparseCore 0:
  9.6 92.0 all-gather.4
  103.3 87.8 all-gather.6
  192.8 87.8 all-gather.10
  282.1 87.8 all-gather.8
  508.0 201.0 all-reduce.4
  712.0 85.2 reduce-scatter.2
  799.7 85.7 reduce-scatter.4

commit v2 on v1

v2 whole, which is shorter than its diff:
```python
import functools

import jax
import jax.numpy as jnp
from jax import lax
from jax.experimental import pallas as pl
from jax.experimental.pallas import tpu as pltpu
from jax.sharding import PartitionSpec as P

HEADS = 12
HEAD_DIM = 64
LEN_A = 1024
LEN_B = 2048
PAIRS = HEADS // 2
WIDE = 2 * HEAD_DIM
UNIT = 3 * LEN_A
BLOCK = 256
EPSILON = 1e-05
NEGATIVE = -1e30
MESH = pl.DeviceIdType.MESH
DMA = pltpu.SemaphoreType.DMA
F32 = jnp.float32
BF16 = jnp.bfloat16
VMEM = pl.BlockSpec(memory_space=pltpu.VMEM)


def dot(a, b):
    return jnp.dot(a, b, preferred_element_type=F32)


def dot_t(a, b):
    return lax.dot_general(a, b, (((1,), (1,)), ((), ())), preferred_element_type=F32)


def t_dot(a, b):
    return lax.dot_general(a, b, (((0,), (0,)), ((), ())), preferred_element_type=F32)


def normed(value):
    centre = jnp.mean(value, axis=-1, keepdims=True)
    centred = value - centre
    spread = jnp.mean(centred * centred, axis=-1, keepdims=True)
    scale = lax.rsqrt(spread + EPSILON)
    return centred * scale, scale


def norm_back(grad, gain, hat, scale):
    scaled = grad * gain
    first = jnp.mean(scaled, axis=-1, keepdims=True)
    second = jnp.mean(scaled * hat, axis=-1, keepdims=True)
    return (scaled - first - hat * second) * scale


class Layout:
    def __init__(self, n_sp):
        self.n = n_sp
        self.sequences = n_sp // 8
        self.short = LEN_A // n_sp
        self.long = LEN_B // n_sp
        self.split = self.sequences * self.short

    def owners(self):
        found = []
        for seq in range(self.sequences):
            for pair in range(PAIRS):
                number = seq * PAIRS + pair
                found.append((number + number // 3 + 1, True, self.split + seq * self.long, self.long, pair, 0))
                found.append((4 * (seq * 2 + pair // 3), False, seq * self.short, self.short, pair, (pair % 3) * LEN_A))
        return found

    def role(self, me):
        is_short = lax.rem(me, 4) == 0
        number = me - me // 4 - 1
        group = me // 4
        seq = jnp.where(is_short, group // 2, number // PAIRS)
        pair = jnp.where(is_short, 3 * lax.rem(group, 2), lax.rem(number, PAIRS))
        return is_short, seq, pair

    def task(self, is_short, index):
        per = LEN_A // BLOCK
        start = jnp.where(is_short, (index // per) * LEN_A, 0)
        block = jnp.where(is_short, lax.rem(index, per), index)
        return pl.multiple_of(start, BLOCK), block

    def tasks(self, is_short):
        return jnp.where(is_short, 3 * LEN_A // BLOCK, LEN_B // BLOCK)


def meet(peers):
    barrier = pltpu.get_barrier_semaphore()
    for wanted, device in peers:

        @pl.when(wanted)
        def _():
            pl.semaphore_signal(barrier, inc=1, device_id=device, device_id_type=MESH)

    pl.semaphore_wait(barrier, sum(jnp.asarray(wanted, jnp.int32) for wanted, _ in peers))


def plane_peers(n):
    me = lax.axis_index("sp")
    return [(True, {"sp": lax.rem(me + step, n)}) for step in range(1, n)]


def remote(source, target, send_sem, recv_sem, device):
    device = device if isinstance(device, dict) else {"sp": device}
    return pltpu.make_async_remote_copy(
        src_ref=source, dst_ref=target, send_sem=send_sem, recv_sem=recv_sem, device_id=device, device_id_type=MESH
    )


def lanes_first():
    return lax.broadcasted_iota(jnp.int32, (1, WIDE), 1) < HEAD_DIM


def halves(value):
    keep = lanes_first()
    zero = jnp.zeros_like(value)
    return jnp.where(keep, value, zero), jnp.where(keep, zero, value)


def causal(rows):
    return lax.broadcasted_iota(jnp.int32, (rows, rows), 0) >= lax.broadcasted_iota(jnp.int32, (rows, rows), 1)


def to_owners(lay, me, cols, slot, source, target, send_sems, recv_sem, local_sem, wanted):
    started = []
    for number, (owner, is_long, start, rows, pair, unit) in enumerate(lay.owners()):
        if pair not in wanted:
            continue
        piece = source.at[pl.ds(start, rows), pl.ds(cols(pair), WIDE)]
        place = target(unit + me * rows, rows)
        far = remote(piece, place, send_sems.at[slot(number)], recv_sem, owner)
        near = pltpu.make_async_copy(piece, place, local_sem)

        @pl.when(me != owner)
        def _():
            far.start()

        @pl.when(me == owner)
        def _():
            near.start()
            near.wait()

        started.append((owner, far))
    return started


def finish_sends(me, started):
    for owner, copy in started:

        @pl.when(me != owner)
        def _():
            copy.wait_send()


def wait_unit(lay, is_short, buffer, sem):
    for short, rows in ((True, 3 * (lay.n - 1) * lay.short), (False, (lay.n - 1) * lay.long)):

        @pl.when(is_short == short)
        def _():
            piece = buffer.at[pl.ds(0, rows)]
            pltpu.make_async_copy(piece, piece, sem).wait()


def send_home(lay, me, is_short, seq, first_pair, base, block, unit_start, source, target, base_col, send_sem, recv_sem, local_sem):
    for short, rows in ((True, lay.short), (False, lay.long)):

        @pl.when(is_short == short)
        def _():
            pair = first_pair + (unit_start // LEN_A if short else 0)
            column = pl.multiple_of(base_col + pair * WIDE, WIDE)
            first = pl.multiple_of(seq * rows + (0 if short else lay.split), 16)
            for part in range(BLOCK // rows):
                home = block * (BLOCK // rows) + part
                piece = source.at[pl.ds(pl.multiple_of(base + part * rows, 16), rows)]
                place = target.at[pl.ds(first, rows), pl.ds(column, WIDE)]

                @pl.when(home != me)
                def _():
                    remote(piece, place, send_sem, recv_sem, home).start()

                @pl.when(home == me)
                def _():
                    near = pltpu.make_async_copy(piece, place, local_sem)
                    near.start()
                    near.wait()


def wait_home(lay, is_short, scratch, sem, tensors, sent):
    for short in (True, False):
        own = 3 * lay.short if short else lay.long
        if sent:
            rows = (3 * LEN_A if short else LEN_B) - own
        else:
            rows = PAIRS * lay.sequences * (lay.short + lay.long) - own

        @pl.when(is_short == short)
        def _():
            for _ in range(tensors):
                piece = scratch.at[pl.ds(0, rows)]
                pltpu.make_async_copy(piece, piece, sem).wait()


class Planes:
    def __init__(self, n_dp):
        self.n = n_dp
        self.me = lax.axis_index("dp")
        self.outer = jnp.logical_or(self.me == 0, self.me == n_dp - 1)
        self.inner = jnp.logical_not(self.outer)
        self.inward = jnp.where(self.me == 0, 1, n_dp - 2)
        self.hosts = jnp.logical_or(self.me == 1, self.me == n_dp - 2)
        self.guest = jnp.where(self.me == 1, 0, n_dp - 1)

    def peers(self, n_sp):
        me = lax.axis_index("sp")
        found = plane_peers(n_sp)
        for sp in range(n_sp):
            found.append((self.outer, {"sp": sp, "dp": self.inward}))
            found.append((self.hosts, {"sp": sp, "dp": self.guest}))
        far = jnp.logical_and(self.inner, self.me + 1 < self.n - 1)
        found.append((far, {"sp": me, "dp": self.me + 1}))
        far = jnp.logical_and(self.inner, self.me - 1 > 0)
        found.append((far, {"sp": me, "dp": self.me - 1}))
        return found

    def takes(self, trained, up):
        other = self.me + 1 if up else self.me - 1
        low, high = (1, self.n - 2) if trained else (0, self.n - 1)
        return jnp.logical_and(other >= low, other <= high)


class Weights:
    def __init__(self, planes, own, every, send, recv, local):
        self.planes, self.own, self.every = planes, own, every
        self.send, self.recv, self.local = send, recv, local

    def copy(self, array, index, up, source):
        other = self.planes.me + 1 if up else self.planes.me - 1
        return remote(
            source, self.every[array].at[index], self.send.at[int(up), array, index], self.recv.at[array, index],
            {"dp": other},
        )

    def begin(self):
        me = self.planes.me
        for array in range(4):
            for up in (True, False):

                @pl.when(self.planes.takes(array < 2, up))
                def _():
                    self.copy(array, me, up, self.own[array]).start()

            pltpu.make_async_copy(self.own[array], self.every[array].at[me], self.local.at[array]).start()

    def own_wait(self):
        for array in range(4):
            pltpu.make_async_copy(self.own[array], self.every[array].at[self.planes.me], self.local.at[array]).wait()

    def pairs(self, array, distance):
        me, n = self.planes.me, self.planes.n
        used = self.planes.inner if array < 2 else True
        for up in (True, False):
            index = me - distance if up else me + distance
            comes = jnp.logical_and(used, jnp.logical_and(index >= 0, index < n))
            yield comes, jnp.logical_and(comes, self.planes.takes(array < 2, up)), jnp.clip(index, 0, n - 1), up

    def pass_on(self, arrays, distance):
        for array in arrays:
            for comes, goes, index, up in self.pairs(array, distance):

                @pl.when(comes)
                def _():
                    place = self.every[array].at[index]
                    pltpu.make_async_copy(place, place, self.recv.at[array, index]).wait()

                @pl.when(goes)
                def _():
                    self.copy(array, index, up, self.every[array].at[index]).start()

    def finish(self):
        for array in range(4):
            for distance in range(self.planes.n):
                for _, goes, index, up in self.pairs(array, distance):
                    goes = goes if distance else self.planes.takes(array < 2, up)

                    @pl.when(goes)
                    def _():
                        self.copy(array, index, up, self.every[array].at[index]).wait_send()


ROWS = 256


def gelu_parts(value):
    root = 0.7978845608028654
    square = value * value
    bent = jnp.tanh(root * value * (1.0 + 0.044715 * square))
    half = 0.5 + 0.5 * bent
    slope = half + 0.5 * value * (1.0 - bent * bent) * (root + 3.0 * 0.044715 * root * square)
    return value * half, slope


def slot_rows(lay, capacity, routes_t):
    n = lay.n
    experts, count = 2 * n, routes_t.shape[1]
    index = lax.broadcasted_iota(jnp.int32, (experts, count), 0)
    matches = [(index == routes_t[c : c + 1]).astype(F32) for c in range(2)]
    earlier = (
        lax.broadcasted_iota(jnp.int32, (count, count), 0) < lax.broadcasted_iota(jnp.int32, (count, count), 1)
    ).astype(F32)
    rank = dot((matches[0] + matches[1]).astype(BF16), earlier.astype(BF16))
    place = rank + (((index % n) * 2 + index // n) * capacity).astype(F32)
    return [jnp.sum(m * place, axis=0, keepdims=True).astype(jnp.int32) for m in matches]


def slot_columns(lay, capacity, routes):
    n = lay.n
    count = routes.shape[0]
    index = lax.broadcasted_iota(jnp.int32, (count, 128), 1)
    matches = [(index == routes[:, c : c + 1]).astype(F32) for c in range(2)]
    earlier = (
        lax.broadcasted_iota(jnp.int32, (count, count), 0) > lax.broadcasted_iota(jnp.int32, (count, count), 1)
    ).astype(F32)
    rank = dot(earlier.astype(BF16), (matches[0] + matches[1]).astype(BF16))
    place = rank + (((index % n) * 2 + index // n) * capacity).astype(F32)
    return [jnp.sum(m * place, axis=1, keepdims=True).astype(jnp.int32) for m in matches], matches


def hot(condition):
    return condition.astype(F32).astype(BF16)


def layer_kernel(
    lay, capacity, n_dp,
    tokens, gain_one, shift_one, w_qkv, w_out, gain_two, shift_two, w_router, routes, routes_t, cotangent, own_a, own_b, own_c, own_d,
    first_norm, unit, attended, log_total, home, middle, second_norm, gates_out, got, got_grad, first_grad, second_grad,
    all_a, all_b, all_c, all_d,
    staged, staged_out, packed, packed_grad, rows_in, rows_grad, weight_a, weight_b, out_sum, in_sum, grad_a, grad_b,
    send, recv, out_send, home_recv, local, stream_send, stream_recv, stream_local, load,
    row_send, row_recv, row_local, back_send, back_recv, back_local,
):
    n = lay.n
    me = lax.axis_index("sp")
    planes = Planes(n_dp)
    is_short, seq, first_pair = lay.role(me)
    meet(planes.peers(n))
    stream = Weights(
        planes, (own_a, own_b, own_c, own_d), (all_a, all_b, all_c, all_d), stream_send, stream_recv, stream_local
    )
    stream.begin()

    hat, _ = normed(tokens[...].astype(F32))
    first_norm[...] = (hat * gain_one[...] + shift_one[...]).astype(BF16)
    started = []
    for chunk in range(9):
        kind, third = divmod(chunk, 3)
        made = dot(first_norm[...], w_qkv[:, chunk * 2 * WIDE : (chunk + 1) * 2 * WIDE]).astype(BF16)
        staged[chunk] = made * BF16(HEAD_DIM**-0.5) if kind == 0 else made
        count = len(lay.owners())
        started += to_owners(
            lay,
            me,
            lambda pair: (pair % 2) * WIDE,
            lambda number: chunk * count + number,
            staged.at[chunk],
            lambda start, rows: unit.at[kind, pl.ds(pl.multiple_of(start, 16), rows)],
            send,
            recv.at[kind],
            local,
            (2 * third, 2 * third + 1),
        )
    for kind in range(3):
        wait_unit(lay, is_short, unit.at[kind], recv.at[kind])
    keep = lanes_first()
    lower = causal(BLOCK)

    def task(index, carry):
        start, block = lay.task(is_short, index)
        base = pl.multiple_of(start + block * BLOCK, BLOCK)
        queries = halves(unit[0, pl.ds(base, BLOCK)])

        def visit(place, state, diagonal):
            keys = unit[1, pl.ds(place, BLOCK)]
            values = unit[2, pl.ds(place, BLOCK)]
            result = []
            for (peak, total, summed), query in zip(state, queries):
                scores = dot_t(query, keys)
                if diagonal:
                    scores = jnp.where(lower, scores, NEGATIVE)
                new_peak = jnp.maximum(peak, jnp.max(scores, axis=1, keepdims=True))
                factor = jnp.exp(peak - new_peak)
                weight = jnp.exp(scores - new_peak)
                total = total * factor + jnp.sum(weight, axis=1, keepdims=True)
                summed = summed * factor + dot(weight.astype(BF16), values)
                result.append((new_peak, total, summed))
            return tuple(result)

        empty = (jnp.full((BLOCK, 1), NEGATIVE, F32), jnp.zeros((BLOCK, 1), F32), jnp.zeros((BLOCK, WIDE), F32))
        state = lax.fori_loop(
            0, block, lambda j, state: visit(pl.multiple_of(start + j * BLOCK, BLOCK), state, False), (empty, empty)
        )
        (peak_a, total_a, summed_a), (peak_b, total_b, summed_b) = visit(base, state, True)
        result = jnp.where(keep, summed_a / total_a, summed_b / total_b)
        attended[pl.ds(base, BLOCK)] = result
        staged_out[pl.ds(base, BLOCK)] = result.astype(BF16)
        log_total[pl.ds(base, BLOCK)] = jnp.where(keep, peak_a + jnp.log(total_a), peak_b + jnp.log(total_b))
        send_home(
            lay, me, is_short, seq, first_pair, base, block, start, staged_out, home, 0, out_send, home_recv, local
        )
        return carry

    lax.fori_loop(0, lay.tasks(is_short), task, 0)
    finish_sends(me, started)
    wait_home(lay, is_short, staged_out, out_send, 1, True)
    wait_home(lay, is_short, staged_out, home_recv, 1, False)

    span = n * capacity
    width, hidden = grad_a.shape
    x1 = tokens[...].astype(F32) + dot(home[...], w_out[...])
    middle[...] = x1
    hat, _ = normed(x1)
    second = (hat * gain_two[...] + shift_two[...]).astype(BF16)
    second_norm[...] = second
    place = slot_rows(lay, capacity, routes_t[...])
    count = tokens.shape[0]

    def dispatch_copies(source, target, which, kind):
        plane = jnp.where(planes.outer, planes.inward, planes.me) if kind == 0 else planes.me
        area = jnp.where(planes.outer, 1, 0) if kind == 0 else 2
        base = pl.multiple_of(area * span + me * capacity, 16)
        into = target.at[pl.ds(base, capacity)]
        for step in range(n):
            to = lax.rem(me + step, n)
            piece = source.at[pl.ds(pl.multiple_of((to * 2 + kind) * capacity, 16), capacity)]
            far = remote(
                piece, into, row_send.at[which, kind, step], row_recv.at[which, area, me], {"sp": to, "dp": plane}
            )
            if step:
                yield True, far
                continue
            if kind == 0:
                yield planes.outer, far
            stays = planes.inner if kind == 0 else True
            yield stays, pltpu.make_async_copy(piece, into, row_local.at[which, kind])

    def each(copies, act):
        for condition, copy in copies:
            if condition is True:
                act(copy)
            else:

                @pl.when(condition)
                def _():
                    act(copy)

    def dispatch(source, target, which):
        for kind in range(2):
            each(dispatch_copies(source, target, which, kind), lambda copy: copy.start())

    for start in range(0, 2 * span, ROWS):
        slots = start + lax.broadcasted_iota(jnp.int32, (ROWS, count), 0)
        packed[start : start + ROWS] = dot(hot(jnp.logical_or(slots == place[0], slots == place[1])), second).astype(BF16)
    dispatch(packed, rows_in, 0)
    logits = dot(second, w_router[...])
    index = lax.broadcasted_iota(jnp.int32, logits.shape, 1)
    chosen = [jnp.sum(jnp.where(index == routes[:, c : c + 1], logits, 0.0), axis=1, keepdims=True) for c in range(2)]
    top = jnp.maximum(chosen[0], chosen[1])
    exped = [jnp.exp(value - top) for value in chosen]
    gates = [value / (exped[0] + exped[1]) for value in exped]
    upstream = cotangent[...].astype(F32)
    lane = lax.broadcasted_iota(jnp.int32, gates_out.shape, 1)
    gates_out[...] = jnp.where(lane == 0, gates[0], gates[1])
    route_grads = [(gate * upstream).astype(BF16) for gate in gates]
    for start in range(0, 2 * span, ROWS):
        slots = start + lax.broadcasted_iota(jnp.int32, (ROWS, count), 0)
        packed_grad[start : start + ROWS] = sum(dot(hot(slots == place[c]), route_grads[c]) for c in range(2)).astype(BF16)
    dispatch(packed_grad, rows_grad, 1)
    stream.own_wait()
    stream.pass_on(range(4), 1)

    def arrived(which, area, host):
        buffer = (rows_in, rows_grad)[which]
        for src in range(n):
            piece = buffer.at[pl.ds(area * span + src * capacity, capacity)]
            wait = pltpu.make_async_copy(piece, piece, row_recv.at[which, area, src]).wait
            if host:
                wait()
            else:
                pl.when(src != me)(wait)

    for which, (source, target) in enumerate(((packed, rows_in), (packed_grad, rows_grad))):
        for kind in range(2):
            each(
                dispatch_copies(source, target, which, kind),
                lambda copy: copy.wait_send() if hasattr(copy, "wait_send") and copy.is_remote else copy.wait(),
            )

    def work(trained, first_row, rows):
        def clear(index, carry):
            part = pl.ds(pl.multiple_of(index * ROWS, ROWS), ROWS)
            out_sum[part] = jnp.zeros((ROWS, out_sum.shape[1]), F32)
            in_sum[part] = jnp.zeros((ROWS, in_sum.shape[1]), F32)
            return carry

        lax.fori_loop(0, rows // ROWS, clear, 0)
        arrays = (0, 1) if trained else (2, 3)
        every = (all_a, all_b) if trained else (all_c, all_d)

        def one(step, carry):
            distance, side = step // 2, lax.rem(step, 2)
            index = jnp.where(side == 0, planes.me - distance, planes.me + distance)
            real = jnp.logical_and(jnp.logical_and(index >= 0, index < n_dp), jnp.logical_or(side == 0, distance > 0))

            @pl.when(jnp.logical_and(side == 0, distance >= 2))
            def _():
                stream.pass_on(arrays, distance)

            @pl.when(real)
            def _():
                loads = [
                    pltpu.make_async_copy(every[i].at[index], (weight_a, weight_b)[i], load.at[i]) for i in range(2)
                ]
                for copy in loads:
                    copy.start()
                for copy in loads:
                    copy.wait()

                def chunk(number, carry):
                    part = pl.ds(pl.multiple_of(number * ROWS, ROWS), ROWS)
                    here = pl.ds(pl.multiple_of(first_row + number * ROWS, ROWS), ROWS)
                    active, slope = gelu_parts(dot(rows_in[here], weight_a[...]))
                    active = active.astype(BF16)
                    back = (dot_t(rows_grad[here], weight_b[...]) * slope).astype(BF16)
                    if trained:
                        packed[part, :hidden] = active
                        packed_grad[part, :hidden] = back
                    out_sum[part] += dot(active, weight_b[...])
                    in_sum[part] += dot_t(back, weight_a[...])
                    return carry

                lax.fori_loop(0, rows // ROWS, chunk, 0)
                if trained:
                    stores = [
                        pltpu.make_async_copy(stage, whole.at[index], load.at[2 + i])
                        for i, (stage, whole) in enumerate(((grad_a, first_grad), (grad_b, second_grad)))
                    ]
                    for total in (span, 2 * span):

                        @pl.when(planes.hosts == (total > span))
                        def _():
                            every_row = pl.ds(0, total)
                            for col in range(0, width, WIDE):
                                cut = pl.ds(col, WIDE)
                                grad_a[cut] = t_dot(rows_in[every_row, cut], packed_grad[every_row, :hidden]).astype(BF16)
                            for col in range(0, hidden, WIDE):
                                cut = pl.ds(col, WIDE)
                                grad_b[cut] = t_dot(packed[every_row, cut], rows_grad[every_row]).astype(BF16)

                    for copy in stores:
                        copy.start()
                    for copy in stores:
                        copy.wait()

            return carry

        lax.fori_loop(0, 2 * n_dp, one, 0)

        def turn(number, carry):
            part = pl.ds(pl.multiple_of(number * ROWS, ROWS), ROWS)
            here = pl.ds(pl.multiple_of(first_row + number * ROWS, ROWS), ROWS)
            rows_in[here] = out_sum[part].astype(BF16)
            rows_grad[here] = in_sum[part].astype(BF16)
            return carry

        lax.fori_loop(0, rows // ROWS, turn, 0)

    def back_copies(kind, guest):
        area = 2 if kind else int(guest)
        plane = planes.guest if guest else planes.me
        for which, (source, target) in enumerate(((rows_in, got), (rows_grad, got_grad))):
            into = target.at[pl.ds(pl.multiple_of((me * 2 + kind) * capacity, 16), capacity)]
            for step in range(n):
                to = lax.rem(me + step, n)
                piece = source.at[pl.ds(pl.multiple_of(area * span + to * capacity, 16), capacity)]
                if step or guest:
                    yield True, remote(
                        piece, into, back_send.at[which, area, step], back_recv.at[which, kind, me], {"sp": to, "dp": plane}
                    )
                else:
                    yield True, pltpu.make_async_copy(piece, into, back_local.at[which, kind])

    @pl.when(planes.inner)
    def _():
        arrived(0, 0, False)
        arrived(1, 0, False)

        @pl.when(planes.hosts)
        def _():
            arrived(0, 1, True)
            arrived(1, 1, True)

        work(True, 0, jnp.where(planes.hosts, 2 * span, span))
        each(back_copies(0, False), lambda copy: copy.start())

        @pl.when(planes.hosts)
        def _():
            each(back_copies(0, True), lambda copy: copy.start())

    arrived(0, 2, False)
    arrived(1, 2, False)
    work(False, 2 * span, span)
    each(back_copies(1, False), lambda copy: copy.start())
    ended = lambda copy: copy.wait_send() if copy.is_remote else copy.wait()
    each(back_copies(1, False), ended)

    @pl.when(planes.inner)
    def _():
        each(back_copies(0, False), ended)

        @pl.when(planes.hosts)
        def _():
            each(back_copies(0, True), ended)

    for kind in range(2):
        for which, buffer in enumerate((got, got_grad)):
            for src in range(n):
                piece = buffer.at[pl.ds((src * 2 + kind) * capacity, capacity)]
                comes = jnp.logical_or(src != me, planes.outer) if kind == 0 else src != me
                pl.when(comes)(pltpu.make_async_copy(piece, piece, back_recv.at[which, kind, src]).wait)
    stream.finish()


ANY = pl.BlockSpec(memory_space=pl.ANY)


def layer(lay, capacity, n_dp, tokens, gain_one, shift_one, w_qkv, w_out, gain_two, shift_two, w_router, routes, cotangent, weights):
    count, width = tokens.shape
    n = lay.n
    owners = len(lay.owners())
    span = n * capacity
    shape = jax.ShapeDtypeStruct
    hidden = weights[0].shape[1]
    every = [shape((n_dp, *weight.shape), BF16) for weight in weights]
    return pl.pallas_call(
        functools.partial(layer_kernel, lay, capacity, n_dp),
        out_shape=(
            shape((count, width), BF16),
            shape((3, UNIT, WIDE), BF16),
            shape((UNIT, WIDE), F32),
            shape((UNIT, WIDE), F32),
            shape((count, width), BF16),
            shape((count, width), F32),
            shape((count, width), BF16),
            shape((count, 128), F32),
            shape((2 * span, width), BF16),
            shape((2 * span, width), BF16),
            every[0],
            every[1],
            *every,
        ),
        in_specs=[VMEM] * 11 + [ANY] * 4,
        out_specs=[VMEM] * 8 + [ANY] * 8,
        scratch_shapes=[
            pltpu.VMEM((9, count, 2 * WIDE), BF16),
            pltpu.VMEM((UNIT, WIDE), BF16),
            pltpu.VMEM((2 * span, width), BF16),
            pltpu.VMEM((2 * span, width), BF16),
            pltpu.VMEM((3 * span, width), BF16),
            pltpu.VMEM((3 * span, width), BF16),
            pltpu.VMEM((width, hidden), BF16),
            pltpu.VMEM((hidden, width), BF16),
            pltpu.VMEM((2 * span, width), F32),
            pltpu.VMEM((2 * span, width), F32),
            pltpu.VMEM((width, hidden), BF16),
            pltpu.VMEM((hidden, width), BF16),
            DMA((9 * owners,)),
            DMA((3,)),
            DMA,
            DMA,
            DMA,
            DMA((2, 4, n_dp)),
            DMA((4, n_dp)),
            DMA((4,)),
            DMA((4,)),
            DMA((2, 2, n)),
            DMA((2, 3, n)),
            DMA((2, 2)),
            DMA((2, 3, n)),
            DMA((2, 2, n)),
            DMA((2, 2)),
        ],
        compiler_params=pltpu.CompilerParams(collective_id=0, has_side_effects=True, vmem_limit_bytes=60 * 2**20),
        cost_estimate=pl.CostEstimate(flops=50 * 10**9, bytes_accessed=100 * 2**20, transcendentals=10**7),
        name="layer",
    )(
        tokens, gain_one, shift_one, w_qkv, w_out, gain_two, shift_two, w_router, routes, routes.T, cotangent, *weights
    )


def back_kernel(
    lay, capacity,
    got, got_grad, middle, second_norm, gates, home_out, w_out, gain_two, w_router, routes, cotangent,
    unit, attended, log_total, first_norm, tokens, gain_one, w_qkv,
    block_out, tokens_grad, grads,
    grad_attended, grad_out, deltas, query_sum, staged, home, send, recv, out_send, home_recv, local,
):
    me = lax.axis_index("sp")
    is_short, seq, first_pair = lay.role(me)
    meet(plane_peers(lay.n))
    place, matches = slot_columns(lay, capacity, routes[...])
    slots = lax.broadcasted_iota(jnp.int32, (tokens.shape[0], got.shape[0]), 1)
    chosen = [hot(slots == place[c]) for c in range(2)]
    upstream = cotangent[...].astype(F32)
    gate = [gates[:, c : c + 1] for c in range(2)]
    total = middle[...]
    grad_gate = []
    for c in range(2):
        produced = dot(chosen[c], got[...])
        total = total + gate[c] * produced
        grad_gate.append(jnp.sum(upstream * produced, axis=1, keepdims=True))
    block_out[...] = total.astype(BF16)
    mean_grad = gate[0] * grad_gate[0] + gate[1] * grad_gate[1]
    grad_logits = sum(matches[c] * (gate[c] * (grad_gate[c] - mean_grad)) for c in range(2))
    high = grad_logits.astype(BF16)
    low = (grad_logits - high.astype(F32)).astype(BF16)
    router_grad = t_dot(second_norm[...], high) + t_dot(second_norm[...], low)
    grad_second = dot_t(high, w_router[...]) + dot_t(low, w_router[...])
    grad_second = grad_second + dot(chosen[0] + chosen[1], got_grad[...])
    hat, scale = normed(middle[...])
    gain_two_grad = jnp.sum(grad_second * hat, axis=0, keepdims=True)
    shift_two_grad = jnp.sum(grad_second, axis=0, keepdims=True)
    grad = upstream + norm_back(grad_second, gain_two[...], hat, scale)
    tokens_grad[...] = grad
    branch = grad.astype(BF16)
    grad_attended[...] = dot_t(branch, w_out[...]).astype(BF16)
    out_proj = t_dot(home_out[...], branch)
    width = w_out.shape[0]
    grads[:width, 3 * width : 4 * width] = out_proj.astype(BF16)
    grads[:width, 4 * width :] = router_grad.astype(BF16)
    started = to_owners(
        lay,
        me,
        lambda pair: pair * WIDE,
        lambda number: number,
        grad_attended,
        lambda start, rows: grad_out.at[pl.ds(pl.multiple_of(start, 16), rows)],
        send,
        recv,
        local,
        range(PAIRS),
    )
    query_sum[...] = jnp.zeros_like(query_sum)
    keep = lanes_first()
    lower = causal(BLOCK)
    wait_unit(lay, is_short, grad_out, recv)

    def make_delta(index, carry):
        part = pl.ds(pl.multiple_of(index * BLOCK, BLOCK), BLOCK)
        first, second = halves(grad_out[part].astype(F32) * attended[part])
        deltas[part] = jnp.where(
            keep, jnp.sum(first, axis=1, keepdims=True), jnp.sum(second, axis=1, keepdims=True)
        )
        return carry

    lax.fori_loop(0, lay.tasks(is_short), make_delta, 0)
    per = jnp.where(is_short, LEN_A // BLOCK, LEN_B // BLOCK)

    def task(index, carry):
        start, block = lay.task(is_short, index)
        base = pl.multiple_of(start + block * BLOCK, BLOCK)
        keys = unit[1, pl.ds(base, BLOCK)]
        values = unit[2, pl.ds(base, BLOCK)]
        key_both = jnp.concatenate(halves(keys), axis=0)

        def visit(place, state, diagonal):
            part = pl.ds(place, BLOCK)
            grad_key, grad_value = state
            queries = halves(unit[0, part])
            outs = halves(grad_out[part])
            weights, grads = [], []
            for which, (query, out) in enumerate(zip(queries, outs)):
                column = which * HEAD_DIM
                scores = dot_t(query, keys)
                if diagonal:
                    scores = jnp.where(lower, scores, NEGATIVE)
                weight = jnp.exp(scores - log_total[part, column : column + 1])
                grad = weight * (dot_t(out, values) - deltas[part, column : column + 1])
                weights.append(weight.astype(BF16))
                grads.append(grad.astype(BF16))
            grad_value = grad_value + t_dot(jnp.concatenate(weights, axis=0), jnp.concatenate(outs, axis=0))
            grad_key = grad_key + t_dot(jnp.concatenate(grads, axis=0), jnp.concatenate(queries, axis=0))
            query_sum[part] += dot(jnp.concatenate(grads, axis=1), key_both)
            return grad_key, grad_value

        zero = jnp.zeros((BLOCK, WIDE), F32)
        state = visit(base, (zero, zero), True)
        grad_key, grad_value = lax.fori_loop(
            block + 1, per, lambda i, state: visit(pl.multiple_of(start + i * BLOCK, BLOCK), state, False), state
        )
        part = pl.ds(base, BLOCK)
        staged[0, part] = (query_sum[part] * HEAD_DIM**-0.5).astype(BF16)
        staged[1, part] = grad_key.astype(BF16)
        staged[2, part] = grad_value.astype(BF16)
        for kind in range(3):
            send_home(
                lay, me, is_short, seq, first_pair, base, block, start, staged.at[kind], home, kind * PAIRS * WIDE,
                out_send.at[kind], home_recv.at[kind], local,
            )
        return carry

    lax.fori_loop(0, lay.tasks(is_short), task, 0)
    for kind in range(3):
        wait_home(lay, is_short, staged.at[kind], home_recv.at[kind], 1, False)
    grad_first = dot_t(home[...], w_qkv[...])
    hat, scale = normed(tokens[...].astype(F32))
    gain_one_grad = jnp.sum(grad_first * hat, axis=0, keepdims=True)
    shift_one_grad = jnp.sum(grad_first, axis=0, keepdims=True)
    tokens_grad[...] += norm_back(grad_first, gain_one[...], hat, scale)
    width = grads.shape[0] - 16
    for chunk in range(0, 3 * PAIRS * WIDE, 2 * WIDE):
        grads[:width, chunk : chunk + 2 * WIDE] = t_dot(first_norm[...], home[:, chunk : chunk + 2 * WIDE]).astype(BF16)
    grads[width:, :] = jnp.zeros((16, grads.shape[1]), BF16)
    for number, vector in enumerate((gain_one_grad, shift_one_grad, gain_two_grad, shift_two_grad)):
        grads[width : width + 1, number * width : (number + 1) * width] = vector.astype(BF16)
    finish_sends(me, started)
    for kind in range(3):
        wait_home(lay, is_short, staged.at[kind], out_send.at[kind], 1, True)


def backward(lay, capacity, values):
    count, width = values[2].shape
    owners = len(lay.owners())
    shape = jax.ShapeDtypeStruct
    return pl.pallas_call(
        functools.partial(back_kernel, lay, capacity),
        out_shape=(shape((count, width), BF16), shape((count, width), F32), shape((width + 16, 4 * width + 128), BF16)),
        in_specs=[VMEM] * 18,
        out_specs=[VMEM] * 3,
        scratch_shapes=[
            pltpu.VMEM((count, width), BF16),
            pltpu.VMEM((UNIT, WIDE), BF16),
            pltpu.VMEM((UNIT, WIDE), F32),
            pltpu.VMEM((UNIT, WIDE), F32),
            pltpu.VMEM((3, UNIT, WIDE), BF16),
            pltpu.VMEM((count, 3 * width), BF16),
            DMA((owners,)),
            DMA,
            DMA((3,)),
            DMA((3,)),
            DMA,
        ],
        compiler_params=pltpu.CompilerParams(collective_id=1, has_side_effects=True, vmem_limit_bytes=60 * 2**20),
        cost_estimate=pl.CostEstimate(flops=16 * 10**9, bytes_accessed=60 * 2**20, transcendentals=5 * 10**6),
        name="backward",
    )(*values)


def reduce_kernel(
    n, first, second, first_out, second_out, below_a, below_b, above_a, above_b,
    mine_a, mine_b, theirs_a, theirs_b, sums_a, sums_b, send, recv, load,
):
    me = lax.axis_index("dp")
    inner = jnp.logical_and(me >= 1, me <= n - 2)
    meet([(me + 1 < n, {"dp": me + 1}), (me > 0, {"dp": me - 1})])
    own, mine, theirs = (first, second), (mine_a, mine_b), (theirs_a, theirs_b)
    from_below, from_above, sums = (below_a, below_b), (above_a, above_b), (sums_a, sums_b)

    def copy(array, index, up, source):
        target = (from_below if up else from_above)[array].at[index]
        return remote(
            source, target, send.at[int(up), array, index], recv.at[int(up), array, index], {"dp": me + 1 if up else me - 1}
        )

    def fetch(source, buffer, number):
        moved = pltpu.make_async_copy(source, buffer, load.at[number])
        moved.start()
        return moved

    def order(up):
        return range(n - 1, -1, -1) if up else range(n)

    def wanted(index, up):
        return jnp.logical_and(inner, index > me if up else index < me)

    for index_up, index_down in zip(order(True), order(False)):
        for array in range(2):
            for up, index in ((True, index_up), (False, index_down)):
                begins = me == 1 if up else me == n - 2

                @pl.when(jnp.logical_and(wanted(index, up), begins))
                def _():
                    copy(array, index, up, own[array].at[index]).start()

    def came(array, index, up):
        buffer = (from_below if up else from_above)[array].at[index]
        pltpu.make_async_copy(buffer, buffer, recv.at[int(up), array, index]).wait()
        return buffer

    for index_up, index_down in zip(order(True), order(False)):
        for array in range(2):
            for up, index in ((True, index_up), (False, index_down)):
                begins = me == 1 if up else me == n - 2

                @pl.when(jnp.logical_and(wanted(index, up), jnp.logical_not(begins)))
                def _():
                    here = fetch(own[array].at[index], mine[array], 0)
                    there = fetch(came(array, index, up), theirs[array], 1)
                    here.wait()
                    there.wait()
                    sums[array][int(up), index] = (mine[array][...].astype(F32) + theirs[array][...].astype(F32)).astype(BF16)
                    copy(array, index, up, sums[array].at[int(up), index]).start()

    for array, out in enumerate((first_out, second_out)):
        out[...] = jnp.zeros_like(out)

        @pl.when(inner)
        def _():
            fetch(own[array].at[me], mine[array], 0).wait()
            out[...] += mine[array][...].astype(F32)

        for up in (True, False):

            @pl.when(me >= 2 if up else me <= n - 3)
            def _():
                fetch(came(array, me, up), theirs[array], 1).wait()
                out[...] += theirs[array][...].astype(F32)

    for array in range(2):
        for up in (True, False):
            for index in range(n):

                @pl.when(wanted(index, up))
                def _():
                    copy(array, index, up, sums[array].at[int(up), index]).wait_send()


def reduce_grads(n, first, second):
    shape = jax.ShapeDtypeStruct
    width, hidden = first.shape[1:]
    found = pl.pallas_call(
        functools.partial(reduce_kernel, n),
        out_shape=(shape((width, hidden), F32), shape((hidden, width), F32), *(shape(g.shape, BF16) for g in (first, second, first, second))),
        in_specs=[ANY] * 2,
        out_specs=[VMEM] * 2 + [ANY] * 4,
        scratch_shapes=[
            pltpu.VMEM((width, hidden), BF16),
            pltpu.VMEM((hidden, width), BF16),
            pltpu.VMEM((width, hidden), BF16),
            pltpu.VMEM((hidden, width), BF16),
            pltpu.VMEM((2, *first.shape), BF16),
            pltpu.VMEM((2, *second.shape), BF16),
            DMA((2, 2, n)),
            DMA((2, 2, n)),
            DMA((2,)),
        ],
        compiler_params=pltpu.CompilerParams(collective_id=2, has_side_effects=True, vmem_limit_bytes=60 * 2**20),
        cost_estimate=pl.CostEstimate(flops=10**7, bytes_accessed=200 * 2**20, transcendentals=0),
        name="reduce_grads",
    )(first, second)
    return found[:2]


def shards(
    tokens, ln1_gain, ln1_shift, w_qkv, w_out, ln2_gain, ln2_shift, w_router,
    train_w1, train_w2, frozen_w1, frozen_w2, routes, cotangent,
):
    lay = Layout(lax.axis_size("sp"))
    n_dp = lax.axis_size("dp")
    tokens, routes, cotangent = tokens[0], routes[0], cotangent[0]
    count, width = tokens.shape
    capacity = 2 * count // lay.n
    experts = w_router.shape[1]
    row = lambda vector: vector.reshape(1, -1)
    router_wide = jnp.pad(w_router, ((0, 0), (0, 128 - experts)))
    weights = [weight[0] for weight in (train_w1, train_w2, frozen_w1, frozen_w2)]
    first_norm, unit, attended, log_total, home, middle, second, gates, got, got_grad, first_grad, second_grad, *_ = layer(
        lay, capacity, n_dp, tokens, row(ln1_gain), row(ln1_shift), w_qkv, w_out, row(ln2_gain), row(ln2_shift),
        router_wide, routes, cotangent, weights,
    )
    block_out, tokens_grad, grads = backward(
        lay, capacity,
        (
            got, got_grad, middle, second, gates, home, w_out, row(ln2_gain), router_wide, routes, cotangent,
            unit, attended, log_total, first_norm, tokens, row(ln1_gain), w_qkv,
        ),
    )
    first_grad, second_grad = reduce_grads(n_dp, first_grad, second_grad)
    total = lax.psum(grads, ("sp", "dp")).astype(F32)
    vectors = total[width, : 4 * width].reshape(4, width)
    return (
        block_out[None],
        tokens_grad[None],
        vectors[0],
        vectors[1],
        total[:width, : 3 * width],
        total[:width, 3 * width : 4 * width],
        vectors[2],
        vectors[3],
        total[:width, 4 * width : 4 * width + experts],
        first_grad[None],
        second_grad[None],
    )


def solution(mesh):
    in_specs = (
        P("dp", "sp", None), P(), P(), P(), P(), P(), P(), P(),
        P("sp", None, "dp"), P("sp", "dp", None), P("sp", None, "dp"), P("sp", "dp", None),
        P("dp", "sp", None), P("dp", "sp", None),
    )
    out_specs = (
        P("dp", "sp", None), P("dp", "sp", None), P(), P(), P(), P(), P(), P(), P(),
        P("sp", None, "dp"), P("sp", "dp", None),
    )
    return jax.shard_map(shards, mesh=mesh, in_specs=in_specs, out_specs=out_specs, check_vma=False)
```

time: 906 us -> 655 us (0.72)
  waiting for transfers between devices: 515 us -> 58.6 us
  Pallas kernels: 287 us -> 549 us
  blocking collectives: 58.2 us -> 0 us
    pallas_call x6 -> x3, Pallas kernels: 287 us -> 549 us  [the longest x1 367 us: layer(): pl.pallas_call(functools.partial(layer_kernel, lay, capacity, n_dp), out_...]
    all_gather x4 -> x0, waiting for transfers between devices: 197 us -> none  [shards(): lax.all_gather(weight[0], 'dp')]
    reduce_scatter x2 -> x0, waiting for transfers between devices: 174 us -> none  [the longest x1 88.2 us: shards(): lax.psum_scatter(first_grad, 'dp', scatter_dimension=0).astype(F32)]
    psum x1, waiting for transfers between devices: 141 us -> 58.6 us  [shards(): total = lax.psum(grads, ('sp', 'dp')).astype(F32)]
    psum x1 -> x0, blocking collectives: 58.2 us -> none  [shards(): last = lax.psum((qkv_grad, gain_one, shift_one), ('sp', 'dp'))]
    unnamed x75 -> x21, local copies, waits for them, and re-layouts: 17.7 us -> 8.5 us
  transfers between devices with their start and end apart: 7 -> 1, of which waited for: 6 -> 1; matrix products, arithmetic and copies ran while one was open for 1% -> 0% of each run, Pallas kernels for 17% -> 18%
where the time goes in v2:
time: 655 us; the launch traced here: 647 us
  Pallas kernels  549 us (84%)
  waiting for transfers between devices  58.6 us (9%)
  local copies, waits for them, and re-layouts  21.6 us (3%)
  between operations  14.5 us (2%)
    pallas_call x1, Pallas kernels, layer(): pl.pallas_call(functools.partial(layer_kernel, lay, capacity, n_dp), out_...  367 us
    pallas_call x1, Pallas kernels, reduce_grads(): pl.pallas_call(functools.partial(reduce_kernel, n), out_shape=(shape((wid...  119 us
    pallas_call x1, Pallas kernels, backward(): pl.pallas_call(functools.partial(back_kernel, lay, capacity), out_shape=(...  63.4 us
    psum x1, waiting for transfers between devices, shards(): total = lax.psum(grads, ('sp', 'dp')).astype(F32)  58.6 us
  transfers between devices with their start and end apart: 1, of which 1 were waited for; matrix products, arithmetic and copies ran while one was open for 0% of the time, Pallas kernels for 18%

profile of v2, /device:TPU:0, one launch (start us, length us, event | category | flops | bytes accessed | tf_op | source)
XLA Modules:
  0.0 646.8 jit_solution(17160274330566410840)
XLA Ops:
  7.2 1.3 reshape.44.gain_one
  8.5 1.3 reshape.46.gain_two
  9.8 1.3 reshape.45.shift_one
  11.0 1.3 reshape.47.shift_two
  12.3 0.8 copy.26
  13.1 0.7 copy.27.routes_t
  13.8 0.9 copy.25
  14.7 0.7 pad.4.w_router
  15.4 366.7 %layer.1 = (bf16[384,768]{1,0:T(8,128)(2,1)}, bf16[3,3072,128]{2,1,0:T(8,128)(2,1)}, f32[3072,128]{1,0:T(8,128)}, f32[3072,128]{1,0:T(8,128)}, bf16[384,768]{1,0...) custom-call(bf16[384,768]{1,0:T(8,128)(2,1)} %bitcast.26, ...), custom_call_target="tpu_custom_call" | custom-call | flops 49999998976 | bytes 104857600 | tf_op jit(solution)/shard_map/layer/pallas_call | solution.py:645
  382.1 63.4 %backward.1 = (bf16[384,768]{1,0:T(8,128)(2,1)}, f32[384,768]{1,0:T(8,128)}, bf16[784,3200]{1,0:T(8,128)(2,1)}) custom-call(bf16[1536,768]{1,0:T(8,128)(2,1)} %get-tuple-element.28.got, bf16[1536,768]{1,0:T(8,128)(2,1)} %get-tuple-element.29.got_grad, f32[384,768]{1,0:T(8,128)} %get-tuple-element.30.middle, bf16[384,768]{1,0:T(8,128)(2,1)} %get-tuple-element.31.second_norm, ...), custom_call_target="tpu_custom_call" | custom-call | flops 16000000000 | bytes 62914560 | tf_op jit(solution)/shard_map/backward/pallas_call | solution.py:835
  445.6 118.7 %reduce_grads.1 = (f32[768,768]{1,0:T(8,128)}, f32[768,768]{1,0:T(8,128)}, bf16[4,768,768]{2,1,0:T(8,128)(2,1)}, bf16[4,768,768]{2,1,0:T(8,128)(2,1)}, bf16[4,76...) custom-call(bf16[4,768,768]{2,1,0:T(8,128)(2,1)} %get-tuple-element.41.first, bf16[4,768,768]{2,1,0:T(8,128)(2,1)} %get-tuple-element.42.second), custom_call_target="tpu_custom_call" | custom-call | flops 10000000 | bytes 209715200 | tf_op jit(solution)/shard_map/reduce_grads/pallas_call | solution.py:941
  564.3 58.6 %all-reduce.3.cloned.1.call-done = bf16[784,3200]{1,0:T(8,128)(2,1)} async-done(((bf16[784,3200]{1,0:T(8,128)(2,1)}), bf16[784,3200]{1,0:T(8,128)(2,1)}) %all-reduce.3.cloned.1.call-update) | async-done | bytes 5017616 | tf_op jit(solution)/shard_map/psum | solution.py:989
  622.9 1.0 slice.43
  623.9 0.8 copy.28
  624.6 3.2 convert_element_type.5
  627.8 0.6 slice_reduce_fusion
  628.5 1.6 slice.40
  630.1 3.4 slice.39
  633.5 0.8 copy.34
  634.3 1.0 copy.35
  635.3 0.3 copy-done.1
  635.6 1.4 copy.36
  637.0 1.1 copy-done
  638.1 1.4 copy.37
  (15 shorter events, 0.1 us)
Async XLA Ops:
  7.2 615.7 %all-reduce.3.cloned.1.call-start = ((), (), s32[]{:S(2)}) async-start(), calls=%async_computation | async-start | bytes 10035200 | tf_op jit(solution)/shard_map/psum | solution.py:989
  13.1 2.3 copy-start.3
  623.9 4.6 slice-start
  624.6 3.9 slice-start.1
  630.0 3.5 copy-start.4
  630.1 4.3 copy-start.2
  633.5 2.1 copy-start.1
  635.6 2.5 copy-start
Sparse Core Ops, SparseCore 0:
  445.7 177.1 all-reduce.2

commit v3 on v2

--- a/solution.py
+++ b/solution.py
@@ -1,4 +1,5 @@
 import functools
+import math
 
 import jax
 import jax.numpy as jnp
@@ -231,9 +232,9 @@
 
 
 class Weights:
-    def __init__(self, planes, own, every, send, recv, local):
+    def __init__(self, planes, own, every, send, recv):
         self.planes, self.own, self.every = planes, own, every
-        self.send, self.recv, self.local = send, recv, local
+        self.send, self.recv = send, recv
 
     def copy(self, array, index, up, source):
         other = self.planes.me + 1 if up else self.planes.me - 1
@@ -242,20 +243,14 @@
             {"dp": other},
         )
 
-    def begin(self):
+    def begin(self, arrays):
         me = self.planes.me
-        for array in range(4):
+        for array in arrays:
             for up in (True, False):
 
                 @pl.when(self.planes.takes(array < 2, up))
                 def _():
                     self.copy(array, me, up, self.own[array]).start()
-
-            pltpu.make_async_copy(self.own[array], self.every[array].at[me], self.local.at[array]).start()
-
-    def own_wait(self):
-        for array in range(4):
-            pltpu.make_async_copy(self.own[array], self.every[array].at[self.planes.me], self.local.at[array]).wait()
 
     def pairs(self, array, distance):
         me, n = self.planes.me, self.planes.n
@@ -290,6 +285,7 @@
 
 
 ROWS = 256
+LIMIT = 60 * 2**20
 
 
 def gelu_parts(value):
@@ -333,22 +329,23 @@
 
 def layer_kernel(
     lay, capacity, n_dp,
-    tokens, gain_one, shift_one, w_qkv, w_out, gain_two, shift_two, w_router, routes, routes_t, cotangent, own_a, own_b, own_c, own_d,
+    tokens, vectors, w_qkv, w_out, w_router, routes, routes_t, cotangent, own_a, own_b, own_c, own_d,
     first_norm, unit, attended, log_total, home, middle, second_norm, gates_out, got, got_grad, first_grad, second_grad,
-    all_a, all_b, all_c, all_d,
-    staged, staged_out, packed, packed_grad, rows_in, rows_grad, weight_a, weight_b, out_sum, in_sum, grad_a, grad_b,
-    send, recv, out_send, home_recv, local, stream_send, stream_recv, stream_local, load,
-    row_send, row_recv, row_local, back_send, back_recv, back_local,
+    all_a, all_b, all_c, all_d, hop_a, hop_b,
+    staged_out, packed, packed_grad, rows_in, rows_grad, weight_a, weight_b, out_sum, in_sum, out_other, in_other, grad_a, grad_b,
+    packed_gates, rows_gates, send, recv, out_send, home_recv, local, stream_send, stream_recv, load,
+    row_send, row_recv, row_local, back_send, back_recv, back_local, hop_send, hop_recv,
 ):
     n = lay.n
     me = lax.axis_index("sp")
+    gain_one, shift_one, gain_two, shift_two = (vectors.at[i : i + 1] for i in range(4))
     planes = Planes(n_dp)
     is_short, seq, first_pair = lay.role(me)
     meet(planes.peers(n))
     stream = Weights(
-        planes, (own_a, own_b, own_c, own_d), (all_a, all_b, all_c, all_d), stream_send, stream_recv, stream_local
+        planes, (own_a, own_b, own_c, own_d), (all_a, all_b, all_c, all_d), stream_send, stream_recv
     )
-    stream.begin()
+    stream.begin((2, 3))
 
     hat, _ = normed(tokens[...].astype(F32))
     first_norm[...] = (hat * gain_one[...] + shift_one[...]).astype(BF16)
@@ -356,20 +353,77 @@
     for chunk in range(9):
         kind, third = divmod(chunk, 3)
         made = dot(first_norm[...], w_qkv[:, chunk * 2 * WIDE : (chunk + 1) * 2 * WIDE]).astype(BF16)
-        staged[chunk] = made * BF16(HEAD_DIM**-0.5) if kind == 0 else made
+        made = made * BF16(HEAD_DIM**-0.5) if kind == 0 else made
+        area = packed.at[pl.ds(kind * tokens.shape[0], tokens.shape[0]), pl.ds(third * 2 * WIDE, 2 * WIDE)]
+        area[...] = made
         count = len(lay.owners())
         started += to_owners(
             lay,
             me,
             lambda pair: (pair % 2) * WIDE,
             lambda number: chunk * count + number,
-            staged.at[chunk],
+            area,
             lambda start, rows: unit.at[kind, pl.ds(pl.multiple_of(start, 16), rows)],
             send,
             recv.at[kind],
             local,
             (2 * third, 2 * third + 1),
         )
+    span = n * capacity
+    width, hidden = grad_a.shape
+    count = tokens.shape[0]
+    place = slot_rows(lay, capacity, routes_t[...])
+
+    def dispatch_copies(which, kind):
+        source, target = ((packed, rows_in), (packed_grad, rows_grad), (packed_gates, rows_gates))[which]
+        plane = jnp.where(planes.outer, planes.inward, planes.me) if kind == 0 else planes.me
+        area = jnp.where(planes.outer, 1, 0) if kind == 0 else 2
+
+        def block(buffer, number):
+            if which == 2:
+                return buffer.at[number]
+            return buffer.at[pl.ds(pl.multiple_of(number * capacity, 16), capacity)]
+
+        into = block(target, area * n + me)
+        for step in range(n):
+            to = lax.rem(me + step, n)
+            piece = block(source, to * 2 + kind)
+            far = remote(
+                piece, into, row_send.at[which, kind, step], row_recv.at[which, area, me], {"sp": to, "dp": plane}
+            )
+            if step:
+                yield True, far
+                continue
+            if kind == 0:
+                yield planes.outer, far
+            stays = planes.inner if kind == 0 else True
+            yield stays, pltpu.make_async_copy(piece, into, row_local.at[which, kind])
+
+    def each(copies, act):
+        for condition, copy in copies:
+            if condition is True:
+                act(copy)
+            else:
+                pl.when(condition)(functools.partial(act, copy))
+
+    def start(copy):
+        copy.start()
+
+    def end(copy):
+        if copy.is_remote:
+            copy.wait_send()
+        else:
+            copy.wait()
+
+    def dispatch(which):
+        for kind in range(2):
+            each(dispatch_copies(which, kind), start)
+
+    for first in range(0, 2 * span, ROWS):
+        slots = first + lax.broadcasted_iota(jnp.int32, (ROWS, count), 0)
+        chosen = hot(jnp.logical_or(slots == place[0], slots == place[1]))
+        packed_grad[first : first + ROWS] = dot(chosen, cotangent[...]).astype(BF16)
+    dispatch(1)
     for kind in range(3):
         wait_unit(lay, is_short, unit.at[kind], recv.at[kind])
     keep = lanes_first()
@@ -415,115 +469,101 @@
     wait_home(lay, is_short, staged_out, out_send, 1, True)
     wait_home(lay, is_short, staged_out, home_recv, 1, False)
 
-    span = n * capacity
-    width, hidden = grad_a.shape
+    stream.begin((0, 1))
+    stream.pass_on((2, 3), 1)
     x1 = tokens[...].astype(F32) + dot(home[...], w_out[...])
     middle[...] = x1
     hat, _ = normed(x1)
     second = (hat * gain_two[...] + shift_two[...]).astype(BF16)
     second_norm[...] = second
-    place = slot_rows(lay, capacity, routes_t[...])
-    count = tokens.shape[0]
-
-    def dispatch_copies(source, target, which, kind):
-        plane = jnp.where(planes.outer, planes.inward, planes.me) if kind == 0 else planes.me
-        area = jnp.where(planes.outer, 1, 0) if kind == 0 else 2
-        base = pl.multiple_of(area * span + me * capacity, 16)
-        into = target.at[pl.ds(base, capacity)]
-        for step in range(n):
-            to = lax.rem(me + step, n)
-            piece = source.at[pl.ds(pl.multiple_of((to * 2 + kind) * capacity, 16), capacity)]
-            far = remote(
-                piece, into, row_send.at[which, kind, step], row_recv.at[which, area, me], {"sp": to, "dp": plane}
-            )
-            if step:
-                yield True, far
-                continue
-            if kind == 0:
-                yield planes.outer, far
-            stays = planes.inner if kind == 0 else True
-            yield stays, pltpu.make_async_copy(piece, into, row_local.at[which, kind])
-
-    def each(copies, act):
-        for condition, copy in copies:
-            if condition is True:
-                act(copy)
-            else:
-
-                @pl.when(condition)
-                def _():
-                    act(copy)
-
-    def dispatch(source, target, which):
-        for kind in range(2):
-            each(dispatch_copies(source, target, which, kind), lambda copy: copy.start())
-
-    for start in range(0, 2 * span, ROWS):
-        slots = start + lax.broadcasted_iota(jnp.int32, (ROWS, count), 0)
-        packed[start : start + ROWS] = dot(hot(jnp.logical_or(slots == place[0], slots == place[1])), second).astype(BF16)
-    dispatch(packed, rows_in, 0)
+    for first in range(0, 2 * span, ROWS):
+        slots = first + lax.broadcasted_iota(jnp.int32, (ROWS, count), 0)
+        chosen = hot(jnp.logical_or(slots == place[0], slots == place[1]))
+        packed[first : first + ROWS] = dot(chosen, second).astype(BF16)
+    dispatch(0)
     logits = dot(second, w_router[...])
     index = lax.broadcasted_iota(jnp.int32, logits.shape, 1)
     chosen = [jnp.sum(jnp.where(index == routes[:, c : c + 1], logits, 0.0), axis=1, keepdims=True) for c in range(2)]
     top = jnp.maximum(chosen[0], chosen[1])
     exped = [jnp.exp(value - top) for value in chosen]
     gates = [value / (exped[0] + exped[1]) for value in exped]
-    upstream = cotangent[...].astype(F32)
     lane = lax.broadcasted_iota(jnp.int32, gates_out.shape, 1)
     gates_out[...] = jnp.where(lane == 0, gates[0], gates[1])
-    route_grads = [(gate * upstream).astype(BF16) for gate in gates]
-    for start in range(0, 2 * span, ROWS):
-        slots = start + lax.broadcasted_iota(jnp.int32, (ROWS, count), 0)
-        packed_grad[start : start + ROWS] = sum(dot(hot(slots == place[c]), route_grads[c]) for c in range(2)).astype(BF16)
-    dispatch(packed_grad, rows_grad, 1)
-    stream.own_wait()
-    stream.pass_on(range(4), 1)
-
-    def arrived(which, area, host):
-        buffer = (rows_in, rows_grad)[which]
+    column, _ = slot_columns(lay, capacity, routes[...])
+    for number in range(2 * n):
+        held = [
+            jnp.where(jnp.logical_and(lane < capacity, lane + number * capacity == column[c]), gates[c], 0.0)
+            for c in range(2)
+        ]
+        packed_gates[number] = jnp.broadcast_to(jnp.sum(held[0] + held[1], axis=0, keepdims=True), (8, 128))
+    dispatch(2)
+
+    def arrived(which, area):
+        buffer = (rows_in, rows_grad, rows_gates)[which]
         for src in range(n):
-            piece = buffer.at[pl.ds(area * span + src * capacity, capacity)]
+            piece = buffer.at[area * n + src] if which == 2 else buffer.at[pl.ds((area * n + src) * capacity, capacity)]
             wait = pltpu.make_async_copy(piece, piece, row_recv.at[which, area, src]).wait
-            if host:
+            if area == 1:
                 wait()
             else:
                 pl.when(src != me)(wait)
 
-    for which, (source, target) in enumerate(((packed, rows_in), (packed_grad, rows_grad))):
+    for which in (1, 0, 2):
         for kind in range(2):
-            each(
-                dispatch_copies(source, target, which, kind),
-                lambda copy: copy.wait_send() if hasattr(copy, "wait_send") and copy.is_remote else copy.wait(),
-            )
-
-    def work(trained, first_row, rows):
-        def clear(index, carry):
+            each(dispatch_copies(which, kind), end)
+
+    def take(area):
+        for which in (1, 0, 2):
+            arrived(which, area)
+        one = lax.broadcasted_iota(jnp.int32, (capacity, 128), 0) == lax.broadcasted_iota(jnp.int32, (capacity, 128), 1)
+
+        def gated(src, carry):
+            gate = jnp.sum(jnp.where(one, rows_gates[area * n + src, 0:1], 0.0), axis=1, keepdims=True)
+            part = pl.ds(pl.multiple_of((area * n + src) * capacity, 16), capacity)
+            rows_grad[part] = (gate * rows_grad[part].astype(F32)).astype(BF16)
+            return carry
+
+        lax.fori_loop(0, n, gated, 0)
+
+    def clear(sums, rows):
+        def one(index, carry):
             part = pl.ds(pl.multiple_of(index * ROWS, ROWS), ROWS)
-            out_sum[part] = jnp.zeros((ROWS, out_sum.shape[1]), F32)
-            in_sum[part] = jnp.zeros((ROWS, in_sum.shape[1]), F32)
+            for total in sums:
+                total[part] = jnp.zeros((ROWS, width), F32)
             return carry
 
-        lax.fori_loop(0, rows // ROWS, clear, 0)
+        lax.fori_loop(0, rows // ROWS, one, 0)
+
+    def work(trained, sums, first_row, rows, nearest, farthest):
         arrays = (0, 1) if trained else (2, 3)
         every = (all_a, all_b) if trained else (all_c, all_d)
+        own = (own_a, own_b) if trained else (own_c, own_d)
 
         def one(step, carry):
             distance, side = step // 2, lax.rem(step, 2)
             index = jnp.where(side == 0, planes.me - distance, planes.me + distance)
             real = jnp.logical_and(jnp.logical_and(index >= 0, index < n_dp), jnp.logical_or(side == 0, distance > 0))
 
-            @pl.when(jnp.logical_and(side == 0, distance >= 2))
+            @pl.when(jnp.logical_and(side == 0, distance >= (2 if trained else 3)))
             def _():
                 stream.pass_on(arrays, distance)
 
             @pl.when(real)
             def _():
-                loads = [
-                    pltpu.make_async_copy(every[i].at[index], (weight_a, weight_b)[i], load.at[i]) for i in range(2)
-                ]
-                for copy in loads:
-                    copy.start()
-                for copy in loads:
+                near = [pltpu.make_async_copy(own[i], (weight_a, weight_b)[i], load.at[i]) for i in range(2)]
+                far = [pltpu.make_async_copy(every[i].at[index], (weight_a, weight_b)[i], load.at[i]) for i in range(2)]
+
+                @pl.when(distance == 0)
+                def _():
+                    for copy in near:
+                        copy.start()
+
+                @pl.when(distance > 0)
+                def _():
+                    for copy in far:
+                        copy.start()
+
+                for copy in near:
                     copy.wait()
 
                 def chunk(number, carry):
@@ -535,8 +575,8 @@
                     if trained:
                         packed[part, :hidden] = active
                         packed_grad[part, :hidden] = back
-                    out_sum[part] += dot(active, weight_b[...])
-                    in_sum[part] += dot_t(back, weight_a[...])
+                    sums[0][part] += dot(active, weight_b[...])
+                    sums[1][part] += dot_t(back, weight_a[...])
                     return carry
 
                 lax.fori_loop(0, rows // ROWS, chunk, 0)
@@ -564,16 +604,17 @@
 
             return carry
 
-        lax.fori_loop(0, 2 * n_dp, one, 0)
-
-        def turn(number, carry):
-            part = pl.ds(pl.multiple_of(number * ROWS, ROWS), ROWS)
+        lax.fori_loop(2 * nearest, 2 * farthest + 2, one, 0)
+
+    def turn(sums, first_row, base, rows):
+        def one(number, carry):
+            part = pl.ds(pl.multiple_of(base + number * ROWS, ROWS), ROWS)
             here = pl.ds(pl.multiple_of(first_row + number * ROWS, ROWS), ROWS)
-            rows_in[here] = out_sum[part].astype(BF16)
-            rows_grad[here] = in_sum[part].astype(BF16)
+            rows_in[here] = sums[0][part].astype(BF16)
+            rows_grad[here] = sums[1][part].astype(BF16)
             return carry
 
-        lax.fori_loop(0, rows // ROWS, turn, 0)
+        lax.fori_loop(0, rows // ROWS, one, 0)
 
     def back_copies(kind, guest):
         area = 2 if kind else int(guest)
@@ -582,7 +623,7 @@
             into = target.at[pl.ds(pl.multiple_of((me * 2 + kind) * capacity, 16), capacity)]
             for step in range(n):
                 to = lax.rem(me + step, n)
-                piece = source.at[pl.ds(pl.multiple_of(area * span + to * capacity, 16), capacity)]
+                piece = source.at[pl.ds(pl.multiple_of((area * n + to) * capacity, 16), capacity)]
                 if step or guest:
                     yield True, remote(
                         piece, into, back_send.at[which, area, step], back_recv.at[which, kind, me], {"sp": to, "dp": plane}
@@ -590,37 +631,65 @@
                 else:
                     yield True, pltpu.make_async_copy(piece, into, back_local.at[which, kind])
 
+    def hops(act):
+        for up in (True, False):
+            for array, (whole, hop) in enumerate(((first_grad, hop_a), (second_grad, hop_b))):
+
+                @pl.when(planes.me == (1 if up else n_dp - 2))
+                def _():
+                    act(
+                        remote(
+                            whole.at[n_dp - 1 if up else 0], hop.at[int(up)], hop_send.at[int(up), array],
+                            hop_recv.at[int(up), array], {"dp": planes.me + (1 if up else -1)},
+                        )
+                    )
+
+    train_sums, frozen_sums = (out_sum, in_sum), (out_other, in_other)
+    train_rows = jnp.where(planes.hosts, 2 * span, span)
+    clear(frozen_sums, span)
+
     @pl.when(planes.inner)
     def _():
-        arrived(0, 0, False)
-        arrived(1, 0, False)
+        clear(train_sums, train_rows)
+        take(0)
 
         @pl.when(planes.hosts)
         def _():
-            arrived(0, 1, True)
-            arrived(1, 1, True)
-
-        work(True, 0, jnp.where(planes.hosts, 2 * span, span))
-        each(back_copies(0, False), lambda copy: copy.start())
-
-        @pl.when(planes.hosts)
-        def _():
-            each(back_copies(0, True), lambda copy: copy.start())
-
-    arrived(0, 2, False)
-    arrived(1, 2, False)
-    work(False, 2 * span, span)
-    each(back_copies(1, False), lambda copy: copy.start())
-    ended = lambda copy: copy.wait_send() if copy.is_remote else copy.wait()
-    each(back_copies(1, False), ended)
+            take(1)
+
+        work(True, train_sums, 0, train_rows, 0, 0)
+        stream.pass_on((0, 1), 1)
+        work(True, train_sums, 0, train_rows, 1, 1)
+
+    take(2)
+    work(False, frozen_sums, 2 * span, span, 0, 1)
+    stream.pass_on((2, 3), 2)
+    work(False, frozen_sums, 2 * span, span, 2, n_dp - 1)
+    turn(frozen_sums, 2 * span, 0, span)
+    each(back_copies(1, False), start)
 
     @pl.when(planes.inner)
     def _():
-        each(back_copies(0, False), ended)
+        work(True, train_sums, 0, train_rows, 2, n_dp - 1)
 
         @pl.when(planes.hosts)
         def _():
-            each(back_copies(0, True), ended)
+            turn(train_sums, span, span, span)
+            each(back_copies(0, True), start)
+
+        turn(train_sums, 0, 0, span)
+        each(back_copies(0, False), start)
+        hops(start)
+
+    each(back_copies(1, False), end)
+
+    @pl.when(planes.inner)
+    def _():
+        each(back_copies(0, False), end)
+
+        @pl.when(planes.hosts)
+        def _():
+            each(back_copies(0, True), end)
 
     for kind in range(2):
         for which, buffer in enumerate((got, got_grad)):
@@ -629,12 +698,19 @@
                 comes = jnp.logical_or(src != me, planes.outer) if kind == 0 else src != me
                 pl.when(comes)(pltpu.make_async_copy(piece, piece, back_recv.at[which, kind, src]).wait)
     stream.finish()
+    hops(end)
+    for up in (True, False):
+        for array, hop in enumerate((hop_a, hop_b)):
+
+            @pl.when(planes.me == (2 if up else n_dp - 3))
+            def _():
+                pltpu.make_async_copy(hop.at[int(up)], hop.at[int(up)], hop_recv.at[int(up), array]).wait()
 
 
 ANY = pl.BlockSpec(memory_space=pl.ANY)
 
 
-def layer(lay, capacity, n_dp, tokens, gain_one, shift_one, w_qkv, w_out, gain_two, shift_two, w_router, routes, cotangent, weights):
+def layer(lay, capacity, n_dp, tokens, vectors, w_qkv, w_out, w_router, routes, cotangent, weights):
     count, width = tokens.shape
     n = lay.n
     owners = len(lay.owners())
@@ -658,11 +734,12 @@
             every[0],
             every[1],
             *every,
+            shape((2, *weights[0].shape), BF16),
+            shape((2, *weights[1].shape), BF16),
         ),
-        in_specs=[VMEM] * 11 + [ANY] * 4,
-        out_specs=[VMEM] * 8 + [ANY] * 8,
+        in_specs=[VMEM] * 8 + [ANY] * 4,
+        out_specs=[VMEM] * 8 + [ANY] * 10,
         scratch_shapes=[
-            pltpu.VMEM((9, count, 2 * WIDE), BF16),
             pltpu.VMEM((UNIT, WIDE), BF16),
             pltpu.VMEM((2 * span, width), BF16),
             pltpu.VMEM((2 * span, width), BF16),
@@ -672,8 +749,12 @@
             pltpu.VMEM((hidden, width), BF16),
             pltpu.VMEM((2 * span, width), F32),
             pltpu.VMEM((2 * span, width), F32),
+            pltpu.VMEM((span, width), F32),
+            pltpu.VMEM((span, width), F32),
             pltpu.VMEM((width, hidden), BF16),
             pltpu.VMEM((hidden, width), BF16),
+            pltpu.VMEM((2 * n, 8, 128), F32),
+            pltpu.VMEM((3 * n, 8, 128), F32),
             DMA((9 * owners,)),
             DMA((3,)),
             DMA,
@@ -682,32 +763,301 @@
             DMA((2, 4, n_dp)),
             DMA((4, n_dp)),
             DMA((4,)),
-            DMA((4,)),
-            DMA((2, 2, n)),
-            DMA((2, 3, n)),
-            DMA((2, 2)),
+            DMA((3, 2, n)),
+            DMA((3, 3, n)),
+            DMA((3, 2)),
             DMA((2, 3, n)),
             DMA((2, 2, n)),
             DMA((2, 2)),
+            DMA((2, 2)),
+            DMA((2, 2)),
         ],
-        compiler_params=pltpu.CompilerParams(collective_id=0, has_side_effects=True, vmem_limit_bytes=60 * 2**20),
+        compiler_params=pltpu.CompilerParams(collective_id=0, has_side_effects=True, vmem_limit_bytes=LIMIT),
         cost_estimate=pl.CostEstimate(flops=50 * 10**9, bytes_accessed=100 * 2**20, transcendentals=10**7),
         name="layer",
     )(
-        tokens, gain_one, shift_one, w_qkv, w_out, gain_two, shift_two, w_router, routes, routes.T, cotangent, *weights
+        tokens, vectors, w_qkv, w_out, w_router, routes, routes.T, cotangent, *weights
     )
 
 
+class Sum:
+    def __init__(self, n_sp, n_dp, pieces, quantum, needed):
+        self.n_sp, self.n_dp = n_sp, n_dp
+        self.bits = n_sp.bit_length() - 1
+        unit = math.lcm(16 * n_sp * n_dp, quantum)
+        units = -(-needed // unit)
+        pieces = min(pieces, units)
+        sizes = [units // pieces + (p < units % pieces) for p in range(pieces)]
+        self.pieces = [(unit * sum(sizes[:p]), unit * size) for p, size in enumerate(sizes)]
+        self.rows = unit * units
+        self.steps = 2 * self.bits + 2
+
+    def order(self, piece):
+        later = list(range(1, self.bits))
+        return [0] + (later[::-1] if piece % 2 else later)
+
+    def landing(self):
+        places, start = [], 0
+        for _, rows in self.pieces:
+            places.append([])
+            for step in range(self.bits + 1):
+                rows = rows // 2 if step < self.bits else rows
+                places[-1].append((start, rows))
+                start += rows
+        return places, start
+
+    def bind(self, mine, landed, whole, send, recv):
+        self.mine, self.landed, self.whole, self.send, self.recv = mine, landed, whole, send, recv
+        self.me, self.plane = lax.axis_index("sp"), lax.axis_index("dp")
+        self.places, _ = self.landing()
+        self.starts = [[start] for start, _ in self.pieces]
+        for piece, (_, rows) in enumerate(self.pieces):
+            for bit in self.order(piece):
+                rows //= 2
+                value = (self.me // (1 << bit)) % 2
+                self.starts[piece].append(self.starts[piece][-1] + value * rows)
+
+    def partner(self, bit):
+        value = (self.me // (1 << bit)) % 2
+        return self.me + (1 - 2 * value) * (1 << bit)
+
+    def peers(self):
+        found = [(True, {"sp": self.partner(bit)}) for bit in range(self.bits)]
+        return found + [(True, {"dp": lax.rem(self.plane + step, self.n_dp)}) for step in range(1, self.n_dp)]
+
+    def cut(self, start, rows):
+        return pl.ds(pl.multiple_of(start, 16), rows)
+
+    def copies(self, piece, step):
+        bits = self.bits
+        rows = self.pieces[piece][1]
+        if step < bits or step > bits + 1:
+            level = step if step < bits else 2 * bits + 1 - step
+            bit = self.order(piece)[level]
+            half = rows >> (level + 1)
+            held, kept = self.starts[piece][level], self.starts[piece][level + 1]
+            if step < bits:
+                start, _ = self.places[piece][step]
+                source = self.mine.at[self.cut(2 * held + half - kept, half)]
+                target = self.landed.at[pl.ds(start, half)]
+            else:
+                source = target = self.whole.at[self.cut(kept, half)]
+            yield remote(source, target, self.send.at[piece, step, 0], self.recv.at[piece, step, 0], self.partner(bit))
+            return
+        block = (rows >> bits) // self.n_dp
+        base = self.starts[piece][bits]
+        start, _ = self.places[piece][bits]
+        for far in range(1, self.n_dp):
+            other = lax.rem(self.plane + far, self.n_dp)
+            if step == bits:
+                source = self.mine.at[self.cut(base + other * block, block)]
+                target = self.landed.at[self.cut(start + self.plane * block, block)]
+            else:
+                source = target = self.whole.at[self.cut(base + self.plane * block, block)]
+            yield remote(source, target, self.send.at[piece, step, far], self.recv.at[piece, step, far], {"dp": other})
+
+    def start(self, piece, step):
+        for copy in self.copies(piece, step):
+            copy.start()
+
+    def add(self, piece, step):
+        for copy in self.copies(piece, step):
+            copy.wait()
+        bits, rows = self.bits, self.pieces[piece][1]
+        if step > bits:
+            return
+        start, _ = self.places[piece][step]
+        if step < bits:
+            size, kept = rows >> (step + 1), self.starts[piece][step + 1]
+            for first, count in blocks(size):
+
+                def one(number, carry):
+                    part = self.cut(kept + first + number * count[0], count[0])
+                    here = self.cut(start + first + number * count[0], count[0])
+                    self.mine[part] = (self.mine[part].astype(F32) + self.landed[here].astype(F32)).astype(BF16)
+                    return carry
+
+                lax.fori_loop(0, count[1], one, 0)
+            return
+        block = (rows >> bits) // self.n_dp
+        own = self.cut(self.starts[piece][bits] + self.plane * block, block)
+        total = self.mine[own].astype(F32)
+        for far in range(1, self.n_dp):
+            other = lax.rem(self.plane + far, self.n_dp)
+            total = total + self.landed[self.cut(start + other * block, block)].astype(F32)
+        self.whole[own] = total.astype(BF16)
+
+
+def blocks(rows, size=512):
+    found = []
+    if rows >= size:
+        found.append((0, (size, rows // size)))
+    if rows % size:
+        found.append((rows - rows % size, (rows % size, 1)))
+    return found
+
+
+def run_sum(total, ready=lambda piece: None, done=lambda piece: None):
+    count = len(total.pieces)
+    for tick in range(total.steps + count):
+        for piece in range(count):
+            step = tick - piece
+            if step > 0 and step <= total.steps:
+                total.add(piece, step - 1)
+                if step == total.steps:
+                    done(piece)
+            if step == 0:
+                ready(piece)
+            if 0 <= step < total.steps:
+                total.start(piece, step)
+
+
+class Gather:
+    def __init__(self, n, own, hop, below, above, theirs, sums, stage, send, recv, load):
+        self.n, self.own, self.hop, self.below, self.above, self.stage = n, own, hop, below, above, stage
+        self.theirs, self.sums, self.send, self.recv, self.load = theirs, sums, send, recv, load
+        self.me = lax.axis_index("dp")
+        self.inner = jnp.logical_and(self.me >= 1, self.me <= n - 2)
+
+    def copy(self, array, index, up, source):
+        target = (self.below if up else self.above)[array].at[index]
+        other = self.me + 1 if up else self.me - 1
+        return remote(
+            source, target, self.send.at[int(up), array, index], self.recv.at[int(up), array, index], {"dp": other}
+        )
+
+    def fetch(self, source, buffer, number):
+        moved = pltpu.make_async_copy(source, buffer, self.load.at[number])
+        moved.start()
+        return moved
+
+    def wanted(self, index, up):
+        return jnp.logical_and(self.inner, index > self.me if up else index < self.me)
+
+    def begins(self, up):
+        return self.me == 1 if up else self.me == self.n - 2
+
+    def hopped(self, index, up):
+        if index not in (0, self.n - 1):
+            return False
+        return self.me == 2 if up else self.me == self.n - 3
+
+    def begin(self, array, index, up):
+        @pl.when(jnp.logical_and(self.wanted(index, up), self.begins(up)))
+        def _():
+            self.copy(array, index, up, self.own[array].at[index]).start()
+
+    def came(self, array, index, up):
+        buffer = (self.below if up else self.above)[array].at[index]
+        pltpu.make_async_copy(buffer, buffer, self.recv.at[int(up), array, index]).wait()
+        return buffer
+
+    def pass_on(self, array, index, up):
+        @pl.when(jnp.logical_and(self.wanted(index, up), jnp.logical_not(self.begins(up))))
+        def _():
+            total, theirs = self.sums[array].at[int(up)], self.theirs[array]
+            here = self.fetch(self.own[array].at[index], total, 0)
+            hopped = self.hopped(index, up)
+
+            @pl.when(hopped)
+            def _():
+                self.fetch(self.hop[array].at[int(up)], theirs, 1).wait()
+
+            @pl.when(jnp.logical_not(hopped))
+            def _():
+                self.fetch(self.came(array, index, up), theirs, 1).wait()
+
+            here.wait()
+            total[...] = (total[...].astype(F32) + theirs[...].astype(F32)).astype(BF16)
+            self.copy(array, index, up, total).start()
+
+    def finish(self, array, index, up):
+        waits = self.wanted(index, up)
+        if index in (0, self.n - 1):
+            waits = jnp.logical_and(waits, jnp.logical_not(self.begins(up)))
+
+        @pl.when(waits)
+        def _():
+            self.copy(array, index, up, self.sums[array].at[int(up)]).wait_send()
+
+    def total(self, array, out):
+        theirs = self.theirs[array]
+
+        @pl.when(self.inner)
+        def _():
+            self.fetch(self.own[array].at[self.me], theirs, 0).wait()
+
+        @pl.when(jnp.logical_not(self.inner))
+        def _():
+            theirs[...] = jnp.zeros_like(theirs)
+
+        sides = ((True, self.me >= 2), (False, self.me <= self.n - 3))
+        for up, comes in sides:
+
+            @pl.when(comes)
+            def _():
+                self.fetch(self.came(array, self.me, up), self.sums[array].at[int(up)], 1).wait()
+
+        size = out.shape[0] // 6
+        lanes = pl.ds(0, out.shape[1])
+        stores = []
+        for number in range(6):
+            part = pl.ds(number * size, size)
+            stage = self.stage.at[number % 2, pl.ds(0, size), lanes]
+            if number >= 2:
+                stores[number - 2].wait()
+            stage[...] = theirs[part].astype(F32)
+            for up, comes in sides:
+
+                @pl.when(comes)
+                def _():
+                    stage[...] += self.sums[array][int(up), part].astype(F32)
+
+            stores.append(pltpu.make_async_copy(stage, out.at[part], self.load.at[3 + number % 2]))
+            stores[number].start()
+        for store in stores[-2:]:
+            store.wait()
+
+
+def gather_scratch(n, first, second):
+    shapes = [first.shape[1:], second.shape[1:]]
+    return [
+        *(pltpu.VMEM(shape, BF16) for shape in shapes),
+        *(pltpu.VMEM((2, *shape), BF16) for shape in shapes),
+        pltpu.VMEM((2, 128, max(map(max, shapes))), F32),
+        DMA((2, 2, n)),
+        DMA((2, 2, n)),
+        DMA((5,)),
+    ]
+
+
 def back_kernel(
-    lay, capacity,
-    got, got_grad, middle, second_norm, gates, home_out, w_out, gain_two, w_router, routes, cotangent,
-    unit, attended, log_total, first_norm, tokens, gain_one, w_qkv,
-    block_out, tokens_grad, grads,
+    lay, capacity, replicated,
+    got, got_grad, middle, second_norm, gates, home_out, w_out, vectors, w_router, routes, cotangent,
+    unit, attended, log_total, first_norm, tokens, w_qkv, first_own, second_own, hop_a, hop_b,
+    block_out, tokens_grad, summed, first_total, second_total, below_a, below_b, above_a, above_b,
     grad_attended, grad_out, deltas, query_sum, staged, home, send, recv, out_send, home_recv, local,
+    theirs_a, theirs_b, sums_a, sums_b, stage, pass_send, pass_recv, load,
+    grads, landed, sum_send, sum_recv,
 ):
+    n_dp = first_own.shape[0]
+    gather = Gather(
+        n_dp, (first_own, second_own), (hop_a, hop_b), (below_a, below_b), (above_a, above_b), (theirs_a, theirs_b),
+        (sums_a, sums_b), stage, pass_send, pass_recv, load,
+    )
+    gain_one, gain_two = vectors.at[0:1], vectors.at[2:3]
+    replicated.bind(grads, landed, summed, sum_send, sum_recv)
     me = lax.axis_index("sp")
     is_short, seq, first_pair = lay.role(me)
-    meet(plane_peers(lay.n))
+    everywhere = [(True, {"dp": lax.rem(gather.me + step, n_dp)}) for step in range(1, n_dp)]
+    meet(plane_peers(lay.n) + everywhere)
+    kept = pltpu.make_async_copy(attended, deltas, load.at[2])
+    kept.start()
+    inside = [(up, index) for index in range(1, n_dp - 1) for up in (True, False)]
+    ends = [(True, n_dp - 1), (False, 0)]
+    for array in range(2):
+        for up, index in inside:
+            gather.begin(array, index, up)
     place, matches = slot_columns(lay, capacity, routes[...])
     slots = lax.broadcasted_iota(jnp.int32, (tokens.shape[0], got.shape[0]), 1)
     chosen = [hot(slots == place[c]) for c in range(2)]
@@ -736,8 +1086,12 @@
     grad_attended[...] = dot_t(branch, w_out[...]).astype(BF16)
     out_proj = t_dot(home_out[...], branch)
     width = w_out.shape[0]
-    grads[:width, 3 * width : 4 * width] = out_proj.astype(BF16)
-    grads[:width, 4 * width :] = router_grad.astype(BF16)
+
+    def put(column, value):
+        for lane in range(0, value.shape[1], WIDE):
+            grads[pl.ds((column + lane) // WIDE * width, width)] = value[:, lane : lane + WIDE].astype(BF16)
+
+    put(0, out_proj)
     started = to_owners(
         lay,
         me,
@@ -750,14 +1104,18 @@
         local,
         range(PAIRS),
     )
+    for array in range(2):
+        for up, index in ends:
+            gather.pass_on(array, index, up)
     query_sum[...] = jnp.zeros_like(query_sum)
     keep = lanes_first()
     lower = causal(BLOCK)
     wait_unit(lay, is_short, grad_out, recv)
+    kept.wait()
 
     def make_delta(index, carry):
         part = pl.ds(pl.multiple_of(index * BLOCK, BLOCK), BLOCK)
-        first, second = halves(grad_out[part].astype(F32) * attended[part])
+        first, second = halves(grad_out[part].astype(F32) * deltas[part])
         deltas[part] = jnp.where(
             keep, jnp.sum(first, axis=1, keepdims=True), jnp.sum(second, axis=1, keepdims=True)
         )
@@ -817,12 +1175,31 @@
     gain_one_grad = jnp.sum(grad_first * hat, axis=0, keepdims=True)
     shift_one_grad = jnp.sum(grad_first, axis=0, keepdims=True)
     tokens_grad[...] += norm_back(grad_first, gain_one[...], hat, scale)
-    width = grads.shape[0] - 16
-    for chunk in range(0, 3 * PAIRS * WIDE, 2 * WIDE):
-        grads[:width, chunk : chunk + 2 * WIDE] = t_dot(first_norm[...], home[:, chunk : chunk + 2 * WIDE]).astype(BF16)
-    grads[width:, :] = jnp.zeros((16, grads.shape[1]), BF16)
-    for number, vector in enumerate((gain_one_grad, shift_one_grad, gain_two_grad, shift_two_grad)):
-        grads[width : width + 1, number * width : (number + 1) * width] = vector.astype(BF16)
+    parts = (gain_one_grad, shift_one_grad, gain_two_grad, shift_two_grad)
+    row = lax.broadcasted_iota(jnp.int32, (8, width), 0)
+    stack = sum(jnp.where(row == i, part, 0.0) for i, part in enumerate(parts)).astype(BF16)
+    lane = lax.broadcasted_iota(jnp.int32, (8, WIDE), 1)
+    spot = hot(lane == HEAD_DIM + lax.broadcasted_iota(jnp.int32, (8, WIDE), 0))
+    grads[pl.ds(width // WIDE * width, width)] = (router_grad + t_dot(stack, spot)).astype(BF16)
+    first = 8
+    last = first + 3 * PAIRS
+    for spare in [7, *range(last, replicated.rows // width)]:
+        grads[pl.ds(spare * width, width)] = jnp.zeros((width, WIDE), BF16)
+
+    def ready(piece):
+        start, rows = replicated.pieces[piece]
+        for column in range(start // width, (start + rows) // width, 2):
+            if first <= column < last:
+                lanes = pl.ds((column - first) * WIDE, 2 * WIDE)
+                put(column * WIDE, t_dot(first_norm[...], home[:, lanes]))
+
+    run_sum(replicated, ready)
+    for array, out in enumerate((first_total, second_total)):
+        for up, index in inside:
+            gather.pass_on(array, index, up)
+        for up, index in inside + ends:
+            gather.finish(array, index, up)
+        gather.total(array, out)
     finish_sends(me, started)
     for kind in range(3):
         wait_home(lay, is_short, staged.at[kind], out_send.at[kind], 1, True)
@@ -832,11 +1209,16 @@
     count, width = values[2].shape
     owners = len(lay.owners())
     shape = jax.ShapeDtypeStruct
+    slices = values[-4:-2]
+    replicated = Sum(lay.n, slices[0].shape[0], 6, 2 * width, 26 * width)
     return pl.pallas_call(
-        functools.partial(back_kernel, lay, capacity),
-        out_shape=(shape((count, width), BF16), shape((count, width), F32), shape((width + 16, 4 * width + 128), BF16)),
-        in_specs=[VMEM] * 18,
-        out_specs=[VMEM] * 3,
+        functools.partial(back_kernel, lay, capacity, replicated),
+        out_shape=(
+            shape((count, width), BF16), shape((count, width), F32), shape((replicated.rows, WIDE), BF16),
+            *(shape(g.shape[1:], F32) for g in slices), *(shape(g.shape, BF16) for g in slices * 2),
+        ),
+        in_specs=[VMEM] * 12 + [ANY] + [VMEM] * 4 + [ANY] * 4,
+        out_specs=[VMEM] * 3 + [ANY] * 6,
         scratch_shapes=[
             pltpu.VMEM((count, width), BF16),
             pltpu.VMEM((UNIT, WIDE), BF16),
@@ -849,116 +1231,16 @@
             DMA((3,)),
             DMA((3,)),
             DMA,
+            *gather_scratch(slices[0].shape[0], *slices),
+            pltpu.VMEM((replicated.rows, WIDE), BF16),
+            pltpu.VMEM((replicated.landing()[1], WIDE), BF16),
+            DMA((len(replicated.pieces), replicated.steps, slices[0].shape[0])),
+            DMA((len(replicated.pieces), replicated.steps, slices[0].shape[0])),
         ],
-        compiler_params=pltpu.CompilerParams(collective_id=1, has_side_effects=True, vmem_limit_bytes=60 * 2**20),
+        compiler_params=pltpu.CompilerParams(collective_id=1, has_side_effects=True, vmem_limit_bytes=LIMIT),
         cost_estimate=pl.CostEstimate(flops=16 * 10**9, bytes_accessed=60 * 2**20, transcendentals=5 * 10**6),
         name="backward",
     )(*values)
-
-
-def reduce_kernel(
-    n, first, second, first_out, second_out, below_a, below_b, above_a, above_b,
-    mine_a, mine_b, theirs_a, theirs_b, sums_a, sums_b, send, recv, load,
-):
-    me = lax.axis_index("dp")
-    inner = jnp.logical_and(me >= 1, me <= n - 2)
-    meet([(me + 1 < n, {"dp": me + 1}), (me > 0, {"dp": me - 1})])
-    own, mine, theirs = (first, second), (mine_a, mine_b), (theirs_a, theirs_b)
-    from_below, from_above, sums = (below_a, below_b), (above_a, above_b), (sums_a, sums_b)
-
-    def copy(array, index, up, source):
-        target = (from_below if up else from_above)[array].at[index]
-        return remote(
-            source, target, send.at[int(up), array, index], recv.at[int(up), array, index], {"dp": me + 1 if up else me - 1}
-        )
-
-    def fetch(source, buffer, number):
-        moved = pltpu.make_async_copy(source, buffer, load.at[number])
-        moved.start()
-        return moved
-
-    def order(up):
-        return range(n - 1, -1, -1) if up else range(n)
-
-    def wanted(index, up):
-        return jnp.logical_and(inner, index > me if up else index < me)
-
-    for index_up, index_down in zip(order(True), order(False)):
-        for array in range(2):
-            for up, index in ((True, index_up), (False, index_down)):
-                begins = me == 1 if up else me == n - 2
-
-                @pl.when(jnp.logical_and(wanted(index, up), begins))
-                def _():
-                    copy(array, index, up, own[array].at[index]).start()
-
-    def came(array, index, up):
-        buffer = (from_below if up else from_above)[array].at[index]
-        pltpu.make_async_copy(buffer, buffer, recv.at[int(up), array, index]).wait()
-        return buffer
-
-    for index_up, index_down in zip(order(True), order(False)):
-        for array in range(2):
-            for up, index in ((True, index_up), (False, index_down)):
-                begins = me == 1 if up else me == n - 2
-
-                @pl.when(jnp.logical_and(wanted(index, up), jnp.logical_not(begins)))
-                def _():
-                    here = fetch(own[array].at[index], mine[array], 0)
-                    there = fetch(came(array, index, up), theirs[array], 1)
-                    here.wait()
-                    there.wait()
-                    sums[array][int(up), index] = (mine[array][...].astype(F32) + theirs[array][...].astype(F32)).astype(BF16)
-                    copy(array, index, up, sums[array].at[int(up), index]).start()
-
-    for array, out in enumerate((first_out, second_out)):
-        out[...] = jnp.zeros_like(out)
-
-        @pl.when(inner)
-        def _():
-            fetch(own[array].at[me], mine[array], 0).wait()
-            out[...] += mine[array][...].astype(F32)
-
-        for up in (True, False):
-
-            @pl.when(me >= 2 if up else me <= n - 3)
-            def _():
-                fetch(came(array, me, up), theirs[array], 1).wait()
-                out[...] += theirs[array][...].astype(F32)
-
-    for array in range(2):
-        for up in (True, False):
-            for index in range(n):
-
-                @pl.when(wanted(index, up))
-                def _():
-                    copy(array, index, up, sums[array].at[int(up), index]).wait_send()
-
-
-def reduce_grads(n, first, second):
-    shape = jax.ShapeDtypeStruct
-    width, hidden = first.shape[1:]
-    found = pl.pallas_call(
-        functools.partial(reduce_kernel, n),
-        out_shape=(shape((width, hidden), F32), shape((hidden, width), F32), *(shape(g.shape, BF16) for g in (first, second, first, second))),
-        in_specs=[ANY] * 2,
-        out_specs=[VMEM] * 2 + [ANY] * 4,
-        scratch_shapes=[
-            pltpu.VMEM((width, hidden), BF16),
-            pltpu.VMEM((hidden, width), BF16),
-            pltpu.VMEM((width, hidden), BF16),
-            pltpu.VMEM((hidden, width), BF16),
-            pltpu.VMEM((2, *first.shape), BF16),
-            pltpu.VMEM((2, *second.shape), BF16),
-            DMA((2, 2, n)),
-            DMA((2, 2, n)),
-            DMA((2,)),
-        ],
-        compiler_params=pltpu.CompilerParams(collective_id=2, has_side_effects=True, vmem_limit_bytes=60 * 2**20),
-        cost_estimate=pl.CostEstimate(flops=10**7, bytes_accessed=200 * 2**20, transcendentals=0),
-        name="reduce_grads",
-    )(first, second)
-    return found[:2]
 
 
 def shards(
@@ -971,35 +1253,38 @@
     count, width = tokens.shape
     capacity = 2 * count // lay.n
     experts = w_router.shape[1]
-    row = lambda vector: vector.reshape(1, -1)
     router_wide = jnp.pad(w_router, ((0, 0), (0, 128 - experts)))
+    vectors = jnp.stack([ln1_gain, ln1_shift, ln2_gain, ln2_shift])
     weights = [weight[0] for weight in (train_w1, train_w2, frozen_w1, frozen_w2)]
-    first_norm, unit, attended, log_total, home, middle, second, gates, got, got_grad, first_grad, second_grad, *_ = layer(
-        lay, capacity, n_dp, tokens, row(ln1_gain), row(ln1_shift), w_qkv, w_out, row(ln2_gain), row(ln2_shift),
-        router_wide, routes, cotangent, weights,
-    )
-    block_out, tokens_grad, grads = backward(
+    (
+        first_norm, unit, attended, log_total, home, middle, second, gates, got, got_grad, first_grad, second_grad,
+        _, _, _, _, hop_a, hop_b,
+    ) = layer(lay, capacity, n_dp, tokens, vectors, w_qkv, w_out, router_wide, routes, cotangent, weights)
+    block_out, tokens_grad, summed, first_total, second_total, *_ = backward(
         lay, capacity,
         (
-            got, got_grad, middle, second, gates, home, w_out, row(ln2_gain), router_wide, routes, cotangent,
-            unit, attended, log_total, first_norm, tokens, row(ln1_gain), w_qkv,
+            got, got_grad, middle, second, gates, home, w_out, vectors, router_wide, routes, cotangent,
+            unit, attended, log_total, first_norm, tokens, w_qkv, first_grad, second_grad, hop_a, hop_b,
         ),
     )
-    first_grad, second_grad = reduce_grads(n_dp, first_grad, second_grad)
-    total = lax.psum(grads, ("sp", "dp")).astype(F32)
-    vectors = total[width, : 4 * width].reshape(4, width)
+
+    def columns(first, count):
+        part = summed[first * width : (first + count) * width].reshape(count, width, WIDE)
+        return jnp.transpose(part, (1, 0, 2)).reshape(width, count * WIDE).astype(F32)
+
+    mixed = columns(width // WIDE, 1)
     return (
         block_out[None],
         tokens_grad[None],
-        vectors[0],
-        vectors[1],
-        total[:width, : 3 * width],
-        total[:width, 3 * width : 4 * width],
-        vectors[2],
-        vectors[3],
-        total[:width, 4 * width : 4 * width + experts],
-        first_grad[None],
-        second_grad[None],
+        mixed[:, HEAD_DIM],
+        mixed[:, HEAD_DIM + 1],
+        columns(8, 3 * PAIRS),
+        columns(0, PAIRS),
+        mixed[:, HEAD_DIM + 2],
+        mixed[:, HEAD_DIM + 3],
+        mixed[:, :experts],
+        first_total[None],
+        second_total[None],
     )
 
 

time: 655 us -> 560 us (0.85)
  waiting for transfers between devices: 58.6 us -> 0 us
  Pallas kernels: 549 us -> 511 us
  local copies, waits for them, and re-layouts: 21.6 us -> 37 us
  between operations: 14.5 us -> 0.93 us
    psum x1 -> x0, waiting for transfers between devices: 58.6 us -> none  [shards(): total = lax.psum(grads, ('sp', 'dp')).astype(F32)]
    pallas_call x1, Pallas kernels: 367 us -> 347 us  [layer(): pl.pallas_call(functools.partial(layer_kernel, lay, capacity, n_dp), out_...]
    pallas_call x2 -> x1, Pallas kernels: 182 us -> 164 us  [backward(): pl.pallas_call(functools.partial(back_kernel, lay, capacity, replicated),...]
    unnamed x21 -> x19, local copies, waits for them, and re-layouts: 8.5 us -> 19.6 us
    convert_element_type x0 -> x2, local copies, waits for them, and re-layouts: none -> 7.24 us  [columns(): jnp.transpose(part, (1, 0, 2)).reshape(width, count * WIDE).astype(F32)]
  transfers between devices with their start and end apart: 1 -> 0, of which waited for: 1 -> 0; matrix products, arithmetic and copies ran while one was open for 0% -> 0% of each run, Pallas kernels for 18% -> 0%
where the time goes in v3:
time: 560 us; the launch traced here: 551 us
  Pallas kernels  511 us (91%)
  local copies, waits for them, and re-layouts  37 us (7%)
    pallas_call x1, Pallas kernels, layer(): pl.pallas_call(functools.partial(layer_kernel, lay, capacity, n_dp), out_...  347 us
    pallas_call x1, Pallas kernels, backward(): pl.pallas_call(functools.partial(back_kernel, lay, capacity, replicated),...  164 us
    unnamed x19, local copies, waits for them, and re-layouts  19.6 us

profile of v3, /device:TPU:0, one launch (start us, length us, event | category | flops | bytes accessed | tf_op | source)
XLA Modules:
  0.0 550.7 jit_solution(12779600166433019047)
XLA Ops:
  0.6 0.7 stack.15
  1.3 0.7 stack.16
  2.0 0.7 stack.17
  2.7 0.7 stack.18
  4.0 0.8 copy.32
  4.9 0.7 copy.33.routes_t
  5.5 0.9 copy.31
  6.4 0.7 pad.4.w_router
  7.2 346.7 %layer.1 = (bf16[384,768]{1,0:T(8,128)(2,1)}, bf16[3,3072,128]{2,1,0:T(8,128)(2,1)}, f32[3072,128]{1,0:T(8,128)}, f32[3072,128]{1,0:T(8,128)}, bf16[384,768]{1,0...) custom-call(bf16[384,768]{1,0:T(8,128)(2,1)} %bitcast.40, ...), custom_call_target="tpu_custom_call" | custom-call | flops 49999998976 | bytes 104857600 | tf_op jit(solution)/shard_map/layer/pallas_call | solution.py:721
  353.9 164.4 %backward.1 = (bf16[384,768]{1,0:T(8,128)(2,1)}, f32[384,768]{1,0:T(8,128)}, bf16[19968,128]{1,0:T(8,128)(2,1)}, f32[768,768]{1,0:T(8,128)}, f32[768,768]{1,0:T(...) custom-call(bf16[1536,768]{1,0:T(8,128)(2,1)} %get-tuple-element.30., ...), custom_call_target="tpu_custom_call" | custom-call | flops 16000000000 | bytes 62914560 | tf_op jit(solution)/shard_map/backward/pallas_call | solution.py:1214
  518.3 1.0 slice_convert_fusion
  519.3 1.5 slice_reduce_fusion
  520.8 0.8 copy.38
  521.5 2.4 slice.28
  523.9 2.1 slice.27
  526.0 2.7 copy.35
  528.8 3.0 copy.37
  531.8 4.5 copy.34
  536.3 8.1 %copy.36 = f32[768,2304]{1,0:T(8,128)} copy(f32[768,2304]{0,1:T(8,128)} %bitcast.24) | data formatting | bytes 14155776
  544.4 0.8 copy.43
  545.3 1.0 copy.44
  546.5 1.4 copy.45
  547.9 1.1 copy-done
  549.0 1.4 copy.46
  (10 shorter events, 0.9 us)
Async XLA Ops:
  4.8 2.3 copy-start.3
  536.3 8.1 %copy-start.4 = (bf16[384,768]{1,0:T(8,128)(2,1)S(1)}, bf16[384,768]{1,0:T(8,128)(2,1)}, u32[]{:S(2)}) copy-start(bf16[384,768]{1,0:T(8,128)(2,1)} %get-tuple-element.44) | copy-start | bytes 1769476
  536.3 8.9 %copy-start.2 = (f32[384,768]{1,0:T(8,128)S(1)}, f32[384,768]{1,0:T(8,128)}, u32[]{:S(2)}) copy-start(f32[384,768]{1,0:T(8,128)} %get-tuple-element.45) | copy-start | bytes 3538948
  544.4 2.1 copy-start.1
  546.5 2.5 copy-start

commit v4 on v3

--- a/solution.py
+++ b/solution.py
@@ -243,12 +243,12 @@
             {"dp": other},
         )
 
-    def begin(self, arrays):
+    def begin(self, arrays, wanted):
         me = self.planes.me
         for array in arrays:
             for up in (True, False):
 
-                @pl.when(self.planes.takes(array < 2, up))
+                @pl.when(jnp.logical_and(wanted, self.planes.takes(array < 2, up)))
                 def _():
                     self.copy(array, me, up, self.own[array]).start()
 
@@ -260,9 +260,13 @@
             comes = jnp.logical_and(used, jnp.logical_and(index >= 0, index < n))
             yield comes, jnp.logical_and(comes, self.planes.takes(array < 2, up)), jnp.clip(index, 0, n - 1), up
 
-    def pass_on(self, arrays, distance):
+    def pass_on(self, arrays, distance, of_ends=None):
         for array in arrays:
             for comes, goes, index, up in self.pairs(array, distance):
+                if of_ends is not None:
+                    end = jnp.logical_or(index == 0, index == self.planes.n - 1)
+                    chosen = end if of_ends else jnp.logical_not(end)
+                    comes, goes = jnp.logical_and(comes, chosen), jnp.logical_and(goes, chosen)
 
                 @pl.when(comes)
                 def _():
@@ -332,7 +336,7 @@
     tokens, vectors, w_qkv, w_out, w_router, routes, routes_t, cotangent, own_a, own_b, own_c, own_d,
     first_norm, unit, attended, log_total, home, middle, second_norm, gates_out, got, got_grad, first_grad, second_grad,
     all_a, all_b, all_c, all_d, hop_a, hop_b,
-    staged_out, packed, packed_grad, rows_in, rows_grad, weight_a, weight_b, out_sum, in_sum, out_other, in_other, grad_a, grad_b,
+    staged_out, packed, packed_grad, rows_in, rows_grad, weight_a, weight_b, out_sum, in_sum, out_other, in_other, back_out, back_grad, grad_a, grad_b,
     packed_gates, rows_gates, send, recv, out_send, home_recv, local, stream_send, stream_recv, load,
     row_send, row_recv, row_local, back_send, back_recv, back_local, hop_send, hop_recv,
 ):
@@ -345,7 +349,8 @@
     stream = Weights(
         planes, (own_a, own_b, own_c, own_d), (all_a, all_b, all_c, all_d), stream_send, stream_recv
     )
-    stream.begin((2, 3))
+    stream.begin((0, 1), planes.outer)
+    stream.begin((2, 3), planes.inner)
 
     hat, _ = normed(tokens[...].astype(F32))
     first_norm[...] = (hat * gain_one[...] + shift_one[...]).astype(BF16)
@@ -469,8 +474,9 @@
     wait_home(lay, is_short, staged_out, out_send, 1, True)
     wait_home(lay, is_short, staged_out, home_recv, 1, False)
 
-    stream.begin((0, 1))
-    stream.pass_on((2, 3), 1)
+    stream.begin((0, 1), planes.inner)
+    stream.pass_on((2, 3), 1, False)
+    stream.pass_on((0, 1), 1, True)
     x1 = tokens[...].astype(F32) + dot(home[...], w_out[...])
     middle[...] = x1
     hat, _ = normed(x1)
@@ -511,6 +517,8 @@
     for which in (1, 0, 2):
         for kind in range(2):
             each(dispatch_copies(which, kind), end)
+    stream.begin((2, 3), planes.outer)
+    stream.pass_on((0, 1), 1, False)
 
     def take(area):
         for which in (1, 0, 2):
@@ -534,8 +542,32 @@
 
         lax.fori_loop(0, rows // ROWS, one, 0)
 
+    def weight_grads(index):
+        stores = [
+            pltpu.make_async_copy(stage, whole.at[index], load.at[2 + i])
+            for i, (stage, whole) in enumerate(((grad_a, first_grad), (grad_b, second_grad)))
+        ]
+        tall = 3 * WIDE
+        for total in (span, 2 * span):
+
+            @pl.when(planes.hosts == (total > span))
+            def _():
+                every_row = pl.ds(0, total)
+                for col in range(0, width, tall):
+                    part = pl.ds(col, tall)
+                    grad_a[part] = t_dot(rows_in[every_row, part], packed_grad[every_row, :hidden]).astype(BF16)
+                for col in range(0, hidden, tall):
+                    part = pl.ds(col, tall)
+                    grad_b[part] = t_dot(packed[every_row, part], rows_grad[every_row]).astype(BF16)
+
+        for copy in stores:
+            copy.start()
+        for copy in stores:
+            copy.wait()
+
     def work(trained, sums, first_row, rows, nearest, farthest):
         arrays = (0, 1) if trained else (2, 3)
+        last = jnp.maximum(planes.me, n_dp - 1 - planes.me)
         every = (all_a, all_b) if trained else (all_c, all_d)
         own = (own_a, own_b) if trained else (own_c, own_d)
 
@@ -544,7 +576,13 @@
             index = jnp.where(side == 0, planes.me - distance, planes.me + distance)
             real = jnp.logical_and(jnp.logical_and(index >= 0, index < n_dp), jnp.logical_or(side == 0, distance > 0))
 
-            @pl.when(jnp.logical_and(side == 0, distance >= (2 if trained else 3)))
+            if trained:
+
+                @pl.when(jnp.logical_and(side == 1, distance == 1))
+                def _():
+                    stream.pass_on((2, 3), 1, True)
+
+            @pl.when(jnp.logical_and(side == 0, distance >= 3))
             def _():
                 stream.pass_on(arrays, distance)
 
@@ -581,26 +619,10 @@
 
                 lax.fori_loop(0, rows // ROWS, chunk, 0)
                 if trained:
-                    stores = [
-                        pltpu.make_async_copy(stage, whole.at[index], load.at[2 + i])
-                        for i, (stage, whole) in enumerate(((grad_a, first_grad), (grad_b, second_grad)))
-                    ]
-                    for total in (span, 2 * span):
-
-                        @pl.when(planes.hosts == (total > span))
-                        def _():
-                            every_row = pl.ds(0, total)
-                            for col in range(0, width, WIDE):
-                                cut = pl.ds(col, WIDE)
-                                grad_a[cut] = t_dot(rows_in[every_row, cut], packed_grad[every_row, :hidden]).astype(BF16)
-                            for col in range(0, hidden, WIDE):
-                                cut = pl.ds(col, WIDE)
-                                grad_b[cut] = t_dot(packed[every_row, cut], rows_grad[every_row]).astype(BF16)
-
-                    for copy in stores:
-                        copy.start()
-                    for copy in stores:
-                        copy.wait()
+
+                    @pl.when(distance < last)
+                    def _():
+                        weight_grads(index)
 
             return carry
 
@@ -610,16 +632,17 @@
         def one(number, carry):
             part = pl.ds(pl.multiple_of(base + number * ROWS, ROWS), ROWS)
             here = pl.ds(pl.multiple_of(first_row + number * ROWS, ROWS), ROWS)
-            rows_in[here] = sums[0][part].astype(BF16)
-            rows_grad[here] = sums[1][part].astype(BF16)
+            back_out[here] = sums[0][part].astype(BF16)
+            back_grad[here] = sums[1][part].astype(BF16)
             return carry
 
         lax.fori_loop(0, rows // ROWS, one, 0)
 
-    def back_copies(kind, guest):
+    def back_copies(kind, guest, whiches=(0, 1)):
         area = 2 if kind else int(guest)
         plane = planes.guest if guest else planes.me
-        for which, (source, target) in enumerate(((rows_in, got), (rows_grad, got_grad))):
+        for which in whiches:
+            source, target = ((back_out, got), (back_grad, got_grad))[which]
             into = target.at[pl.ds(pl.multiple_of((me * 2 + kind) * capacity, 16), capacity)]
             for step in range(n):
                 to = lax.rem(me + step, n)
@@ -648,39 +671,42 @@
     train_rows = jnp.where(planes.hosts, 2 * span, span)
     clear(frozen_sums, span)
 
+    clear(train_sums, train_rows)
+
     @pl.when(planes.inner)
     def _():
-        clear(train_sums, train_rows)
         take(0)
 
         @pl.when(planes.hosts)
         def _():
             take(1)
 
-        work(True, train_sums, 0, train_rows, 0, 0)
-        stream.pass_on((0, 1), 1)
-        work(True, train_sums, 0, train_rows, 1, 1)
+        work(True, train_sums, 0, train_rows, 0, 1)
+        stream.pass_on((0, 1), 2)
+        work(True, train_sums, 0, train_rows, 2, n_dp - 1)
+
+        @pl.when(planes.hosts)
+        def _():
+            turn(train_sums, span, span, span)
+            each(back_copies(0, True, (0,)), start)
+
+        turn(train_sums, 0, 0, span)
+        each(back_copies(0, False), start)
+        weight_grads(jnp.where(planes.me > n_dp - 1 - planes.me, 0, n_dp - 1))
 
     take(2)
     work(False, frozen_sums, 2 * span, span, 0, 1)
     stream.pass_on((2, 3), 2)
+
+    hops(start)
+
+    @pl.when(planes.hosts)
+    def _():
+        each(back_copies(0, True, (1,)), start)
+
     work(False, frozen_sums, 2 * span, span, 2, n_dp - 1)
     turn(frozen_sums, 2 * span, 0, span)
     each(back_copies(1, False), start)
-
-    @pl.when(planes.inner)
-    def _():
-        work(True, train_sums, 0, train_rows, 2, n_dp - 1)
-
-        @pl.when(planes.hosts)
-        def _():
-            turn(train_sums, span, span, span)
-            each(back_copies(0, True), start)
-
-        turn(train_sums, 0, 0, span)
-        each(back_copies(0, False), start)
-        hops(start)
-
     each(back_copies(1, False), end)
 
     @pl.when(planes.inner)
@@ -751,6 +777,8 @@
             pltpu.VMEM((2 * span, width), F32),
             pltpu.VMEM((span, width), F32),
             pltpu.VMEM((span, width), F32),
+            pltpu.VMEM((3 * span, width), BF16),
+            pltpu.VMEM((3 * span, width), BF16),
             pltpu.VMEM((width, hidden), BF16),
             pltpu.VMEM((hidden, width), BF16),
             pltpu.VMEM((2 * n, 8, 128), F32),
@@ -897,12 +925,11 @@
     return found
 
 
-def run_sum(total, ready=lambda piece: None, done=lambda piece: None):
-    count = len(total.pieces)
-    for tick in range(total.steps + count):
-        for piece in range(count):
-            step = tick - piece
-            if step > 0 and step <= total.steps:
+def run_sum(total, ahead, ready, done):
+    begun = [ahead] + [1 - piece for piece in range(1, len(total.pieces))]
+    while any(step <= total.steps for step in begun):
+        for piece, step in enumerate(begun):
+            if 0 < step <= total.steps:
                 total.add(piece, step - 1)
                 if step == total.steps:
                     done(piece)
@@ -910,6 +937,7 @@
                 ready(piece)
             if 0 <= step < total.steps:
                 total.start(piece, step)
+            begun[piece] += 1
 
 
 class Gather:
@@ -998,22 +1026,21 @@
             def _():
                 self.fetch(self.came(array, self.me, up), self.sums[array].at[int(up)], 1).wait()
 
-        size = out.shape[0] // 6
-        lanes = pl.ds(0, out.shape[1])
+        rows, lanes = out.shape
         stores = []
-        for number in range(6):
-            part = pl.ds(number * size, size)
-            stage = self.stage.at[number % 2, pl.ds(0, size), lanes]
+        for number in range(lanes // WIDE):
+            part = pl.ds(number * WIDE, WIDE)
+            stage = self.stage.at[number % 2, pl.ds(0, rows), pl.ds(0, WIDE)]
             if number >= 2:
                 stores[number - 2].wait()
-            stage[...] = theirs[part].astype(F32)
+            stage[...] = theirs[:, part].astype(F32)
             for up, comes in sides:
 
                 @pl.when(comes)
                 def _():
-                    stage[...] += self.sums[array][int(up), part].astype(F32)
-
-            stores.append(pltpu.make_async_copy(stage, out.at[part], self.load.at[3 + number % 2]))
+                    stage[...] += self.sums[array][int(up), :, part].astype(F32)
+
+            stores.append(pltpu.make_async_copy(stage, out.at[:, part], self.load.at[3 + number % 2]))
             stores[number].start()
         for store in stores[-2:]:
             store.wait()
@@ -1024,7 +1051,6 @@
     return [
         *(pltpu.VMEM(shape, BF16) for shape in shapes),
         *(pltpu.VMEM((2, *shape), BF16) for shape in shapes),
-        pltpu.VMEM((2, 128, max(map(max, shapes))), F32),
         DMA((2, 2, n)),
         DMA((2, 2, n)),
         DMA((5,)),
@@ -1035,10 +1061,10 @@
     lay, capacity, replicated,
     got, got_grad, middle, second_norm, gates, home_out, w_out, vectors, w_router, routes, cotangent,
     unit, attended, log_total, first_norm, tokens, w_qkv, first_own, second_own, hop_a, hop_b,
-    block_out, tokens_grad, summed, first_total, second_total, below_a, below_b, above_a, above_b,
+    block_out, tokens_grad, qkv_grad, out_proj_grad, router_out, vectors_out, first_total, second_total, below_a, below_b, above_a, above_b,
     grad_attended, grad_out, deltas, query_sum, staged, home, send, recv, out_send, home_recv, local,
-    theirs_a, theirs_b, sums_a, sums_b, stage, pass_send, pass_recv, load,
-    grads, landed, sum_send, sum_recv,
+    theirs_a, theirs_b, sums_a, sums_b, pass_send, pass_recv, load,
+    grads, landed, summed, stage, sum_send, sum_recv,
 ):
     n_dp = first_own.shape[0]
     gather = Gather(
@@ -1092,6 +1118,9 @@
             grads[pl.ds((column + lane) // WIDE * width, width)] = value[:, lane : lane + WIDE].astype(BF16)
 
     put(0, out_proj)
+    early = 4 if replicated.pieces[0][1] <= width // WIDE * width else 0
+    if early:
+        replicated.start(0, 0)
     started = to_owners(
         lay,
         me,
@@ -1165,6 +1194,13 @@
                 lay, me, is_short, seq, first_pair, base, block, start, staged.at[kind], home, kind * PAIRS * WIDE,
                 out_send.at[kind], home_recv.at[kind], local,
             )
+        for step in range(1, early):
+
+            @pl.when(index == 2 * step)
+            def _():
+                replicated.add(0, step - 1)
+                replicated.start(0, step)
+
         return carry
 
     lax.fori_loop(0, lay.tasks(is_short), task, 0)
@@ -1176,14 +1212,13 @@
     shift_one_grad = jnp.sum(grad_first, axis=0, keepdims=True)
     tokens_grad[...] += norm_back(grad_first, gain_one[...], hat, scale)
     parts = (gain_one_grad, shift_one_grad, gain_two_grad, shift_two_grad)
-    row = lax.broadcasted_iota(jnp.int32, (8, width), 0)
-    stack = sum(jnp.where(row == i, part, 0.0) for i, part in enumerate(parts)).astype(BF16)
-    lane = lax.broadcasted_iota(jnp.int32, (8, WIDE), 1)
-    spot = hot(lane == HEAD_DIM + lax.broadcasted_iota(jnp.int32, (8, WIDE), 0))
-    grads[pl.ds(width // WIDE * width, width)] = (router_grad + t_dot(stack, spot)).astype(BF16)
+    grads[pl.ds(width // WIDE * width, width)] = router_grad.astype(BF16)
+    rows = [part[:, lane : lane + WIDE] for part in parts for lane in range(0, width, WIDE)]
+    rows.append(jnp.zeros((width - len(rows), WIDE), F32))
+    grads[pl.ds(7 * width, width)] = jnp.concatenate(rows, axis=0).astype(BF16)
     first = 8
     last = first + 3 * PAIRS
-    for spare in [7, *range(last, replicated.rows // width)]:
+    for spare in range(last, replicated.rows // width):
         grads[pl.ds(spare * width, width)] = jnp.zeros((width, WIDE), BF16)
 
     def ready(piece):
@@ -1193,7 +1228,30 @@
                 lanes = pl.ds((column - first) * WIDE, 2 * WIDE)
                 put(column * WIDE, t_dot(first_norm[...], home[:, lanes]))
 
-    run_sum(replicated, ready)
+    stores = []
+
+    def done(piece):
+        start, rows = replicated.pieces[piece]
+        for column in range(start // width, (start + rows) // width, 2):
+            blocks = [summed.at[pl.ds((column + i) * width, width)] for i in range(2)]
+            if column == 6:
+                router_out[...] = blocks[0][...].astype(F32)
+                vectors_out[...] = blocks[1][0:32].astype(F32)
+            elif column < last:
+                number = len(stores)
+                if number >= 2:
+                    stores[number - 2].wait()
+                for i in range(2):
+                    stage[number % 2, :, i * WIDE : (i + 1) * WIDE] = blocks[i][...].astype(F32)
+                target, lane = (out_proj_grad, column * WIDE) if column < 6 else (qkv_grad, (column - first) * WIDE)
+                stores.append(
+                    pltpu.make_async_copy(stage.at[number % 2], target.at[:, pl.ds(lane, 2 * WIDE)], load.at[3 + number % 2])
+                )
+                stores[number].start()
+
+    run_sum(replicated, early, ready, done)
+    for store in stores[-2:]:
+        store.wait()
     for array, out in enumerate((first_total, second_total)):
         for up, index in inside:
             gather.pass_on(array, index, up)
@@ -1214,11 +1272,12 @@
     return pl.pallas_call(
         functools.partial(back_kernel, lay, capacity, replicated),
         out_shape=(
-            shape((count, width), BF16), shape((count, width), F32), shape((replicated.rows, WIDE), BF16),
+            shape((count, width), BF16), shape((count, width), F32),
+            shape((width, 3 * width), F32), shape((width, width), F32), shape((width, WIDE), F32), shape((32, WIDE), F32),
             *(shape(g.shape[1:], F32) for g in slices), *(shape(g.shape, BF16) for g in slices * 2),
         ),
         in_specs=[VMEM] * 12 + [ANY] + [VMEM] * 4 + [ANY] * 4,
-        out_specs=[VMEM] * 3 + [ANY] * 6,
+        out_specs=[VMEM] * 2 + [ANY] * 2 + [VMEM] * 2 + [ANY] * 6,
         scratch_shapes=[
             pltpu.VMEM((count, width), BF16),
             pltpu.VMEM((UNIT, WIDE), BF16),
@@ -1234,6 +1293,8 @@
             *gather_scratch(slices[0].shape[0], *slices),
             pltpu.VMEM((replicated.rows, WIDE), BF16),
             pltpu.VMEM((replicated.landing()[1], WIDE), BF16),
+            pltpu.VMEM((replicated.rows, WIDE), BF16),
+            pltpu.VMEM((2, width, 2 * WIDE), F32),
             DMA((len(replicated.pieces), replicated.steps, slices[0].shape[0])),
             DMA((len(replicated.pieces), replicated.steps, slices[0].shape[0])),
         ],
@@ -1260,29 +1321,24 @@
         first_norm, unit, attended, log_total, home, middle, second, gates, got, got_grad, first_grad, second_grad,
         _, _, _, _, hop_a, hop_b,
     ) = layer(lay, capacity, n_dp, tokens, vectors, w_qkv, w_out, router_wide, routes, cotangent, weights)
-    block_out, tokens_grad, summed, first_total, second_total, *_ = backward(
+    block_out, tokens_grad, qkv_grad, out_proj, router, vector_rows, first_total, second_total, *_ = backward(
         lay, capacity,
         (
             got, got_grad, middle, second, gates, home, w_out, vectors, router_wide, routes, cotangent,
             unit, attended, log_total, first_norm, tokens, w_qkv, first_grad, second_grad, hop_a, hop_b,
         ),
     )
-
-    def columns(first, count):
-        part = summed[first * width : (first + count) * width].reshape(count, width, WIDE)
-        return jnp.transpose(part, (1, 0, 2)).reshape(width, count * WIDE).astype(F32)
-
-    mixed = columns(width // WIDE, 1)
+    found = vector_rows[: 4 * width // WIDE].reshape(4, width)
     return (
         block_out[None],
         tokens_grad[None],
-        mixed[:, HEAD_DIM],
-        mixed[:, HEAD_DIM + 1],
-        columns(8, 3 * PAIRS),
-        columns(0, PAIRS),
-        mixed[:, HEAD_DIM + 2],
-        mixed[:, HEAD_DIM + 3],
-        mixed[:, :experts],
+        found[0],
+        found[1],
+        qkv_grad,
+        out_proj,
+        found[2],
+        found[3],
+        router[:, :experts],
         first_total[None],
         second_total[None],
     )

time: 560 us -> 521 us (0.930)
  the two profiles are of different devices: /device:TPU:0 before, /device:TPU:19 now
where the time goes in v4:
time: 521 us; the launch traced here: 512 us
  Pallas kernels  486 us (93%)
  local copies, waits for them, and re-layouts  25 us (5%)
    pallas_call x1, Pallas kernels, layer(): pl.pallas_call(functools.partial(layer_kernel, lay, capacity, n_dp), out_...  300 us
    pallas_call x1, Pallas kernels, backward(): pl.pallas_call(functools.partial(back_kernel, lay, capacity, replicated),...  186 us
    unnamed x19, local copies, waits for them, and re-layouts  19.4 us

profile of v4, /device:TPU:19, one launch (start us, length us, event | category | flops | bytes accessed | tf_op | source)
XLA Modules:
  0.0 512.5 jit_solution(1971162313541530714)
XLA Ops:
  0.6 0.7 stack.15
  1.3 0.7 stack.16
  2.0 0.7 stack.17
  2.7 0.7 stack.18
  3.4 0.6 pad_maximum_fusion.vectors
  4.0 0.8 copy.26
  4.8 0.0 copy-start.4
  4.9 0.7 copy.27.routes_t
  5.5 0.9 copy.25
  6.4 0.7 pad.4.w_router
  7.2 0.0 copy-done.4
  7.2 300.2 %layer.1 = (bf16[384,768]{1,0:T(8,128)(2,1)}, bf16[3,3072,128]{2,1,0:T(8,128)(2,1)}, f32[3072,128]{1,0:T(8,128)}, f32[3072,128]{1,0:T(8,128)}, bf16[384,768]{1,0...) custom-call(bf16[384,768]{1,0:T(8,128)(2,1)} %bitcast.34, ...), custom_call_target="tpu_custom_call" | custom-call | flops 49999998976 | bytes 104857600 | tf_op jit(solution)/shard_map/layer/pallas_call | solution.py:747
  307.4 185.5 %backward.1 = (bf16[384,768]{1,0:T(8,128)(2,1)}, f32[384,768]{1,0:T(8,128)}, f32[768,2304]{1,0:T(8,128)}, f32[768,768]{1,0:T(8,128)}, f32[768,128]{1,0:T(8,128)}...) custom-call(bf16[1536,768]{1,0:T(8,128)(2,1)} %get-tuple-element.33., ...), custom_call_target="tpu_custom_call" | custom-call | flops 16000000000 | bytes 62914560 | tf_op jit(solution)/shard_map/backward/pallas_call | solution.py:1272
  493.0 1.4 slice_bitcast_fusion
  494.4 1.8 copy.28
  496.1 1.9 copy.35
  498.1 0.0 copy-done.3
  498.1 1.0 copy.36
  499.1 6.6 %copy.37 = f32[768,2304]{1,0:T(8,128)} copy(f32[768,2304]{1,0:T(8,128)} %get-tuple-element.85) | data formatting | bytes 14155776
  505.6 1.4 copy.38
  507.1 1.1 copy-done.1
  508.2 1.4 copy.39
  509.6 1.1 copy-done
  510.7 1.4 copy.40
  (5 shorter events, 0.0 us)
Async XLA Ops:
  4.8 2.3 copy-start.4
  492.9 5.1 copy-start.3
  499.1 6.6 %copy-start.2 = (f32[768,768]{1,0:T(8,128)S(1)}, f32[768,768]{1,0:T(8,128)}, u32[]{:S(2)}) copy-start(f32[768,768]{1,0:T(8,128)} %get-tuple-element.86) | copy-start | bytes 7077892
  505.6 2.5 copy-start.1
  508.2 2.5 copy-start

commit v5 on v4

--- a/solution.py
+++ b/solution.py
@@ -349,8 +349,7 @@
     stream = Weights(
         planes, (own_a, own_b, own_c, own_d), (all_a, all_b, all_c, all_d), stream_send, stream_recv
     )
-    stream.begin((0, 1), planes.outer)
-    stream.begin((2, 3), planes.inner)
+    stream.begin((2, 3), True)
 
     hat, _ = normed(tokens[...].astype(F32))
     first_norm[...] = (hat * gain_one[...] + shift_one[...]).astype(BF16)
@@ -474,9 +473,8 @@
     wait_home(lay, is_short, staged_out, out_send, 1, True)
     wait_home(lay, is_short, staged_out, home_recv, 1, False)
 
+    stream.pass_on((2, 3), 1)
     stream.begin((0, 1), planes.inner)
-    stream.pass_on((2, 3), 1, False)
-    stream.pass_on((0, 1), 1, True)
     x1 = tokens[...].astype(F32) + dot(home[...], w_out[...])
     middle[...] = x1
     hat, _ = normed(x1)
@@ -517,8 +515,8 @@
     for which in (1, 0, 2):
         for kind in range(2):
             each(dispatch_copies(which, kind), end)
-    stream.begin((2, 3), planes.outer)
-    stream.pass_on((0, 1), 1, False)
+    stream.begin((0, 1), planes.outer)
+    stream.pass_on((2, 3), 2)
 
     def take(area):
         for which in (1, 0, 2):
@@ -541,6 +539,8 @@
             return carry
 
         lax.fori_loop(0, rows // ROWS, one, 0)
+
+    last = jnp.maximum(planes.me, n_dp - 1 - planes.me)
 
     def weight_grads(index):
         stores = [
@@ -565,9 +565,8 @@
         for copy in stores:
             copy.wait()
 
-    def work(trained, sums, first_row, rows, nearest, farthest):
+    def work(trained, sums, first_row, base, rows, nearest, farthest, passing=True):
         arrays = (0, 1) if trained else (2, 3)
-        last = jnp.maximum(planes.me, n_dp - 1 - planes.me)
         every = (all_a, all_b) if trained else (all_c, all_d)
         own = (own_a, own_b) if trained else (own_c, own_d)
 
@@ -576,13 +575,7 @@
             index = jnp.where(side == 0, planes.me - distance, planes.me + distance)
             real = jnp.logical_and(jnp.logical_and(index >= 0, index < n_dp), jnp.logical_or(side == 0, distance > 0))
 
-            if trained:
-
-                @pl.when(jnp.logical_and(side == 1, distance == 1))
-                def _():
-                    stream.pass_on((2, 3), 1, True)
-
-            @pl.when(jnp.logical_and(side == 0, distance >= 3))
+            @pl.when(jnp.logical_and(passing, jnp.logical_and(side == 0, distance >= 3)))
             def _():
                 stream.pass_on(arrays, distance)
 
@@ -605,7 +598,7 @@
                     copy.wait()
 
                 def chunk(number, carry):
-                    part = pl.ds(pl.multiple_of(number * ROWS, ROWS), ROWS)
+                    part = pl.ds(pl.multiple_of(base + number * ROWS, ROWS), ROWS)
                     here = pl.ds(pl.multiple_of(first_row + number * ROWS, ROWS), ROWS)
                     active, slope = gelu_parts(dot(rows_in[here], weight_a[...]))
                     active = active.astype(BF16)
@@ -662,7 +655,7 @@
                 def _():
                     act(
                         remote(
-                            whole.at[n_dp - 1 if up else 0], hop.at[int(up)], hop_send.at[int(up), array],
+                            whole.at[2 if up else n_dp - 3], hop.at[int(up)], hop_send.at[int(up), array],
                             hop_recv.at[int(up), array], {"dp": planes.me + (1 if up else -1)},
                         )
                     )
@@ -681,32 +674,34 @@
         def _():
             take(1)
 
-        work(True, train_sums, 0, train_rows, 0, 1)
+        work(True, train_sums, 0, 0, train_rows, 0, 0)
+
+    take(2)
+    work(False, frozen_sums, 2 * span, 0, span, 0, 1)
+    stream.pass_on((0, 1), 1, True)
+    work(False, frozen_sums, 2 * span, 0, span, 2, n_dp - 1)
+    turn(frozen_sums, 2 * span, 0, span)
+    each(back_copies(1, False), start)
+
+    @pl.when(planes.inner)
+    def _():
+        stream.pass_on((0, 1), 1, False)
+        work(True, train_sums, 0, 0, train_rows, 1, 1)
         stream.pass_on((0, 1), 2)
-        work(True, train_sums, 0, train_rows, 2, n_dp - 1)
+        hops(start)
+        work(True, train_sums, 0, 0, train_rows, 2, last - 1)
 
         @pl.when(planes.hosts)
         def _():
+            work(True, train_sums, span, span, span, last, last)
             turn(train_sums, span, span, span)
-            each(back_copies(0, True, (0,)), start)
-
+            each(back_copies(0, True), start)
+
+        work(True, train_sums, 0, 0, span, last, last, jnp.logical_not(planes.hosts))
         turn(train_sums, 0, 0, span)
         each(back_copies(0, False), start)
         weight_grads(jnp.where(planes.me > n_dp - 1 - planes.me, 0, n_dp - 1))
 
-    take(2)
-    work(False, frozen_sums, 2 * span, span, 0, 1)
-    stream.pass_on((2, 3), 2)
-
-    hops(start)
-
-    @pl.when(planes.hosts)
-    def _():
-        each(back_copies(0, True, (1,)), start)
-
-    work(False, frozen_sums, 2 * span, span, 2, n_dp - 1)
-    turn(frozen_sums, 2 * span, 0, span)
-    each(back_copies(1, False), start)
     each(back_copies(1, False), end)
 
     @pl.when(planes.inner)
@@ -809,14 +804,17 @@
 
 
 class Sum:
-    def __init__(self, n_sp, n_dp, pieces, quantum, needed):
+    def __init__(self, n_sp, n_dp, pieces, quantum, needed, first):
         self.n_sp, self.n_dp = n_sp, n_dp
         self.bits = n_sp.bit_length() - 1
         unit = math.lcm(16 * n_sp * n_dp, quantum)
         units = -(-needed // unit)
-        pieces = min(pieces, units)
-        sizes = [units // pieces + (p < units % pieces) for p in range(pieces)]
+        sizes = [first // unit] if first >= unit else []
+        left = units - sum(sizes)
+        pieces = min(pieces, left)
+        sizes += [left // pieces + (p < left % pieces) for p in range(pieces)]
         self.pieces = [(unit * sum(sizes[:p]), unit * size) for p, size in enumerate(sizes)]
+        self.early = first >= unit
         self.rows = unit * units
         self.steps = 2 * self.bits + 2
 
@@ -925,8 +923,10 @@
     return found
 
 
-def run_sum(total, ahead, ready, done):
-    begun = [ahead] + [1 - piece for piece in range(1, len(total.pieces))]
+def run_sum(total, ahead, ready, done, between):
+    begun = [-(piece // 2) for piece in range(len(total.pieces) - total.early)]
+    begun = [ahead] * total.early + begun
+    rounds = 0
     while any(step <= total.steps for step in begun):
         for piece, step in enumerate(begun):
             if 0 < step <= total.steps:
@@ -938,6 +938,8 @@
             if 0 <= step < total.steps:
                 total.start(piece, step)
             begun[piece] += 1
+        between(rounds)
+        rounds += 1
 
 
 class Gather:
@@ -966,11 +968,12 @@
         return self.me == 1 if up else self.me == self.n - 2
 
     def hopped(self, index, up):
-        if index not in (0, self.n - 1):
-            return False
-        return self.me == 2 if up else self.me == self.n - 3
+        return index == (2 if up else self.n - 3)
 
     def begin(self, array, index, up):
+        if self.hopped(index, up):
+            return
+
         @pl.when(jnp.logical_and(self.wanted(index, up), self.begins(up)))
         def _():
             self.copy(array, index, up, self.own[array].at[index]).start()
@@ -985,23 +988,14 @@
         def _():
             total, theirs = self.sums[array].at[int(up)], self.theirs[array]
             here = self.fetch(self.own[array].at[index], total, 0)
-            hopped = self.hopped(index, up)
-
-            @pl.when(hopped)
-            def _():
-                self.fetch(self.hop[array].at[int(up)], theirs, 1).wait()
-
-            @pl.when(jnp.logical_not(hopped))
-            def _():
-                self.fetch(self.came(array, index, up), theirs, 1).wait()
-
+            self.fetch(self.came(array, index, up), theirs, 1).wait()
             here.wait()
             total[...] = (total[...].astype(F32) + theirs[...].astype(F32)).astype(BF16)
             self.copy(array, index, up, total).start()
 
     def finish(self, array, index, up):
         waits = self.wanted(index, up)
-        if index in (0, self.n - 1):
+        if self.hopped(index, up):
             waits = jnp.logical_and(waits, jnp.logical_not(self.begins(up)))
 
         @pl.when(waits)
@@ -1022,7 +1016,13 @@
         sides = ((True, self.me >= 2), (False, self.me <= self.n - 3))
         for up, comes in sides:
 
-            @pl.when(comes)
+            near = self.me == (2 if up else self.n - 3)
+
+            @pl.when(jnp.logical_and(comes, near))
+            def _():
+                self.fetch(self.hop[array].at[int(up)], self.sums[array].at[int(up)], 1).wait()
+
+            @pl.when(jnp.logical_and(comes, jnp.logical_not(near)))
             def _():
                 self.fetch(self.came(array, self.me, up), self.sums[array].at[int(up)], 1).wait()
 
@@ -1064,7 +1064,7 @@
     block_out, tokens_grad, qkv_grad, out_proj_grad, router_out, vectors_out, first_total, second_total, below_a, below_b, above_a, above_b,
     grad_attended, grad_out, deltas, query_sum, staged, home, send, recv, out_send, home_recv, local,
     theirs_a, theirs_b, sums_a, sums_b, pass_send, pass_recv, load,
-    grads, landed, summed, stage, sum_send, sum_recv,
+    grads, landed, summed, stage, sum_send, sum_recv, out_sems,
 ):
     n_dp = first_own.shape[0]
     gather = Gather(
@@ -1081,9 +1081,8 @@
     kept.start()
     inside = [(up, index) for index in range(1, n_dp - 1) for up in (True, False)]
     ends = [(True, n_dp - 1), (False, 0)]
-    for array in range(2):
-        for up, index in inside:
-            gather.begin(array, index, up)
+    for up, index in ends:
+        gather.begin(0, index, up)
     place, matches = slot_columns(lay, capacity, routes[...])
     slots = lax.broadcasted_iota(jnp.int32, (tokens.shape[0], got.shape[0]), 1)
     chosen = [hot(slots == place[c]) for c in range(2)]
@@ -1118,8 +1117,8 @@
             grads[pl.ds((column + lane) // WIDE * width, width)] = value[:, lane : lane + WIDE].astype(BF16)
 
     put(0, out_proj)
-    early = 4 if replicated.pieces[0][1] <= width // WIDE * width else 0
-    if early:
+    moments = (1, 2, 3, 5, 7)
+    if replicated.early:
         replicated.start(0, 0)
     started = to_owners(
         lay,
@@ -1133,9 +1132,8 @@
         local,
         range(PAIRS),
     )
-    for array in range(2):
-        for up, index in ends:
-            gather.pass_on(array, index, up)
+    for up, index in ends:
+        gather.begin(1, index, up)
     query_sum[...] = jnp.zeros_like(query_sum)
     keep = lanes_first()
     lower = causal(BLOCK)
@@ -1194,16 +1192,26 @@
                 lay, me, is_short, seq, first_pair, base, block, start, staged.at[kind], home, kind * PAIRS * WIDE,
                 out_send.at[kind], home_recv.at[kind], local,
             )
-        for step in range(1, early):
-
-            @pl.when(index == 2 * step)
+        @pl.when(index == 1)
+        def _():
+            for up, which in ends:
+                gather.pass_on(0, which, up)
+
+        for step, moment in enumerate(moments if replicated.early else ()):
+
+            @pl.when(index == moment)
             def _():
-                replicated.add(0, step - 1)
-                replicated.start(0, step)
+                replicated.add(0, step)
+                replicated.start(0, step + 1)
 
         return carry
 
     lax.fori_loop(0, lay.tasks(is_short), task, 0)
+    for up, index in ends:
+        gather.pass_on(1, index, up)
+    for array in range(2):
+        for up, index in inside:
+            gather.begin(array, index, up)
     for kind in range(3):
         wait_home(lay, is_short, staged.at[kind], home_recv.at[kind], 1, False)
     grad_first = dot_t(home[...], w_qkv[...])
@@ -1233,31 +1241,29 @@
     def done(piece):
         start, rows = replicated.pieces[piece]
         for column in range(start // width, (start + rows) // width, 2):
-            blocks = [summed.at[pl.ds((column + i) * width, width)] for i in range(2)]
+            parts = [summed.at[pl.ds((column + i) * width, width)] for i in range(2)]
             if column == 6:
-                router_out[...] = blocks[0][...].astype(F32)
-                vectors_out[...] = blocks[1][0:32].astype(F32)
+                router_out[...] = parts[0][...].astype(F32)
+                vectors_out[...] = parts[1][0:32].astype(F32)
             elif column < last:
-                number = len(stores)
-                if number >= 2:
-                    stores[number - 2].wait()
                 for i in range(2):
-                    stage[number % 2, :, i * WIDE : (i + 1) * WIDE] = blocks[i][...].astype(F32)
-                target, lane = (out_proj_grad, column * WIDE) if column < 6 else (qkv_grad, (column - first) * WIDE)
-                stores.append(
-                    pltpu.make_async_copy(stage.at[number % 2], target.at[:, pl.ds(lane, 2 * WIDE)], load.at[3 + number % 2])
-                )
-                stores[number].start()
-
-    run_sum(replicated, early, ready, done)
-    for store in stores[-2:]:
+                    target, lane = (out_proj_grad, column) if column < 6 else (qkv_grad, column - first)
+                    lanes = pl.ds((lane + i) * WIDE, WIDE)
+                    stores.append(pltpu.make_async_copy(parts[i], target.at[:, lanes], out_sems.at[len(stores)]))
+                    stores[-1].start()
+
+    def between(number):
+        if number in (5, 6):
+            array = number - 5
+            for up, index in inside:
+                gather.pass_on(array, index, up)
+            for up, index in inside + ends:
+                gather.finish(array, index, up)
+            gather.total(array, (first_total, second_total)[array])
+
+    run_sum(replicated, len(moments) + 1, ready, done, between)
+    for store in stores:
         store.wait()
-    for array, out in enumerate((first_total, second_total)):
-        for up, index in inside:
-            gather.pass_on(array, index, up)
-        for up, index in inside + ends:
-            gather.finish(array, index, up)
-        gather.total(array, out)
     finish_sends(me, started)
     for kind in range(3):
         wait_home(lay, is_short, staged.at[kind], out_send.at[kind], 1, True)
@@ -1268,12 +1274,12 @@
     owners = len(lay.owners())
     shape = jax.ShapeDtypeStruct
     slices = values[-4:-2]
-    replicated = Sum(lay.n, slices[0].shape[0], 6, 2 * width, 26 * width)
+    replicated = Sum(lay.n, slices[0].shape[0], 6, 2 * width, 26 * width, width // WIDE * width)
     return pl.pallas_call(
         functools.partial(back_kernel, lay, capacity, replicated),
         out_shape=(
             shape((count, width), BF16), shape((count, width), F32),
-            shape((width, 3 * width), F32), shape((width, width), F32), shape((width, WIDE), F32), shape((32, WIDE), F32),
+            shape((width, 3 * width), BF16), shape((width, width), BF16), shape((width, WIDE), F32), shape((32, WIDE), F32),
             *(shape(g.shape[1:], F32) for g in slices), *(shape(g.shape, BF16) for g in slices * 2),
         ),
         in_specs=[VMEM] * 12 + [ANY] + [VMEM] * 4 + [ANY] * 4,
@@ -1294,9 +1300,10 @@
             pltpu.VMEM((replicated.rows, WIDE), BF16),
             pltpu.VMEM((replicated.landing()[1], WIDE), BF16),
             pltpu.VMEM((replicated.rows, WIDE), BF16),
-            pltpu.VMEM((2, width, 2 * WIDE), F32),
+            pltpu.VMEM((2, width, WIDE), F32),
             DMA((len(replicated.pieces), replicated.steps, slices[0].shape[0])),
             DMA((len(replicated.pieces), replicated.steps, slices[0].shape[0])),
+            DMA((4 * PAIRS,)),
         ],
         compiler_params=pltpu.CompilerParams(collective_id=1, has_side_effects=True, vmem_limit_bytes=LIMIT),
         cost_estimate=pl.CostEstimate(flops=16 * 10**9, bytes_accessed=60 * 2**20, transcendentals=5 * 10**6),
@@ -1334,8 +1341,8 @@
         tokens_grad[None],
         found[0],
         found[1],
-        qkv_grad,
-        out_proj,
+        qkv_grad.astype(F32),
+        out_proj.astype(F32),
         found[2],
         found[3],
         router[:, :experts],

time: 521 us -> 471 us (0.904)
  the two profiles are of different devices: /device:TPU:19 before, /device:TPU:9 now
where the time goes in v5:
time: 471 us; the launch traced here: 462 us
  Pallas kernels  439 us (93%)
  local copies, waits for them, and re-layouts  15.1 us (3%)
  other arithmetic  6.94 us (1%)
    pallas_call x1, Pallas kernels, layer(): pl.pallas_call(functools.partial(layer_kernel, lay, capacity, n_dp), out_...  279 us
    pallas_call x1, Pallas kernels, backward(): pl.pallas_call(functools.partial(back_kernel, lay, capacity, replicated),...  160 us
    unnamed x19, local copies, waits for them, and re-layouts  9.49 us

profile of v5, /device:TPU:9, one launch (start us, length us, event | category | flops | bytes accessed | tf_op | source)
XLA Modules:
  0.0 462.4 jit_solution(8122296181460692342)
XLA Ops:
  0.6 0.7 stack.15
  1.3 0.7 stack.16
  2.0 0.7 stack.17
  2.7 0.7 stack.18
  3.4 0.6 pad_maximum_fusion.vectors
  4.0 0.8 copy.26
  4.8 0.0 copy-start.4
  4.9 0.7 copy.27.routes_t
  5.5 0.9 copy.25
  6.4 0.7 pad.4.w_router
  7.2 0.0 copy-done.4
  7.2 279.5 %layer.1 = (bf16[384,768]{1,0:T(8,128)(2,1)}, bf16[3,3072,128]{2,1,0:T(8,128)(2,1)}, f32[3072,128]{1,0:T(8,128)}, f32[3072,128]{1,0:T(8,128)}, bf16[384,768]{1,0...) custom-call(bf16[384,768]{1,0:T(8,128)(2,1)} %bitcast.34, ...), custom_call_target="tpu_custom_call" | custom-call | flops 49999998976 | bytes 104857600 | tf_op jit(solution)/shard_map/layer/pallas_call | solution.py:742
  286.6 159.7 %backward.1 = (bf16[384,768]{1,0:T(8,128)(2,1)}, f32[384,768]{1,0:T(8,128)}, bf16[768,2304]{1,0:T(8,128)(2,1)}, bf16[768,768]{1,0:T(8,128)(2,1)}, f32[768,128]{1...) custom-call(bf16[1536,768]{1,0:T(8,128)(2,1)} %get-tuple-element.33., ...), custom_call_target="tpu_custom_call" | custom-call | flops 16000000000 | bytes 62914560 | tf_op jit(solution)/shard_map/backward/pallas_call | solution.py:1278
  446.4 0.0 copy-start
  446.4 1.5 slice_bitcast_fusion
  447.8 1.8 copy.28
  449.6 2.8 convert_element_type.9
  452.5 3.5 convert_element_type.8
  455.9 0.8 copy.33
  456.8 1.0 copy.34
  457.8 0.3 copy-done.2
  458.0 1.4 copy.35
  459.4 1.1 copy-done.1
  460.5 1.4 copy.36
  (7 shorter events, 0.0 us)
Async XLA Ops:
  4.8 2.3 copy-start.4
  446.4 6.1 %copy-start = (bf16[768,2304]{1,0:T(8,128)(2,1)S(1)}, bf16[768,2304]{1,0:T(8,128)(2,1)}, u32[]{:S(2)}) copy-start(bf16[768,2304]{1,0:T(8,128)(2,1)} %get-tuple-element.50) | copy-start | bytes 10616836
  452.4 3.5 copy-start.5
  452.5 4.3 copy-start.3
  455.9 2.1 copy-start.2
  458.0 2.5 copy-start.1

commit v6 on v5

--- a/solution.py
+++ b/solution.py
@@ -314,6 +314,11 @@
     return [jnp.sum(m * place, axis=0, keepdims=True).astype(jnp.int32) for m in matches]
 
 
+def upright(routes_t):
+    tall = jnp.concatenate([routes_t.astype(F32), jnp.zeros((WIDE - 2, routes_t.shape[1]), F32)], axis=0)
+    return jnp.transpose(tall).astype(jnp.int32)
+
+
 def slot_columns(lay, capacity, routes):
     n = lay.n
     count = routes.shape[0]
@@ -333,18 +338,25 @@
 
 def layer_kernel(
     lay, capacity, n_dp,
-    tokens, vectors, w_qkv, w_out, w_router, routes, routes_t, cotangent, own_a, own_b, own_c, own_d,
-    first_norm, unit, attended, log_total, home, middle, second_norm, gates_out, got, got_grad, first_grad, second_grad,
+    tokens, vec_a, vec_b, vec_c, vec_d, w_router, routes_t, w_qkv_in, w_out_in, cotangent_in, own_a, own_b, own_c, own_d,
+    first_norm_out, unit_out, attended_out, log_total_out, home_out, middle_out, second_out, gates_out, got, got_grad, first_grad, second_grad,
     all_a, all_b, all_c, all_d, hop_a, hop_b,
     staged_out, packed, packed_grad, rows_in, rows_grad, weight_a, weight_b, out_sum, in_sum, out_other, in_other, back_out, back_grad, grad_a, grad_b,
     packed_gates, rows_gates, send, recv, out_send, home_recv, local, stream_send, stream_recv, load,
     row_send, row_recv, row_local, back_send, back_recv, back_local, hop_send, hop_recv,
+    first_norm, unit, attended, log_total, home, middle, second_norm, out_sems, w_qkv, w_out, cotangent, in_sems,
 ):
     n = lay.n
     me = lax.axis_index("sp")
-    gain_one, shift_one, gain_two, shift_two = (vectors.at[i : i + 1] for i in range(4))
+    gain_one, shift_one, gain_two, shift_two = (vec[...].reshape(1, -1) for vec in (vec_a, vec_b, vec_c, vec_d))
     planes = Planes(n_dp)
     is_short, seq, first_pair = lay.role(me)
+    entering = [
+        pltpu.make_async_copy(source, target, in_sems.at[number])
+        for number, (source, target) in enumerate(((w_qkv_in, w_qkv), (cotangent_in, cotangent), (w_out_in, w_out)))
+    ]
+    for copy in entering:
+        copy.start()
     meet(planes.peers(n))
     stream = Weights(
         planes, (own_a, own_b, own_c, own_d), (all_a, all_b, all_c, all_d), stream_send, stream_recv
@@ -352,7 +364,9 @@
     stream.begin((2, 3), True)
 
     hat, _ = normed(tokens[...].astype(F32))
-    first_norm[...] = (hat * gain_one[...] + shift_one[...]).astype(BF16)
+    for copy in entering:
+        copy.wait()
+    first_norm[...] = (hat * gain_one + shift_one).astype(BF16)
     started = []
     for chunk in range(9):
         kind, third = divmod(chunk, 3)
@@ -478,14 +492,26 @@
     x1 = tokens[...].astype(F32) + dot(home[...], w_out[...])
     middle[...] = x1
     hat, _ = normed(x1)
-    second = (hat * gain_two[...] + shift_two[...]).astype(BF16)
+    second = (hat * gain_two + shift_two).astype(BF16)
     second_norm[...] = second
+    leaving = [
+        pltpu.make_async_copy(source, target, out_sems.at[number])
+        for number, (source, target) in enumerate(
+            (
+                (first_norm, first_norm_out), (unit, unit_out), (attended, attended_out), (log_total, log_total_out),
+                (home, home_out), (middle, middle_out), (second_norm, second_out),
+            )
+        )
+    ]
+    for copy in leaving:
+        copy.start()
     for first in range(0, 2 * span, ROWS):
         slots = first + lax.broadcasted_iota(jnp.int32, (ROWS, count), 0)
         chosen = hot(jnp.logical_or(slots == place[0], slots == place[1]))
         packed[first : first + ROWS] = dot(chosen, second).astype(BF16)
     dispatch(0)
-    logits = dot(second, w_router[...])
+    logits = dot_t(second, w_router[...])
+    routes = upright(routes_t[...])
     index = lax.broadcasted_iota(jnp.int32, logits.shape, 1)
     chosen = [jnp.sum(jnp.where(index == routes[:, c : c + 1], logits, 0.0), axis=1, keepdims=True) for c in range(2)]
     top = jnp.maximum(chosen[0], chosen[1])
@@ -493,7 +519,7 @@
     gates = [value / (exped[0] + exped[1]) for value in exped]
     lane = lax.broadcasted_iota(jnp.int32, gates_out.shape, 1)
     gates_out[...] = jnp.where(lane == 0, gates[0], gates[1])
-    column, _ = slot_columns(lay, capacity, routes[...])
+    column, _ = slot_columns(lay, capacity, routes)
     for number in range(2 * n):
         held = [
             jnp.where(jnp.logical_and(lane < capacity, lane + number * capacity == column[c]), gates[c], 0.0)
@@ -719,6 +745,8 @@
                 comes = jnp.logical_or(src != me, planes.outer) if kind == 0 else src != me
                 pl.when(comes)(pltpu.make_async_copy(piece, piece, back_recv.at[which, kind, src]).wait)
     stream.finish()
+    for copy in leaving:
+        copy.wait()
     hops(end)
     for up in (True, False):
         for array, hop in enumerate((hop_a, hop_b)):
@@ -731,7 +759,7 @@
 ANY = pl.BlockSpec(memory_space=pl.ANY)
 
 
-def layer(lay, capacity, n_dp, tokens, vectors, w_qkv, w_out, w_router, routes, cotangent, weights):
+def layer(lay, capacity, n_dp, tokens, vectors, w_router, routes_t, w_qkv, w_out, cotangent, weights):
     count, width = tokens.shape
     n = lay.n
     owners = len(lay.owners())
@@ -758,8 +786,8 @@
             shape((2, *weights[0].shape), BF16),
             shape((2, *weights[1].shape), BF16),
         ),
-        in_specs=[VMEM] * 8 + [ANY] * 4,
-        out_specs=[VMEM] * 8 + [ANY] * 10,
+        in_specs=[VMEM] * 7 + [ANY] * 7,
+        out_specs=[ANY] * 7 + [VMEM] + [ANY] * 10,
         scratch_shapes=[
             pltpu.VMEM((UNIT, WIDE), BF16),
             pltpu.VMEM((2 * span, width), BF16),
@@ -794,12 +822,22 @@
             DMA((2, 2)),
             DMA((2, 2)),
             DMA((2, 2)),
+            pltpu.VMEM((count, width), BF16),
+            pltpu.VMEM((3, UNIT, WIDE), BF16),
+            pltpu.VMEM((UNIT, WIDE), F32),
+            pltpu.VMEM((UNIT, WIDE), F32),
+            pltpu.VMEM((count, width), BF16),
+            pltpu.VMEM((count, width), F32),
+            pltpu.VMEM((count, width), BF16),
+            DMA((7,)),
+            *(pltpu.VMEM(value.shape, BF16) for value in (w_qkv, w_out, cotangent)),
+            DMA((3,)),
         ],
         compiler_params=pltpu.CompilerParams(collective_id=0, has_side_effects=True, vmem_limit_bytes=LIMIT),
         cost_estimate=pl.CostEstimate(flops=50 * 10**9, bytes_accessed=100 * 2**20, transcendentals=10**7),
         name="layer",
     )(
-        tokens, vectors, w_qkv, w_out, w_router, routes, routes.T, cotangent, *weights
+        tokens, *vectors, w_router, routes_t, w_qkv, w_out, cotangent, *weights
     )
 
 
@@ -1059,31 +1097,37 @@
 
 def back_kernel(
     lay, capacity, replicated,
-    got, got_grad, middle, second_norm, gates, home_out, w_out, vectors, w_router, routes, cotangent,
-    unit, attended, log_total, first_norm, tokens, w_qkv, first_own, second_own, hop_a, hop_b,
+    got, got_grad, middle, second_norm, gates, home_out, w_out, vec_a, vec_b, w_router, routes_t, cotangent,
+    unit_in, attended, log_total_in, first_norm_in, tokens, w_qkv_in, first_own, second_own, hop_a, hop_b,
     block_out, tokens_grad, qkv_grad, out_proj_grad, router_out, vectors_out, first_total, second_total, below_a, below_b, above_a, above_b,
     grad_attended, grad_out, deltas, query_sum, staged, home, send, recv, out_send, home_recv, local,
     theirs_a, theirs_b, sums_a, sums_b, pass_send, pass_recv, load,
-    grads, landed, summed, stage, sum_send, sum_recv, out_sems,
+    grads, landed, summed, stage, sum_send, sum_recv, out_sems, unit, log_total, first_norm, w_qkv, late_sems,
 ):
     n_dp = first_own.shape[0]
     gather = Gather(
         n_dp, (first_own, second_own), (hop_a, hop_b), (below_a, below_b), (above_a, above_b), (theirs_a, theirs_b),
         (sums_a, sums_b), stage, pass_send, pass_recv, load,
     )
-    gain_one, gain_two = vectors.at[0:1], vectors.at[2:3]
+    gain_one, gain_two = (vec[...].reshape(1, -1) for vec in (vec_a, vec_b))
     replicated.bind(grads, landed, summed, sum_send, sum_recv)
     me = lax.axis_index("sp")
     is_short, seq, first_pair = lay.role(me)
     everywhere = [(True, {"dp": lax.rem(gather.me + step, n_dp)}) for step in range(1, n_dp)]
+    late = [
+        pltpu.make_async_copy(source, target, late_sems.at[number])
+        for number, (source, target) in enumerate(
+            ((attended, deltas), (unit_in, unit), (log_total_in, log_total), (first_norm_in, first_norm), (w_qkv_in, w_qkv))
+        )
+    ]
+    for copy in late:
+        copy.start()
     meet(plane_peers(lay.n) + everywhere)
-    kept = pltpu.make_async_copy(attended, deltas, load.at[2])
-    kept.start()
     inside = [(up, index) for index in range(1, n_dp - 1) for up in (True, False)]
     ends = [(True, n_dp - 1), (False, 0)]
     for up, index in ends:
         gather.begin(0, index, up)
-    place, matches = slot_columns(lay, capacity, routes[...])
+    place, matches = slot_columns(lay, capacity, upright(routes_t[...]))
     slots = lax.broadcasted_iota(jnp.int32, (tokens.shape[0], got.shape[0]), 1)
     chosen = [hot(slots == place[c]) for c in range(2)]
     upstream = cotangent[...].astype(F32)
@@ -1099,27 +1143,16 @@
     grad_logits = sum(matches[c] * (gate[c] * (grad_gate[c] - mean_grad)) for c in range(2))
     high = grad_logits.astype(BF16)
     low = (grad_logits - high.astype(F32)).astype(BF16)
-    router_grad = t_dot(second_norm[...], high) + t_dot(second_norm[...], low)
-    grad_second = dot_t(high, w_router[...]) + dot_t(low, w_router[...])
+    experts = w_router.shape[0]
+    grad_second = dot(high[:, :experts], w_router[...]) + dot(low[:, :experts], w_router[...])
     grad_second = grad_second + dot(chosen[0] + chosen[1], got_grad[...])
     hat, scale = normed(middle[...])
-    gain_two_grad = jnp.sum(grad_second * hat, axis=0, keepdims=True)
-    shift_two_grad = jnp.sum(grad_second, axis=0, keepdims=True)
-    grad = upstream + norm_back(grad_second, gain_two[...], hat, scale)
+    grad = upstream + norm_back(grad_second, gain_two, hat, scale)
     tokens_grad[...] = grad
     branch = grad.astype(BF16)
     grad_attended[...] = dot_t(branch, w_out[...]).astype(BF16)
-    out_proj = t_dot(home_out[...], branch)
     width = w_out.shape[0]
 
-    def put(column, value):
-        for lane in range(0, value.shape[1], WIDE):
-            grads[pl.ds((column + lane) // WIDE * width, width)] = value[:, lane : lane + WIDE].astype(BF16)
-
-    put(0, out_proj)
-    moments = (1, 2, 3, 5, 7)
-    if replicated.early:
-        replicated.start(0, 0)
     started = to_owners(
         lay,
         me,
@@ -1134,11 +1167,23 @@
     )
     for up, index in ends:
         gather.begin(1, index, up)
+    def put(column, value):
+        for lane in range(0, value.shape[1], WIDE):
+            grads[pl.ds((column + lane) // WIDE * width, width)] = value[:, lane : lane + WIDE].astype(BF16)
+
+    put(0, t_dot(home_out[...], branch))
+    moments = (1, 2, 3, 5, 7)
+    if replicated.early:
+        replicated.start(0, 0)
+    router_grad = t_dot(second_norm[...], high) + t_dot(second_norm[...], low)
+    gain_two_grad = jnp.sum(grad_second * hat, axis=0, keepdims=True)
+    shift_two_grad = jnp.sum(grad_second, axis=0, keepdims=True)
     query_sum[...] = jnp.zeros_like(query_sum)
     keep = lanes_first()
     lower = causal(BLOCK)
     wait_unit(lay, is_short, grad_out, recv)
-    kept.wait()
+    for copy in late:
+        copy.wait()
 
     def make_delta(index, carry):
         part = pl.ds(pl.multiple_of(index * BLOCK, BLOCK), BLOCK)
@@ -1214,47 +1259,48 @@
             gather.begin(array, index, up)
     for kind in range(3):
         wait_home(lay, is_short, staged.at[kind], home_recv.at[kind], 1, False)
-    grad_first = dot_t(home[...], w_qkv[...])
-    hat, scale = normed(tokens[...].astype(F32))
-    gain_one_grad = jnp.sum(grad_first * hat, axis=0, keepdims=True)
-    shift_one_grad = jnp.sum(grad_first, axis=0, keepdims=True)
-    tokens_grad[...] += norm_back(grad_first, gain_one[...], hat, scale)
-    parts = (gain_one_grad, shift_one_grad, gain_two_grad, shift_two_grad)
-    grads[pl.ds(width // WIDE * width, width)] = router_grad.astype(BF16)
-    rows = [part[:, lane : lane + WIDE] for part in parts for lane in range(0, width, WIDE)]
-    rows.append(jnp.zeros((width - len(rows), WIDE), F32))
-    grads[pl.ds(7 * width, width)] = jnp.concatenate(rows, axis=0).astype(BF16)
-    first = 8
-    last = first + 3 * PAIRS
-    for spare in range(last, replicated.rows // width):
-        grads[pl.ds(spare * width, width)] = jnp.zeros((width, WIDE), BF16)
+    first, last = PAIRS, 4 * PAIRS
 
     def ready(piece):
         start, rows = replicated.pieces[piece]
         for column in range(start // width, (start + rows) // width, 2):
-            if first <= column < last:
+            if column == last:
+                grads[pl.ds(column * width, width)] = router_grad.astype(BF16)
+                parts = (*extra, gain_two_grad, shift_two_grad)
+                rows = [part[:, lane : lane + WIDE] for part in parts for lane in range(0, width, WIDE)]
+                rows.append(jnp.zeros((width - len(rows), WIDE), F32))
+                grads[pl.ds((column + 1) * width, width)] = jnp.concatenate(rows, axis=0).astype(BF16)
+            elif column > last:
+                grads[pl.ds(column * width, 2 * width)] = jnp.zeros((2 * width, WIDE), BF16)
+            elif first <= column:
                 lanes = pl.ds((column - first) * WIDE, 2 * WIDE)
                 put(column * WIDE, t_dot(first_norm[...], home[:, lanes]))
 
-    stores = []
+    stores, extra = [], []
 
     def done(piece):
         start, rows = replicated.pieces[piece]
         for column in range(start // width, (start + rows) // width, 2):
             parts = [summed.at[pl.ds((column + i) * width, width)] for i in range(2)]
-            if column == 6:
-                router_out[...] = parts[0][...].astype(F32)
+            if column == last:
+                router_out[...] = jnp.transpose(parts[0][...].astype(F32))[: router_out.shape[0]]
                 vectors_out[...] = parts[1][0:32].astype(F32)
             elif column < last:
                 for i in range(2):
-                    target, lane = (out_proj_grad, column) if column < 6 else (qkv_grad, column - first)
+                    target, lane = (out_proj_grad, column) if column < first else (qkv_grad, column - first)
                     lanes = pl.ds((lane + i) * WIDE, WIDE)
                     stores.append(pltpu.make_async_copy(parts[i], target.at[:, lanes], out_sems.at[len(stores)]))
                     stores[-1].start()
 
     def between(number):
-        if number in (5, 6):
-            array = number - 5
+        if number == 0:
+            grad_first = dot_t(home[...], w_qkv[...])
+            hat, scale = normed(tokens[...].astype(F32))
+            extra.append(jnp.sum(grad_first * hat, axis=0, keepdims=True))
+            extra.append(jnp.sum(grad_first, axis=0, keepdims=True))
+            tokens_grad[...] += norm_back(grad_first, gain_one, hat, scale)
+        if number in (6, 7):
+            array = number - 6
             for up, index in inside:
                 gather.pass_on(array, index, up)
             for up, index in inside + ends:
@@ -1274,15 +1320,16 @@
     owners = len(lay.owners())
     shape = jax.ShapeDtypeStruct
     slices = values[-4:-2]
+    late = [values[number] for number in (12, 14, 15, 17)]
     replicated = Sum(lay.n, slices[0].shape[0], 6, 2 * width, 26 * width, width // WIDE * width)
     return pl.pallas_call(
         functools.partial(back_kernel, lay, capacity, replicated),
         out_shape=(
             shape((count, width), BF16), shape((count, width), F32),
-            shape((width, 3 * width), BF16), shape((width, width), BF16), shape((width, WIDE), F32), shape((32, WIDE), F32),
+            shape((width, 3 * width), BF16), shape((width, width), BF16), shape(values[9].shape, F32), shape((32, WIDE), F32),
             *(shape(g.shape[1:], F32) for g in slices), *(shape(g.shape, BF16) for g in slices * 2),
         ),
-        in_specs=[VMEM] * 12 + [ANY] + [VMEM] * 4 + [ANY] * 4,
+        in_specs=[VMEM] * 12 + [ANY] * 4 + [VMEM] + [ANY] * 5,
         out_specs=[VMEM] * 2 + [ANY] * 2 + [VMEM] * 2 + [ANY] * 6,
         scratch_shapes=[
             pltpu.VMEM((count, width), BF16),
@@ -1304,6 +1351,8 @@
             DMA((len(replicated.pieces), replicated.steps, slices[0].shape[0])),
             DMA((len(replicated.pieces), replicated.steps, slices[0].shape[0])),
             DMA((4 * PAIRS,)),
+            *(pltpu.VMEM(value.shape, value.dtype) for value in late),
+            DMA((5,)),
         ],
         compiler_params=pltpu.CompilerParams(collective_id=1, has_side_effects=True, vmem_limit_bytes=LIMIT),
         cost_estimate=pl.CostEstimate(flops=16 * 10**9, bytes_accessed=60 * 2**20, transcendentals=5 * 10**6),
@@ -1320,18 +1369,19 @@
     tokens, routes, cotangent = tokens[0], routes[0], cotangent[0]
     count, width = tokens.shape
     capacity = 2 * count // lay.n
-    experts = w_router.shape[1]
-    router_wide = jnp.pad(w_router, ((0, 0), (0, 128 - experts)))
-    vectors = jnp.stack([ln1_gain, ln1_shift, ln2_gain, ln2_shift])
+    router_t, routes_t = w_router.T, routes.T
     weights = [weight[0] for weight in (train_w1, train_w2, frozen_w1, frozen_w2)]
     (
         first_norm, unit, attended, log_total, home, middle, second, gates, got, got_grad, first_grad, second_grad,
         _, _, _, _, hop_a, hop_b,
-    ) = layer(lay, capacity, n_dp, tokens, vectors, w_qkv, w_out, router_wide, routes, cotangent, weights)
+    ) = layer(
+        lay, capacity, n_dp, tokens, (ln1_gain, ln1_shift, ln2_gain, ln2_shift), router_t, routes_t, w_qkv, w_out, cotangent,
+        weights,
+    )
     block_out, tokens_grad, qkv_grad, out_proj, router, vector_rows, first_total, second_total, *_ = backward(
         lay, capacity,
         (
-            got, got_grad, middle, second, gates, home, w_out, vectors, router_wide, routes, cotangent,
+            got, got_grad, middle, second, gates, home, w_out, ln1_gain, ln2_gain, router_t, routes_t, cotangent,
             unit, attended, log_total, first_norm, tokens, w_qkv, first_grad, second_grad, hop_a, hop_b,
         ),
     )
@@ -1345,7 +1395,7 @@
         out_proj.astype(F32),
         found[2],
         found[3],
-        router[:, :experts],
+        router.T,
         first_total[None],
         second_total[None],
     )

time: 471 us -> 453 us (0.962)
  the two profiles are of different devices: /device:TPU:9 before, /device:TPU:0 now
where the time goes in v6:
time: 453 us; the launch traced here: 444 us
  Pallas kernels  429 us (95%)
  local copies, waits for them, and re-layouts  7.87 us (2%)
  other arithmetic  6.32 us (1%)
    pallas_call x1, Pallas kernels, layer(): pl.pallas_call(functools.partial(layer_kernel, lay, capacity, n_dp), out_...  279 us
    pallas_call x1, Pallas kernels, backward(): pl.pallas_call(functools.partial(back_kernel, lay, capacity, replicated),...  150 us

profile of v6, /device:TPU:0, one launch (start us, length us, event | category | flops | bytes accessed | tf_op | source)
XLA Modules:
  0.0 444.2 jit_solution(10544802817189382275)
XLA Ops:
  0.6 278.9 %layer.1 = (bf16[384,768]{1,0:T(8,128)(2,1)}, bf16[3,3072,128]{2,1,0:T(8,128)(2,1)}, f32[3072,128]{1,0:T(8,128)}, f32[3072,128]{1,0:T(8,128)}, bf16[384,768]{1,0...) custom-call(bf16[384,768]{1,0:T(8,128)(2,1)} %bitcast.32, ...), custom_call_target="tpu_custom_call" | custom-call | flops 49999998976 | bytes 104857600 | tf_op jit(solution)/shard_map/layer/pallas_call | solution.py:770
  279.6 150.3 %backward.1 = (bf16[384,768]{1,0:T(8,128)(2,1)}, f32[384,768]{1,0:T(8,128)}, bf16[768,2304]{1,0:T(8,128)(2,1)}, bf16[768,768]{1,0:T(8,128)(2,1)}, f32[16,768]{1,...) custom-call(bf16[1536,768]{1,0:T(8,128)(2,1)} %get-tuple-element.33., ...), custom_call_target="tpu_custom_call" | custom-call | flops 16000000000 | bytes 62914560 | tf_op jit(solution)/shard_map/backward/pallas_call | solution.py:1325
  429.8 0.0 copy-start
  429.9 1.5 slice_bitcast_fusion
  431.3 2.8 convert_element_type.7
  434.2 0.0 copy-done
  434.2 0.0 copy-start.4
  434.2 0.0 copy-start.3
  434.2 3.5 convert_element_type.6
  437.7 0.0 copy-done.4
  437.7 0.0 copy-start.5
  437.7 0.0 copy-start.2
  437.7 0.8 copy.30
  438.5 0.0 copy-done.3
  438.5 1.0 copy.31
  439.5 0.0 copy-done.5
  439.5 0.6 copy.32
  440.1 0.0 copy-done.2
  440.1 0.0 copy-start.1
  440.1 1.4 copy.33
  441.5 1.1 copy-done.1
  442.6 1.4 copy.34
Async XLA Ops:
  429.8 4.3 copy-start
  434.2 3.5 copy-start.4
  434.2 4.3 copy-start.3
  437.7 1.8 copy-start.5
  437.7 2.5 copy-start.2
  440.1 2.5 copy-start.1

commit v7 on v6

--- a/solution.py
+++ b/solution.py
@@ -981,8 +981,8 @@
 
 
 class Gather:
-    def __init__(self, n, own, hop, below, above, theirs, sums, stage, send, recv, load):
-        self.n, self.own, self.hop, self.below, self.above, self.stage = n, own, hop, below, above, stage
+    def __init__(self, n, own, hop, below, above, theirs, sums, send, recv, load):
+        self.n, self.own, self.hop, self.below, self.above = n, own, hop, below, above
         self.theirs, self.sums, self.send, self.recv, self.load = theirs, sums, send, recv, load
         self.me = lax.axis_index("dp")
         self.inner = jnp.logical_and(self.me >= 1, self.me <= n - 2)
@@ -1040,48 +1040,12 @@
         def _():
             self.copy(array, index, up, self.sums[array].at[int(up)]).wait_send()
 
-    def total(self, array, out):
-        theirs = self.theirs[array]
-
-        @pl.when(self.inner)
-        def _():
-            self.fetch(self.own[array].at[self.me], theirs, 0).wait()
-
-        @pl.when(jnp.logical_not(self.inner))
-        def _():
-            theirs[...] = jnp.zeros_like(theirs)
-
-        sides = ((True, self.me >= 2), (False, self.me <= self.n - 3))
-        for up, comes in sides:
-
-            near = self.me == (2 if up else self.n - 3)
-
-            @pl.when(jnp.logical_and(comes, near))
+    def arrived(self, array):
+        for up, comes in ((True, self.me > 2), (False, self.me < self.n - 3)):
+
+            @pl.when(comes)
             def _():
-                self.fetch(self.hop[array].at[int(up)], self.sums[array].at[int(up)], 1).wait()
-
-            @pl.when(jnp.logical_and(comes, jnp.logical_not(near)))
-            def _():
-                self.fetch(self.came(array, self.me, up), self.sums[array].at[int(up)], 1).wait()
-
-        rows, lanes = out.shape
-        stores = []
-        for number in range(lanes // WIDE):
-            part = pl.ds(number * WIDE, WIDE)
-            stage = self.stage.at[number % 2, pl.ds(0, rows), pl.ds(0, WIDE)]
-            if number >= 2:
-                stores[number - 2].wait()
-            stage[...] = theirs[:, part].astype(F32)
-            for up, comes in sides:
-
-                @pl.when(comes)
-                def _():
-                    stage[...] += self.sums[array][int(up), :, part].astype(F32)
-
-            stores.append(pltpu.make_async_copy(stage, out.at[:, part], self.load.at[3 + number % 2]))
-            stores[number].start()
-        for store in stores[-2:]:
-            store.wait()
+                self.came(array, self.me, up)
 
 
 def gather_scratch(n, first, second):
@@ -1099,15 +1063,15 @@
     lay, capacity, replicated,
     got, got_grad, middle, second_norm, gates, home_out, w_out, vec_a, vec_b, w_router, routes_t, cotangent,
     unit_in, attended, log_total_in, first_norm_in, tokens, w_qkv_in, first_own, second_own, hop_a, hop_b,
-    block_out, tokens_grad, qkv_grad, out_proj_grad, router_out, vectors_out, first_total, second_total, below_a, below_b, above_a, above_b,
+    block_out, tokens_grad, qkv_grad, out_proj_grad, router_out, vectors_out, below_a, below_b, above_a, above_b,
     grad_attended, grad_out, deltas, query_sum, staged, home, send, recv, out_send, home_recv, local,
     theirs_a, theirs_b, sums_a, sums_b, pass_send, pass_recv, load,
-    grads, landed, summed, stage, sum_send, sum_recv, out_sems, unit, log_total, first_norm, w_qkv, late_sems,
+    grads, landed, summed, sum_send, sum_recv, out_sems, unit, log_total, first_norm, w_qkv, late_sems,
 ):
     n_dp = first_own.shape[0]
     gather = Gather(
         n_dp, (first_own, second_own), (hop_a, hop_b), (below_a, below_b), (above_a, above_b), (theirs_a, theirs_b),
-        (sums_a, sums_b), stage, pass_send, pass_recv, load,
+        (sums_a, sums_b), pass_send, pass_recv, load,
     )
     gain_one, gain_two = (vec[...].reshape(1, -1) for vec in (vec_a, vec_b))
     replicated.bind(grads, landed, summed, sum_send, sum_recv)
@@ -1172,7 +1136,7 @@
             grads[pl.ds((column + lane) // WIDE * width, width)] = value[:, lane : lane + WIDE].astype(BF16)
 
     put(0, t_dot(home_out[...], branch))
-    moments = (1, 2, 3, 5, 7)
+    moments = (2, 3, 5, 6, 7)
     if replicated.early:
         replicated.start(0, 0)
     router_grad = t_dot(second_norm[...], high) + t_dot(second_norm[...], low)
@@ -1299,13 +1263,13 @@
             extra.append(jnp.sum(grad_first * hat, axis=0, keepdims=True))
             extra.append(jnp.sum(grad_first, axis=0, keepdims=True))
             tokens_grad[...] += norm_back(grad_first, gain_one, hat, scale)
-        if number in (6, 7):
-            array = number - 6
+        if number in (7, 8):
+            array = number - 7
             for up, index in inside:
                 gather.pass_on(array, index, up)
             for up, index in inside + ends:
                 gather.finish(array, index, up)
-            gather.total(array, (first_total, second_total)[array])
+            gather.arrived(array)
 
     run_sum(replicated, len(moments) + 1, ready, done, between)
     for store in stores:
@@ -1327,10 +1291,10 @@
         out_shape=(
             shape((count, width), BF16), shape((count, width), F32),
             shape((width, 3 * width), BF16), shape((width, width), BF16), shape(values[9].shape, F32), shape((32, WIDE), F32),
-            *(shape(g.shape[1:], F32) for g in slices), *(shape(g.shape, BF16) for g in slices * 2),
+            *(shape(g.shape, BF16) for g in slices * 2),
         ),
         in_specs=[VMEM] * 12 + [ANY] * 4 + [VMEM] + [ANY] * 5,
-        out_specs=[VMEM] * 2 + [ANY] * 2 + [VMEM] * 2 + [ANY] * 6,
+        out_specs=[VMEM] * 2 + [ANY] * 2 + [VMEM] * 2 + [ANY] * 4,
         scratch_shapes=[
             pltpu.VMEM((count, width), BF16),
             pltpu.VMEM((UNIT, WIDE), BF16),
@@ -1347,7 +1311,6 @@
             pltpu.VMEM((replicated.rows, WIDE), BF16),
             pltpu.VMEM((replicated.landing()[1], WIDE), BF16),
             pltpu.VMEM((replicated.rows, WIDE), BF16),
-            pltpu.VMEM((2, width, WIDE), F32),
             DMA((len(replicated.pieces), replicated.steps, slices[0].shape[0])),
             DMA((len(replicated.pieces), replicated.steps, slices[0].shape[0])),
             DMA((4 * PAIRS,)),
@@ -1378,13 +1341,22 @@
         lay, capacity, n_dp, tokens, (ln1_gain, ln1_shift, ln2_gain, ln2_shift), router_t, routes_t, w_qkv, w_out, cotangent,
         weights,
     )
-    block_out, tokens_grad, qkv_grad, out_proj, router, vector_rows, first_total, second_total, *_ = backward(
+    block_out, tokens_grad, qkv_grad, out_proj, router, vector_rows, below_a, below_b, above_a, above_b = backward(
         lay, capacity,
         (
             got, got_grad, middle, second, gates, home, w_out, ln1_gain, ln2_gain, router_t, routes_t, cotangent,
             unit, attended, log_total, first_norm, tokens, w_qkv, first_grad, second_grad, hop_a, hop_b,
         ),
     )
+    plane = lax.axis_index("dp")
+
+    def total(own, hop, below, above):
+        at = lambda whole: lax.dynamic_index_in_dim(whole, plane, 0, keepdims=False).astype(F32)
+        inner = jnp.logical_and(plane >= 1, plane <= n_dp - 2)
+        up = jnp.where(plane == 2, hop[1].astype(F32), jnp.where(plane > 2, at(below), 0.0))
+        down = jnp.where(plane == n_dp - 3, hop[0].astype(F32), jnp.where(plane < n_dp - 3, at(above), 0.0))
+        return jnp.where(inner, at(own), 0.0) + up + down
+
     found = vector_rows[: 4 * width // WIDE].reshape(4, width)
     return (
         block_out[None],
@@ -1396,8 +1368,8 @@
         found[2],
         found[3],
         router.T,
-        first_total[None],
-        second_total[None],
+        total(first_grad, hop_a, below_a, above_a)[None],
+        total(second_grad, hop_b, below_b, above_b)[None],
     )
 
 

time: 453 us -> 450 us (level)
  other arithmetic: 6.32 us -> 11.2 us
  local copies, waits for them, and re-layouts: 7.87 us -> 3.08 us
    add x0 -> x1, other arithmetic: none -> 6.15 us  [total(): return jnp.where(inner, at(own), 0.0) + up + down]
where the time goes in v7:
time: 450 us; the launch traced here: 441 us
  Pallas kernels  426 us (95%)
  other arithmetic  11.2 us (2%)
    pallas_call x1, Pallas kernels, layer(): pl.pallas_call(functools.partial(layer_kernel, lay, capacity, n_dp), out_...  279 us
    pallas_call x1, Pallas kernels, backward(): pl.pallas_call(functools.partial(back_kernel, lay, capacity, replicated),...  147 us

profile of v7, /device:TPU:0, one launch (start us, length us, event | category | flops | bytes accessed | tf_op | source)
XLA Modules:
  0.0 441.5 jit_solution(16233525517715054778)
XLA Ops:
  0.6 278.9 %layer.1 = (bf16[384,768]{1,0:T(8,128)(2,1)}, bf16[3,3072,128]{2,1,0:T(8,128)(2,1)}, f32[3072,128]{1,0:T(8,128)}, f32[3072,128]{1,0:T(8,128)}, bf16[384,768]{1,0...) custom-call(bf16[384,768]{1,0:T(8,128)(2,1)} %bitcast.28, ...), custom_call_target="tpu_custom_call" | custom-call | flops 49999998976 | bytes 104857600 | tf_op jit(solution)/shard_map/layer/pallas_call | solution.py:770
  279.5 0.0 copy-start.1
  279.5 147.4 %backward.1 = (bf16[384,768]{1,0:T(8,128)(2,1)}, f32[384,768]{1,0:T(8,128)}, bf16[768,2304]{1,0:T(8,128)(2,1)}, bf16[768,768]{1,0:T(8,128)(2,1)}, f32[16,768]{1,...) custom-call(bf16[1536,768]{1,0:T(8,128)(2,1)} %get-tuple-element.35., ...), custom_call_target="tpu_custom_call" | custom-call | flops 16000000000 | bytes 62914560 | tf_op jit(solution)/shard_map/backward/pallas_call | solution.py:1289
  426.9 0.0 copy-done.1
  427.0 0.0 copy-start
  427.0 6.2 %select_add_fusion = (f32[1,768,768]{2,1,0:T(8,128)}, f32[1,768,768]{2,1,0:T(8,128)}) fusion(bf16[4,768,768]{2,1,0:T(8,128)(2,1)} %get-tuple-element.58, s32[]{:T(128)S(6)} %select_n.74, bf16[2,768,768]{2,1,0:T(8,128)(2,1)} %get-tuple-element.48.hop_b, bf16[4,768,768]{2,1,0:T(8,128)(2,1)} %get-tuple-element.57, ...), kind=kLoop, calls=%fused_computation | loop fusion | flops 14155776 | bytes 16515081 | tf_op jit(solution)/shard_map/add | solution.py:1358
  433.1 0.0 copy-done
  433.1 0.0 copy-start.2
  433.1 3.5 convert_element_type.46
  436.6 0.0 copy-start.6
  436.6 0.0 copy-start.4
  436.6 0.0 copy-done.2
  436.6 0.0 copy-start.3
  436.6 1.6 convert_element_type.47
  438.2 0.0 copy-start.5
  438.2 0.0 copy-done.6
  438.2 0.6 slice_bitcast_fusion
  438.8 0.0 copy-done.4
  438.8 0.8 copy.28
  439.6 0.0 copy-done.3
  439.6 1.0 copy.29
  440.7 0.0 copy-done.5
  440.7 0.6 copy.30
Async XLA Ops:
  279.5 147.4 %copy-start.1 = (bf16[2,768,768]{2,1,0:T(8,128)(2,1)S(1)}, bf16[2,768,768]{2,1,0:T(8,128)(2,1)}, u32[]{:S(2)}) copy-start(bf16[2,768,768]{2,1,0:T(8,128)(2,1)} %get-tuple-element.47.hop_a) | copy-start | bytes 7077892
  427.0 6.2 %copy-start = (bf16[768,2304]{1,0:T(8,128)(2,1)S(1)}, bf16[768,2304]{1,0:T(8,128)(2,1)}, u32[]{:S(2)}) copy-start(bf16[768,2304]{1,0:T(8,128)(2,1)} %get-tuple-element.52) | copy-start | bytes 10616836
  433.1 3.5 copy-start.2
  436.6 1.6 copy-start.6
  436.6 2.2 copy-start.4
  436.6 3.0 copy-start.3
  438.2 2.4 copy-start.5
